TPU v7x, 32 devices: a whole 2x2x4 slice. The times are simulated.
32 devices in a mesh: dp: 16 (over z, x, core), tensor: 2 (over y).
Axes of the slice: x: 2, y: 2, z: 4, core: 2. Of those that a mesh axis runs over, the one named last changes fastest.
Arguments:
- tokens: bfloat16 [16384, 768], P(('dp', 'tensor')), may hold values from -6 to 6
- segment_ids: int32 [16, 1024], P('dp'), may hold values from 0 to 4, as said below
- pad_mask: int32 [16, 1024], P('dp'), may hold values from 0 to 1, as said below
- norm1_gain: float32 [768], replicated, may hold values from 0.5 to 1.5
- norm1_shift: float32 [768], replicated, may hold values from -1 to 1
- w_query: bfloat16 [768, 768], P(None, 'tensor'), may hold values from -2 to 2
- w_key: bfloat16 [768, 768], P(None, 'tensor'), may hold values from -2 to 2
- w_value: bfloat16 [768, 768], P(None, 'tensor'), may hold values from -0.21875 to 0.21875
- w_out: bfloat16 [768, 768], P('tensor'), may hold values from -0.4375 to 0.4375
- norm2_gain: float32 [768], replicated, may hold values from 0.5 to 1.5
- norm2_shift: float32 [768], replicated, may hold values from -1 to 1
- w_up: bfloat16 [768, 3072], P(None, 'tensor'), may hold values from -0.21875 to 0.21875
- w_down: bfloat16 [3072, 768], P('tensor'), may hold values from -0.109375 to 0.109375
- cotangent: bfloat16 [16384, 768], P(('dp', 'tensor')), may hold values from -6 to 6
Outputs:
- mixed: bfloat16 [16384, 768], P(('dp', 'tensor'))
- tokens_grad: bfloat16 [16384, 768], P(('dp', 'tensor'))
- norm1_gain_grad: float32 [768], replicated
- norm1_shift_grad: float32 [768], replicated
- w_query_grad: float32 [768, 768], P(None, 'tensor')
- w_key_grad: float32 [768, 768], P(None, 'tensor')
- w_value_grad: float32 [768, 768], P(None, 'tensor')
- w_out_grad: float32 [768, 768], P('tensor')
- norm2_gain_grad: float32 [768], replicated
- norm2_shift_grad: float32 [768], replicated
- w_up_grad: float32 [768, 3072], P(None, 'tensor')
- w_down_grad: float32 [3072, 768], P('tensor')
Inputs may be any that keep to these rules, and one draw needn't show every extreme that they name: `segment_ids`: in each row the numbers never fall from one position to the next, and positions 256 to 767 lie in one document. `pad_mask`: in each row the pad slots form one nonempty run at the end, inside the row's last document.
All inputs are finite; a program needn't handle non-finite values.
Results may differ from a plain program's by a relative error of at most 0.014.
Values may be sent and summed in bfloat16 or wider, within the bound.
No kernel may reach another device: no remote copies, remote signals or barrier semaphores. Data moves between devices by JAX's collectives and lax.ppermute only.
A program may use at most 192 MiB of HBM per device.

v0:
```python
import jax
import jax.numpy as jnp
from jax import lax
from jax.sharding import PartitionSpec as P

HEAD_DIM = 64


eps_norm = 1e-05


def broadcast(value, axis, source):
    kept = jnp.where(lax.axis_index(axis) == source, value, 0).astype(value.dtype)
    return lax.psum(kept, axis)


def shifted(shard, axis, by):
    devices = lax.axis_size(axis)
    pairs = [(i, i + by) for i in range(devices) if 0 <= i + by < devices]
    return lax.ppermute(shard, axis, pairs)


def norm_rows(values, norm_gain, norm_shift):
    center = values - jnp.mean(values, axis=-1, keepdims=True)
    inverse = lax.rsqrt(jnp.mean(center * center, axis=-1, keepdims=True) + eps_norm)
    scaled = center * inverse
    return (scaled * norm_gain + norm_shift, scaled, inverse)


def norm_back(grad_normed, scaled, inverse, norm_gain):
    grad_scaled = grad_normed * norm_gain
    grad_input = inverse * (
        grad_scaled
        - jnp.mean(grad_scaled, axis=-1, keepdims=True)
        - scaled * jnp.mean(grad_scaled * scaled, axis=-1, keepdims=True)
    )
    return (grad_input, jnp.sum(grad_normed * scaled, axis=0), jnp.sum(grad_normed, axis=0))


def row_masks(seg_row, pad_row):
    length = seg_row.shape[0]
    row_ids = jnp.arange(length)[:, None]
    col_ids = jnp.arange(length)[None, :]
    same_doc = seg_row[:, None] == seg_row[None, :]
    real_key = pad_row[None, :] > 0
    allowed = same_doc & (col_ids <= row_ids) & real_key | (col_ids == row_ids)
    picked = same_doc & (col_ids < row_ids) & real_key & (pad_row[:, None] > 0)
    return (allowed, picked)


def zero_head_scores(query_zero, key_zero):
    return (
        jnp.einsum("sid,sjd->sij", query_zero, key_zero, preferred_element_type=jnp.float32) * 0.125
    )


def leading_select(zero_scores, picked):
    return jnp.where(picked, jax.nn.softplus(zero_scores), 0.0).astype(jnp.bfloat16)


def head_forward(query_head, key_head, value_head, penalty_seq, allow_seq):
    scores = (
        jnp.einsum("id,jd->ij", query_head, key_head, preferred_element_type=jnp.float32) * 0.125
    )
    logits = jnp.where(allow_seq, scores - penalty_seq, -1e30)
    largest = jnp.max(logits, axis=-1, keepdims=True)
    weights = jnp.exp(logits - largest)
    totals = jnp.sum(weights, axis=-1, keepdims=True)
    probs_low = (weights / totals).astype(jnp.bfloat16)
    output = jnp.dot(probs_low, value_head, preferred_element_type=jnp.float32)
    return (output.astype(jnp.bfloat16), (largest + jnp.log(totals))[:, 0])


def head_backward(query_head, key_head, value_head, grad_head, penalty_seq, allow_seq, lse_head):
    scores = (
        jnp.einsum("id,jd->ij", query_head, key_head, preferred_element_type=jnp.float32) * 0.125
    )
    logits = jnp.where(allow_seq, scores - penalty_seq, -1e30)
    probs_full = jnp.exp(logits - lse_head[:, None])
    grad_probs = jnp.einsum("id,jd->ij", grad_head, value_head, preferred_element_type=jnp.float32)
    row_dot = jnp.sum(probs_full * grad_probs, axis=-1, keepdims=True)
    grad_logits = probs_full * (grad_probs - row_dot)
    grad_value = jnp.einsum(
        "ij,id->jd", probs_full.astype(jnp.bfloat16), grad_head, preferred_element_type=jnp.float32
    )
    return (grad_logits, grad_value.astype(jnp.bfloat16))


def query_key_grads(score_grad, query_head, key_head):
    grad_query = 0.125 * jnp.einsum(
        "ij,jd->id", score_grad, key_head, preferred_element_type=jnp.float32
    )
    grad_key = 0.125 * jnp.einsum(
        "ij,id->jd", score_grad, query_head, preferred_element_type=jnp.float32
    )
    return (grad_query.astype(jnp.bfloat16), grad_key.astype(jnp.bfloat16))


def leading_grads(score_grad, query_head, key_head, extra_query, extra_key):
    grad_query = 0.125 * (
        jnp.einsum("ij,jd->id", score_grad, key_head, preferred_element_type=jnp.float32)
        + extra_query
    )
    grad_key = 0.125 * (
        jnp.einsum("ij,id->jd", score_grad, query_head, preferred_element_type=jnp.float32)
        + extra_key
    )
    return (grad_query.astype(jnp.bfloat16), grad_key.astype(jnp.bfloat16))


def leading_terms(penalty_total, zero_scores, keep, query_zero, key_zero):
    length = penalty_total.shape[-1]
    positions = jnp.arange(length)
    upper_ones = (positions[None, :] > positions[:, None]).astype(jnp.float32)
    select_grad = jnp.einsum(
        "ki,sij->skj",
        upper_ones,
        penalty_total,
        precision=lax.Precision.HIGHEST,
        preferred_element_type=jnp.float32,
    )
    through = jnp.where(keep, select_grad * jax.nn.sigmoid(zero_scores), 0.0)
    extra_query = jnp.einsum(
        "skj,sjd->skd",
        through,
        key_zero.astype(jnp.float32),
        precision=lax.Precision.HIGHEST,
        preferred_element_type=jnp.float32,
    )
    extra_key = jnp.einsum(
        "skj,skd->sjd",
        through,
        query_zero.astype(jnp.float32),
        precision=lax.Precision.HIGHEST,
        preferred_element_type=jnp.float32,
    )
    return (extra_query, extra_key)


def body(
    tokens,
    segment_ids,
    pad_mask,
    norm1_gain,
    norm1_shift,
    w_query,
    w_key,
    w_value,
    w_out,
    norm2_gain,
    norm2_shift,
    w_up,
    w_down,
    cotangent,
):
    seq_count, seq_len = segment_ids.shape
    heads_here = w_query.shape[1] // HEAD_DIM
    inputs = tokens.astype(jnp.float32)
    normed1, scaled1, inverse1 = norm_rows(inputs, norm1_gain, norm1_shift)
    gathered1 = lax.all_gather(normed1.astype(jnp.bfloat16), "tensor", axis=0, tiled=True)

    def project(weight):
        product = jnp.dot(gathered1, weight, preferred_element_type=jnp.float32).astype(
            jnp.bfloat16
        )
        return product.reshape(seq_count, seq_len, heads_here, HEAD_DIM).transpose(0, 2, 1, 3)

    queries = project(w_query)
    keys_all = project(w_key)
    values_all = project(w_value)
    allowed, picked = jax.vmap(row_masks)(segment_ids, pad_mask)
    query_zero, key_zero = (queries[:, 0], keys_all[:, 0])
    zero_scores = zero_head_scores(query_zero, key_zero)
    select = broadcast(leading_select(zero_scores, picked), "tensor", 0)
    positions = jnp.arange(seq_len)
    lower_ones = (positions[None, :] < positions[:, None]).astype(jnp.bfloat16)
    penalty = jnp.einsum("ik,skj->sij", lower_ones, select, preferred_element_type=jnp.float32)

    def forward_sequence(pieces):
        q_seq, k_seq, v_seq, penalty_seq, allow_seq = pieces
        return lax.map(
            lambda heads_in: head_forward(
                heads_in[0], heads_in[1], heads_in[2], penalty_seq, allow_seq
            ),
            (q_seq, k_seq, v_seq),
        )

    heads_out, log_totals = lax.map(
        forward_sequence, (queries, keys_all, values_all, penalty, allowed)
    )
    heads_flat = heads_out.transpose(0, 2, 1, 3).reshape(seq_count * seq_len, heads_here * HEAD_DIM)
    attended = lax.psum_scatter(
        jnp.dot(heads_flat, w_out, preferred_element_type=jnp.float32),
        "tensor",
        scatter_dimension=0,
        tiled=True,
    )
    hidden = inputs + attended
    normed2, scaled2, inverse2 = norm_rows(hidden, norm2_gain, norm2_shift)
    gathered2 = lax.all_gather(normed2.astype(jnp.bfloat16), "tensor", axis=0, tiled=True)
    up_values = jnp.dot(gathered2, w_up, preferred_element_type=jnp.float32)
    active = jax.nn.gelu(up_values, approximate=False).astype(jnp.bfloat16)
    block_out = hidden + lax.psum_scatter(
        jnp.dot(active, w_down, preferred_element_type=jnp.float32).astype(jnp.bfloat16),
        "tensor",
        scatter_dimension=0,
        tiled=True,
    ).astype(jnp.float32)
    grad_full = lax.all_gather(cotangent, "tensor", axis=0, tiled=True)
    down_grad = jnp.einsum("rf,rd->fd", active, grad_full, preferred_element_type=jnp.float32)
    grad_active = jnp.einsum("rd,fd->rf", grad_full, w_down, preferred_element_type=jnp.float32)
    gelu_value, gelu_back = jax.vjp(
        lambda values: jax.nn.gelu(values, approximate=False), up_values
    )
    grad_upper = gelu_back(grad_active)[0].astype(jnp.bfloat16)
    up_grad = jnp.einsum("rd,rf->df", gathered2, grad_upper, preferred_element_type=jnp.float32)
    grad_normed2 = lax.psum_scatter(
        jnp.einsum("rf,df->rd", grad_upper, w_up, preferred_element_type=jnp.float32),
        "tensor",
        scatter_dimension=0,
        tiled=True,
    )
    grad_hidden_norm, gain2_grad, shift2_grad = norm_back(
        grad_normed2, scaled2, inverse2, norm2_gain
    )
    grad_hidden = cotangent.astype(jnp.float32) + grad_hidden_norm
    grad_attn_full = lax.all_gather(grad_hidden.astype(jnp.bfloat16), "tensor", axis=0, tiled=True)
    out_grad = jnp.einsum(
        "rh,rd->hd", heads_flat, grad_attn_full, preferred_element_type=jnp.float32
    )
    grad_mixed = jnp.einsum(
        "rd,hd->rh", grad_attn_full, w_out, preferred_element_type=jnp.float32
    ).astype(jnp.bfloat16)
    grad_mixed = grad_mixed.reshape(seq_count, seq_len, heads_here, HEAD_DIM).transpose(0, 2, 1, 3)

    def backward_sequence(pieces):
        q_seq, k_seq, v_seq, g_seq, penalty_seq, allow_seq, lse_seq = pieces

        def other_head(penalty_sum, heads_in):
            q_head, k_head, v_head, g_head, l_head = heads_in
            grad_logits, grad_value = head_backward(
                q_head, k_head, v_head, g_head, penalty_seq, allow_seq, l_head
            )
            grad_query, grad_key = query_key_grads(grad_logits.astype(jnp.bfloat16), q_head, k_head)
            return (penalty_sum - grad_logits, (grad_query, grad_key, grad_value))

        zero_logits, zero_value = head_backward(
            q_seq[0], k_seq[0], v_seq[0], g_seq[0], penalty_seq, allow_seq, lse_seq[0]
        )
        penalty_sum, rest_grads = lax.scan(
            other_head, -zero_logits, (q_seq[1:], k_seq[1:], v_seq[1:], g_seq[1:], lse_seq[1:])
        )
        return (penalty_sum, zero_logits, zero_value, rest_grads[0], rest_grads[1], rest_grads[2])

    results = lax.map(
        backward_sequence, (queries, keys_all, values_all, grad_mixed, penalty, allowed, log_totals)
    )
    penalty_grad, zero_logits, zero_value, rest_query, rest_key, rest_value = results
    is_owner = lax.axis_index("tensor") == 0
    partner = shifted(penalty_grad.astype(jnp.bfloat16), "tensor", -1).astype(penalty_grad.dtype)
    extra_query, extra_key = leading_terms(
        penalty_grad + partner, zero_scores, picked & is_owner, query_zero, key_zero
    )
    zero_query, zero_key = jax.vmap(leading_grads)(
        zero_logits.astype(jnp.bfloat16), queries[:, 0], keys_all[:, 0], extra_query, extra_key
    )

    def flatten(head_grads):
        return head_grads.transpose(0, 2, 1, 3).reshape(seq_count * seq_len, heads_here * HEAD_DIM)

    query_flat = flatten(jnp.concatenate([zero_query[:, None], rest_query], axis=1))
    key_flat = flatten(jnp.concatenate([zero_key[:, None], rest_key], axis=1))
    value_flat = flatten(jnp.concatenate([zero_value[:, None], rest_value], axis=1))
    query_grad = jnp.einsum("rd,rh->dh", gathered1, query_flat, preferred_element_type=jnp.float32)
    key_grad = jnp.einsum("rd,rh->dh", gathered1, key_flat, preferred_element_type=jnp.float32)
    value_grad = jnp.einsum("rd,rh->dh", gathered1, value_flat, preferred_element_type=jnp.float32)
    total_term = jnp.einsum("rh,dh->rd", query_flat, w_query, preferred_element_type=jnp.float32)
    total_term = total_term + jnp.einsum(
        "rh,dh->rd", key_flat, w_key, preferred_element_type=jnp.float32
    )
    grad_normed1 = lax.psum_scatter(
        (
            total_term
            + jnp.einsum("rh,dh->rd", value_flat, w_value, preferred_element_type=jnp.float32)
        ).astype(jnp.bfloat16),
        "tensor",
        scatter_dimension=0,
        tiled=True,
    ).astype(jnp.float32)
    grad_input_norm, gain1_grad, shift1_grad = norm_back(
        grad_normed1, scaled1, inverse1, norm1_gain
    )
    tokens_grad = (grad_hidden + grad_input_norm).astype(jnp.bfloat16)
    (
        query_grad,
        key_grad,
        value_grad,
        out_grad,
        up_grad,
        down_grad,
        gain1_grad,
        shift1_grad,
        gain2_grad,
        shift2_grad,
    ) = lax.psum(
        (
            query_grad,
            key_grad,
            value_grad,
            out_grad,
            up_grad,
            down_grad,
            gain1_grad,
            shift1_grad,
            gain2_grad,
            shift2_grad,
        ),
        "dp",
    )
    gain1_grad, shift1_grad, gain2_grad, shift2_grad = lax.psum(
        (gain1_grad, shift1_grad, gain2_grad, shift2_grad), "tensor"
    )
    return (
        block_out.astype(jnp.bfloat16),
        tokens_grad,
        gain1_grad,
        shift1_grad,
        query_grad,
        key_grad,
        value_grad,
        out_grad,
        gain2_grad,
        shift2_grad,
        up_grad,
        down_grad,
    )


def solution(mesh):
    in_specs = (
        P(("dp", "tensor"), None),
        P("dp", None),
        P("dp", None),
        P(),
        P(),
        P(None, "tensor"),
        P(None, "tensor"),
        P(None, "tensor"),
        P("tensor", None),
        P(),
        P(),
        P(None, "tensor"),
        P("tensor", None),
        P(("dp", "tensor"), None),
    )
    out_specs = (
        P(("dp", "tensor"), None),
        P(("dp", "tensor"), None),
        P(),
        P(),
        P(None, "tensor"),
        P(None, "tensor"),
        P(None, "tensor"),
        P("tensor", None),
        P(),
        P(),
        P(None, "tensor"),
        P("tensor", None),
    )
    return jax.shard_map(body, mesh=mesh, in_specs=in_specs, out_specs=out_specs, check_vma=False)
```

profile of v0, /device:TPU:1, one launch (start us, length us, event | category | flops | bytes accessed | tf_op | source)
XLA Modules:
  0.0 876.7 jit_solution(12181371838334113526)
XLA Ops:
  13.3 29.4 %all-gather.5.cloned.1.call-done = bf16[1024,768]{1,0:T(8,128)(2,1)} async-done(((bf16[512,768]{1,0:T(8,128)(2,1)}), bf16[1024,768]{1,0:T(8,128)(2,1)}) %all-gather.5.cloned.1.call-update) | async-done | bytes 1572880 | tf_op jit(solution)/shard_map/all_gather | solution.py:160
  50.5 6.0 fusion.90
  60.5 59.1 %all-reduce.6.cloned.1.call-done = bf16[1024,1024]{0,1:T(8,128)(2,1)} async-done(((bf16[1024,1024]{0,1:T(8,128)(2,1)}), bf16[1024,1024]{0,1:T(8,128)(2,1)}) %all-reduce.6.cloned.1.call-update) | async-done | bytes 2097168 | tf_op jit(solution)/shard_map/psum | solution.py:14
  119.6 5.9 fusion.87
  125.6 36.5 %while.54 = (s32[]{:T(128)}, bf16[6,1024,64]{1,2,0:T(8,128)(2,1)S(1)}, f32[6,1024]{1,0:T(8,128)S(1)}, bf16[6,1024,64]{2,1,0:T(8,128)(2,1)}, bf16[6,1024,64]{2,1,...) while((s32[]{:T(128)}, ...), condition=%wide.region_6.7_spmd.clone, body=%wide.region_3.6_spmd.clone.sunk | while | flops 284228608 | bytes 17747064 | solution.py:181
  125.6 3.5 fusion.200
  131.6 3.5 fusion.200
  137.7 3.5 fusion.200
  143.8 3.5 fusion.200
  149.9 3.5 fusion.200
  156.0 3.5 fusion.200
  162.9 4.0 fusion.128
  167.3 43.2 %reduce-scatter.5.cloned.1.call-done = f32[512,768]{1,0:T(8,128)} async-done(((f32[1024,768]{1,0:T(8,128)}), f32[512,768]{1,0:T(8,128)}) %reduce-scatter.5.cloned.1.call-update) | async-done | bytes 1572880 | tf_op jit(solution)/shard_map/reduce_scatter | solution.py:192
  215.2 26.7 %all-gather.7.cloned.1.call-done = bf16[1024,768]{1,0:T(8,128)(2,1)} async-done(((bf16[512,768]{1,0:T(8,128)(2,1)}), bf16[1024,768]{1,0:T(8,128)(2,1)}) %all-gather.7.cloned.1.call-update) | async-done | bytes 1572880 | tf_op jit(solution)/shard_map/all_gather | solution.py:200
  241.9 7.4 fusion.129
  249.3 21.2 %all-gather.9.cloned.1.call-done = bf16[1024,768]{1,0:T(8,128)(2,1)} async-done(((bf16[512,768]{1,0:T(8,128)(2,1)}), bf16[1024,768]{1,0:T(8,128)(2,1)}) %all-gather.9.cloned.1.call-update) | async-done | bytes 1572880 | tf_op jit(solution)/shard_map/all_gather | solution.py:209
  270.6 19.0 %add_convert_fusion = (bf16[1024,1536]{1,0:T(8,128)(2,1)S(1)}, f32[1024,1536]{1,0:T(8,128)}) fusion(f32[1024,1536]{1,0:T(8,128)} %fusion.129, bf16[1024,768]{1,0:T(8,128)(2,1)} %all-gather.9.cloned.1.call-done, bf16[1536,768]{1,0:T(8,128)(2,1)S(1)} %copy-done), kind=kOutput, calls=%fused_computation.71 | convolution fusion | flops 2529165312 | bytes 19660800 | tf_op jit(solution)/shard_map/rd,fd->rf/dot_general | solution.py:211
  291.3 4.3 fusion.130
  295.7 6.2 multiply_convert_fusion
  303.6 3.7 convolution_convert_fusion
  307.4 31.8 %reduce-scatter.9.cloned.1.call-done = f32[512,768]{1,0:T(8,128)} async-done(((f32[1024,768]{1,0:T(8,128)}), f32[512,768]{1,0:T(8,128)}) %reduce-scatter.9.cloned.1.call-update) | async-done | bytes 1572880 | tf_op jit(solution)/shard_map/reduce_scatter | solution.py:217
  339.2 2.6 multiply_reduce_fusion.2
  341.8 25.9 %reduce-scatter.7.cloned.1.call-done = bf16[512,768]{1,0:T(8,128)(2,1)} async-done(((bf16[1024,768]{1,0:T(8,128)(2,1)}), bf16[512,768]{1,0:T(8,128)(2,1)}) %reduce-scatter.7.cloned.1.call-update) | async-done | bytes 786448 | tf_op jit(solution)/shard_map/reduce_scatter | solution.py:203
  367.6 4.0 fusion.124
  372.1 2.6 slice_bitcast_fusion.3
  374.7 3.1 slice_bitcast_fusion
  377.8 21.2 %all-gather.11.cloned.1.call-done = bf16[1024,768]{1,0:T(8,128)(2,1)} async-done(((bf16[512,768]{1,0:T(8,128)(2,1)}), bf16[1024,768]{1,0:T(8,128)(2,1)}) %all-gather.11.cloned.1.call-update) | async-done | bytes 1572880 | tf_op jit(solution)/shard_map/all_gather | solution.py:227
  403.3 5.4 multiply_reduce_fusion.1
  408.8 4.2 fusion.98
  413.0 81.9 %while.55 = (s32[]{:T(128)}, f32[1024,1024]{0,1:T(8,128)}, bf16[5,1024,64]{1,2,0:T(8,128)(2,1)}, bf16[5,1024,64]{1,2,0:T(8,128)(2,1)}, bf16[5,1024,64]{1,2,0:T(8...) while((s32[]{:T(128)}, f32[1024,1024]{0,1:T(8,128)}, ...), condition=%wide.region_17.18_spmd.clone, body=%wide.region_15.17_spmd.clone.sunk | while | flops 689241088 | bytes 96635104 | solution.py:250
  415.3 4.2 multiply_reduce_fusion.7
  419.5 2.5 fusion.215
  422.1 2.6 fusion.212
  424.6 2.6 fusion.214
  431.7 4.2 multiply_reduce_fusion.7
  435.9 2.5 fusion.215
  438.4 2.6 fusion.212
  441.0 2.6 fusion.214
  448.1 4.2 multiply_reduce_fusion.7
  452.3 2.5 fusion.215
  454.8 2.6 fusion.212
  457.4 2.6 fusion.214
  464.4 4.2 multiply_reduce_fusion.7
  468.6 2.5 fusion.215
  471.2 2.6 fusion.212
  473.8 2.6 fusion.214
  480.8 4.2 multiply_reduce_fusion.7
  485.0 2.5 fusion.215
  487.5 2.6 fusion.212
  490.1 2.6 fusion.214
  494.8 2.7 convert_bitcast_fusion
  505.5 40.5 %collective-permute-done = bf16[1,1024,1024]{1,2,0:T(8,128)(2,1)S(1)} collective-permute-done((bf16[1,1024,1024]{1,2,0:T(8,128)(2,1)S(1)}, bf16[1,1024,1024]{1,2,0:T(8,128)(2,1)S(1)}, u32[]{:S(2)}, u32[]{:S(2)}) %collective-permute-start) | collective-permute-done | bytes 2097184 | tf_op jit(solution)/shard_map/ppermute | solution.py:20
  546.0 7.4 fusion.71
  553.4 3.3 fusion.118
  556.7 3.0 fusion.119
  564.3 7.4 fusion.138
  571.7 4.4 fusion.137
  584.0 7.3 reduce-scatter.11.cloned.1.call-done
  593.3 59.6 %all-reduce = (f32[768]{0:T(1024)S(1)}, f32[768]{0:T(1024)S(1)}, f32[768]{0:T(1024)S(1)}, f32[768]{0:T(1024)S(1)}) all-reduce(f32[768]{0:T(1024)S(1)} %get-tuple-element.247, f32[768]{0:T(1024)S(1)} %get-tuple-element.251, f32[768]{0:T(1024)S(1)} %get-tuple-element.244, ...), channel_id=1, replica_groups=mesh['dp'=16,'tensor'=2] {'dp'}, use_global_device_ids=true, to_apply=%region_22.23 | all-reduce | flops 3072 | bytes 24576 | tf_op jit(solution)/shard_map/psum | solution.py:305
  653.0 6.6 all-reduce.2
  659.5 2.6 fusion.104
  662.1 196.4 %all-reduce.8.cloned.1.call-done = (f32[768,384]{1,0:T(8,128)}, f32[768,384]{1,0:T(8,128)}, f32[768,384]{1,0:T(8,128)}, f32[384,768]{1,0:T(8,128)}, f32[768,1536]{1,0:T(8,128)}, /*index=5*/f32[1536,768]{1,0:T(8,128)}) async-done(((f32[768,384]{1,0:T(8,128)}, f32[768,384]{1,0:T(8,128)}, f32[768,384]{1,0:T(8,128)}, f32[384,768]{1,0:T(8,128)}, f32[768,1536]{1,0:T(8,128)}, /*index=5*/f32[1536,768]{1,0:T(8,128)}), ...) | async-done | bytes 14155792 | tf_op jit(solution)/shard_map/psum | solution.py:305
  858.6 2.5 copy.68
  864.7 2.4 copy.72
  (231 shorter events, 98.0 us)
Async XLA Ops:
  7.2 263.4 %copy-start = (bf16[1536,768]{1,0:T(8,128)(2,1)S(1)}, bf16[1536,768]{1,0:T(8,128)(2,1)}, u32[]{:S(2)}) copy-start(bf16[1536,768]{1,0:T(8,128)(2,1)} %param.30) | copy-start | bytes 7077892
  7.2 6.1 copy-start.43
  7.2 35.5 %all-gather.5.cloned.1.call-start = ((), (), s32[]{:S(2)}) async-start(), calls=%async_computation.4 | async-start | bytes 2359296 | tf_op jit(solution)/shard_map/all_gather | solution.py:160
  13.2 106.4 %all-reduce.6.cloned.1.call-start = ((), (), s32[]{:S(2)}) async-start(), calls=%async_computation.5 | async-start | bytes 4194304 | tf_op jit(solution)/shard_map/psum | solution.py:14
  46.6 3.9 copy-start.41
  56.5 154.0 %reduce-scatter.5.cloned.1.call-start = ((), (), s32[]{:S(2)}) async-start(), calls=%async_computation.6 | async-start | bytes 4718592 | tf_op jit(solution)/shard_map/reduce_scatter | solution.py:192
  60.5 65.0 %copy-start.26 = (bf16[6,1024,64]{1,2,0:T(8,128)(2,1)S(1)}, bf16[6,1024,64]{1,2,0:T(8,128)(2,1)}, u32[]{:S(2)}) copy-start(bf16[6,1024,64]{1,2,0:T(8,128)(2,1)} %custom-call) | copy-start | bytes 2359300
  162.9 47.6 %copy-start.10 = (bf16[512,768]{1,0:T(8,128)(2,1)S(1)}, bf16[512,768]{1,0:T(8,128)(2,1)}, u32[]{:S(2)}) copy-start(bf16[512,768]{1,0:T(8,128)(2,1)} %param.18) | copy-start | bytes 2359300
  167.0 46.3 %copy-start.37 = (f32[768]{0:T(1024)S(1)}, f32[768]{0:T(1024)}, u32[]{:S(2)}) copy-start(f32[768]{0:T(1024)} %param.27) | copy-start | bytes 9220
  167.0 46.3 %copy-start.42 = (f32[768]{0:T(1024)S(1)}, f32[768]{0:T(1024)}, u32[]{:S(2)}) copy-start(f32[768]{0:T(1024)} %param.28) | copy-start | bytes 9220
  167.0 74.9 %all-gather.7.cloned.1.call-start = ((), (), s32[]{:S(2)}) async-start(), calls=%async_computation.7 | async-start | bytes 2359296 | tf_op jit(solution)/shard_map/all_gather | solution.py:200
  214.6 56.0 %all-gather.9.cloned.1.call-start = ((), (), s32[]{:S(2)}) async-start(), calls=%async_computation.9 | async-start | bytes 2359296 | tf_op jit(solution)/shard_map/all_gather | solution.py:209
  215.2 124.0 %reduce-scatter.9.cloned.1.call-start = ((), (), s32[]{:S(2)}) async-start(), calls=%async_computation.10 | async-start | bytes 4718592 | tf_op jit(solution)/shard_map/reduce_scatter | solution.py:217
  270.6 20.7 %copy-start.44 = (bf16[768,1536]{1,0:T(8,128)(2,1)S(1)}, bf16[768,1536]{1,0:T(8,128)(2,1)}, u32[]{:S(2)}) copy-start(bf16[768,1536]{1,0:T(8,128)(2,1)} %param.29) | copy-start | bytes 7077892
  289.5 1.8 copy-start.19
  295.7 71.9 %reduce-scatter.7.cloned.1.call-start = ((), (), s32[]{:S(2)}) async-start(), calls=%async_computation.8 | async-start | bytes 2359296 | tf_op jit(solution)/shard_map/reduce_scatter | solution.py:203
  307.3 60.3 %copy-start.6 = (f32[512,768]{1,0:T(8,128)S(1)}, f32[512,768]{1,0:T(8,128)}, u32[]{:S(2)}) copy-start(f32[512,768]{1,0:T(8,128)} %copy-done.5) | copy-start | bytes 4718596
  307.3 60.3 %copy-start.18 = (bf16[512,768]{1,0:T(8,128)(2,1)S(1)}, bf16[512,768]{1,0:T(8,128)(2,1)}, u32[]{:S(2)}) copy-start(bf16[512,768]{1,0:T(8,128)(2,1)} %param.31) | copy-start | bytes 2359300
  307.4 91.6 %all-gather.11.cloned.1.call-start = ((), (), s32[]{:S(2)}) async-start(), calls=%async_computation.11 | async-start | bytes 2359296 | tf_op jit(solution)/shard_map/all_gather | solution.py:227
  371.6 3.1 copy-start.13
  371.6 219.8 %reduce-scatter.11.cloned.1.call-start = ((), (), s32[]{:S(2)}) async-start(), calls=%async_computation.12 | async-start | bytes 2359296 | tf_op jit(solution)/shard_map/reduce_scatter | solution.py:281
  374.7 24.3 %copy-start.31 = (bf16[384,768]{1,0:T(8,128)(2,1)S(1)}, bf16[384,768]{1,0:T(8,128)(2,1)}, u32[]{:S(2)}) copy-start(bf16[384,768]{1,0:T(8,128)(2,1)} %param.26) | copy-start | bytes 1769476
  402.1 6.7 copy-start.12
  408.8 4.2 copy-start.7
  413.0 2.3 copy-start.17
  419.5 2.5 copy-start.2
  424.6 4.7 copy-start.3
  429.3 2.3 copy-start.17
  435.9 2.5 copy-start.2
  441.0 4.7 copy-start.3
  445.7 2.3 copy-start.17
  452.3 2.5 copy-start.2
  457.4 4.7 copy-start.3
  462.1 2.3 copy-start.17
  468.6 2.5 copy-start.2
  473.7 4.7 copy-start.3
  478.5 2.3 copy-start.17
  485.0 2.5 copy-start.2
  490.1 4.7 copy-start.3
  494.8 4.3 copy-start.8
  497.5 4.7 copy-start.9
  497.5 48.5 %collective-permute-start = (bf16[1,1024,1024]{1,2,0:T(8,128)(2,1)S(1)}, bf16[1,1024,1024]{1,2,0:T(8,128)(2,1)S(1)}, u32[]{:S(2)}, u32[]{:S(2)}) collective-permute-start(bf16[1,1024,1024]{1,2,0:T(8,128)(2,1)S(1)} %convert_bitcast_fusion), channel_id=1, source_target_pairs={{1,0},{3,2},{5,4},{7,6},{9,8},{11,10},{13,12},{15,14},{17,16},{19,... | collective-permute-start | bytes 6291464 | tf_op jit(solution)/shard_map/ppermute | solution.py:20
  500.8 45.2 %copy-start.16 = (f32[1024,1024]{0,1:T(8,128)S(1)}, f32[1024,1024]{0,1:T(8,128)}, u32[]{:S(2)}) copy-start(f32[1024,1024]{0,1:T(8,128)} %get-tuple-element.328) | copy-start | bytes 12582916
  502.2 43.8 %copy-start.4 = (f32[1024,1024]{0,1:T(8,128)S(1)}, f32[1024,1024]{0,1:T(8,128)}, u32[]{:S(2)}) copy-start(f32[1024,1024]{0,1:T(8,128)} %get-tuple-element.188) | copy-start | bytes 12582916
  556.7 3.0 copy-start.30
  556.7 3.1 copy-start.32
  564.2 294.3 %all-reduce.8.cloned.1.call-start = ((), (), s32[]{:S(2)}) async-start(), calls=%async_computation.13 | async-start | bytes 28311552 | tf_op jit(solution)/shard_map/psum | solution.py:305
  564.3 7.4 copy-start.20
  564.3 7.4 copy-start.22
  571.7 4.4 copy-start.28
  571.7 4.4 copy-start.46
  576.1 1.8 copy-start.45
  584.0 7.4 copy-start.11
  584.0 7.4 copy-start.36
  584.0 7.4 copy-start.38
  584.0 7.4 copy-start.40
  584.0 75.5 %copy-start.14 = (f32[512,768]{1,0:T(8,128)S(1)}, f32[512,768]{1,0:T(8,128)}, u32[]{:S(2)}) copy-start(f32[512,768]{1,0:T(8,128)} %get-tuple-element.313) | copy-start | bytes 4718596
  858.6 2.5 copy-start.25
  858.6 3.5 copy-start.24
  858.6 4.5 copy-start.23
  861.1 3.6 copy-start.15
  863.1 4.0 slice-start
  864.7 2.5 slice-start.1
  864.7 4.7 copy-start.1
  (8 other events, 9.4 us)
Sparse Core Ops, SparseCore 0:
  13.4 29.2 all-gather.4
  56.7 62.9 all-reduce.5
  167.1 43.3 reduce-scatter.4
  214.7 27.2 all-gather.6
  243.3 27.2 all-gather.8
  295.8 43.3 reduce-scatter.8
  341.5 26.0 reduce-scatter.6
  371.7 27.2 all-gather.10
  564.4 26.9 reduce-scatter.10
  598.3 260.1 all-reduce.7
where the time goes:
time: 888 us; the launch traced here: 877 us
  waiting for transfers between devices  503 us (57%)
  matrix products  206 us (23%)
  blocking collectives  66.2 us (7%)
  other arithmetic  50.8 us (6%)
  local copies, waits for them, and re-layouts  32.1 us (4%)
  between operations  15.1 us (2%)
    psum x1, waiting for transfers between devices, body(): lax.psum((query_grad, key_grad, value_grad, out_grad, up_grad, down_grad,...  196 us
    psum x1, blocking collectives, body(): lax.psum((query_grad, key_grad, value_grad, out_grad, up_grad, down_grad,...  59.6 us
    psum x1, waiting for transfers between devices, broadcast(): return lax.psum(kept, axis)  59.1 us
    reduce_scatter x1, waiting for transfers between devices, body(): lax.psum_scatter(jnp.dot(heads_flat, w_out, preferred_element_type=jnp.fl...  43.2 us
    ppermute x1, waiting for transfers between devices, shifted(): return lax.ppermute(shard, axis, pairs)  40.5 us
    reduce_scatter x1, waiting for transfers between devices, body(): lax.psum_scatter(jnp.einsum('rf,df->rd', grad_upper, w_up, preferred_elem...  31.8 us
    all_gather x1, waiting for transfers between devices, body(): lax.all_gather(normed1.astype(jnp.bfloat16), 'tensor', axis=0, tiled=True)  29.4 us
    all_gather x1, waiting for transfers between devices, body(): lax.all_gather(normed2.astype(jnp.bfloat16), 'tensor', axis=0, tiled=True)  26.7 us
  transfers between devices with their start and end apart: 11, of which 11 were waited for; matrix products, arithmetic and copies ran while one was open for 7% of the time, Pallas kernels for 0%

commit v1 on v0

v1 whole, which is shorter than its diff:
```python
import functools

import jax
import jax.numpy as jnp
from jax import lax
from jax.experimental import pallas as pl
from jax.experimental.pallas import tpu as pltpu
from jax.sharding import PartitionSpec as P

HEAD_DIM = 64
EPS = 1e-05
FAR = 1e30
FORWARD_BLOCK = 512
BF16 = jnp.bfloat16
F32 = jnp.float32
TN = (((0,), (0,)), ((), ()))
NT = (((1,), (1,)), ((), ()))
NN = (((1,), (0,)), ((), ()))
TT = (((0,), (1,)), ((), ()))
ERF_P = 0.39
ERF_C = (
    0.23532589847272212,
    0.09138415344709826,
    0.6495700167142381,
    -0.6354134214178592,
    0.8866724519682867,
    -0.22753910091022167,
)


def dot(left, right, dims):
    return lax.dot_general(left, right, dims, preferred_element_type=F32)


def cost(flops, nbytes):
    return pl.CostEstimate(flops=int(flops), bytes_accessed=int(nbytes), transcendentals=0)


def params():
    return pltpu.CompilerParams(vmem_limit_bytes=58 << 20)


def sds(shape, dtype):
    return jax.ShapeDtypeStruct(shape, dtype)


SMEM = pl.BlockSpec(memory_space=pltpu.SMEM)


def whole(shape):
    return pl.BlockSpec(shape, lambda *_: (0,) * len(shape))


def normalize(values):
    center = values - jnp.mean(values, axis=-1, keepdims=True)
    inverse = lax.rsqrt(jnp.mean(center * center, axis=-1, keepdims=True) + EPS)
    return center * inverse, inverse


def norm_back(grad_normed, scaled, inverse, gain):
    grad_scaled = grad_normed * gain
    return inverse * (
        grad_scaled
        - jnp.mean(grad_scaled, axis=-1, keepdims=True)
        - scaled * jnp.mean(grad_scaled * scaled, axis=-1, keepdims=True)
    )


def gelu_pair(x):
    z = jnp.abs(x) * 0.7071067811865476
    t = 1.0 / (1.0 + ERF_P * z)
    poly = ERF_C[5]
    for coefficient in ERF_C[4::-1]:
        poly = poly * t + coefficient
    bell = jnp.exp(-0.5 * x * x)
    tail = 0.5 * poly * t * bell
    phi = jnp.where(x >= 0, 1.0 - tail, tail)
    return x * phi, phi + x * bell * 0.3989422804014327


def norm1_kernel(tokens, gain, shift, out):
    scaled, _ = normalize(tokens[...].astype(F32))
    out[...] = (scaled * gain[...] + shift[...]).astype(BF16)


def norm1(tokens, gain, shift):
    return pl.pallas_call(
        norm1_kernel,
        out_shape=sds(tokens.shape, BF16),
        compiler_params=params(),
        cost_estimate=cost(0, 4 * tokens.size),
    )(tokens, gain, shift)


def masks(seg_pad, cols, low, high):
    width = high - low
    seg_row = seg_pad[0:1, low:high]
    pad_row = seg_pad[1:2, low:high]
    row_key = jnp.where(pad_row > 0, seg_row, -2.0)
    col_seg = cols[:high, 0:1]
    col_pad = cols[:high, 1:2]
    col_key = jnp.where(col_pad > 0, col_seg, -1.0)
    key_at = lax.broadcasted_iota(jnp.int32, (high, width), 0)
    query_at = lax.broadcasted_iota(jnp.int32, (high, width), 1) + low
    allowed = ((col_key == seg_row) & (key_at <= query_at)) | (key_at == query_at)
    picked = (col_key == row_key) & (key_at < query_at)
    return allowed, picked


def penalty_kernel(block, core, n1_own, n1_other, wqk0, seg_pad, n1_out, penalty, qk0):
    seq = n1_out.shape[0]
    half = seq // 2
    here = core[0]
    n1_out[pl.ds(pl.multiple_of(here * half, half), half), :] = n1_own[...]
    n1_out[pl.ds(pl.multiple_of((1 - here) * half, half), half), :] = n1_other[...]
    qk = dot(wqk0[...], n1_out[...], TT)
    q0 = (qk[:HEAD_DIM].astype(BF16) * 0.125).astype(BF16)
    k0 = qk[HEAD_DIM:].astype(BF16)
    qk0[:HEAD_DIM, :] = q0
    qk0[HEAD_DIM:, :] = k0
    seg_value = seg_pad[...]
    cols = seg_value.T
    earlier = lax.broadcasted_iota(jnp.int32, (block, block + 128), 0)
    later = lax.broadcasted_iota(jnp.int32, (block, block + 128), 1)
    sums = ((earlier < later) | (later >= block)).astype(F32).astype(BF16)
    carry = jnp.zeros((seq, 128), F32)
    for low in range(0, seq, block):
        high = low + block
        allowed, picked = masks(seg_value, cols, low, high)
        score = dot(k0[:, :high], q0[:, low:high], TN)
        small = jnp.exp(-jnp.abs(score))
        log1p = jnp.where(small < 1e-3, small - 0.5 * small * small, jnp.log(1.0 + small))
        select = jnp.where(picked, jnp.maximum(score, 0.0) + log1p, 0.0).astype(BF16)
        total = dot(select, sums, NN)
        before = jnp.concatenate([carry[:high]] * (block // 128), axis=1)
        penalty[:high, low:high] = jnp.where(allowed, total[:, :block] + before, FAR)
        if high % FORWARD_BLOCK:
            edge = high + FORWARD_BLOCK - high % FORWARD_BLOCK
            penalty[high:edge, low:high] = jnp.full((edge - high, block), FAR, F32)
        carry = jnp.concatenate([carry[:high] + total[:, block:], carry[high:]], axis=0)


def penalty_call(core, n1_own, n1_other, wqk0, seg_pad):
    half, dim = n1_own.shape
    seq = 2 * half
    return pl.pallas_call(
        functools.partial(penalty_kernel, 256),
        in_specs=[SMEM] + [pl.BlockSpec(memory_space=pltpu.VMEM)] * 4,
        out_shape=[sds((seq, dim), BF16), sds((seq, seq), F32), sds((2 * HEAD_DIM, seq), BF16)],
        compiler_params=params(),
        cost_estimate=cost(3e9, 8e6),
    )(core, n1_own, n1_other, wqk0, seg_pad)


def forward_kernel(block, n1, weights, penalty, qkv, out, lse):
    head = pl.program_id(0)
    third = qkv.shape[0] // 3
    seq = qkv.shape[1]

    @pl.when(head == 0)
    def _():
        product = dot(weights[...], n1[...], TT).astype(BF16)
        qkv[:third, :] = (product[:third] * 0.125).astype(BF16)
        qkv[third:, :] = product[third:]

    at = pl.multiple_of(head * HEAD_DIM, HEAD_DIM)
    query = qkv[pl.ds(at, HEAD_DIM), :]
    key = qkv[pl.ds(third + at, HEAD_DIM), :]
    value = qkv[pl.ds(2 * third + at, HEAD_DIM), :]
    value = jnp.concatenate([value, jnp.ones((16, seq), BF16)], axis=0)
    for low in range(0, seq, block):
        high = low + block
        logits = dot(key[:, :high], query[:, low:high], TN) - penalty[:high, low:high]
        largest = jnp.max(logits, axis=0, keepdims=True)
        weight = jnp.exp(logits - largest).astype(BF16)
        result = dot(value[:, :high], weight, NN)
        total = result[HEAD_DIM : HEAD_DIM + 1, :]
        out[:, low:high] = (result[:HEAD_DIM] / total).astype(BF16)
        lse[:, low:high] = largest + jnp.log(total)


def forward_call(n1, weights, penalty):
    seq, dim = n1.shape
    width = weights.shape[1]
    heads = width // (3 * HEAD_DIM)
    return pl.pallas_call(
        functools.partial(forward_kernel, FORWARD_BLOCK),
        grid=(heads,),
        in_specs=[whole((seq, dim)), whole((dim, width)), whole((seq, seq))],
        out_specs=[
            whole((width, seq)),
            pl.BlockSpec((HEAD_DIM, seq), lambda h: (h, 0)),
            pl.BlockSpec((None, 1, seq), lambda h: (h, 0, 0)),
        ],
        out_shape=[
            sds((width, seq), BF16),
            sds((heads * HEAD_DIM, seq), BF16),
            sds((heads, 1, seq), F32),
        ],
        compiler_params=params(),
        cost_estimate=cost(5e9, 8e6),
    )(n1, weights, penalty)


def project_kernel(core, out_l, out_r, w_l, w_r, own, send):
    half = own.shape[0]
    here = core[0]
    mixed = jnp.concatenate([w_l[...], w_r[...]], axis=0)

    def part(which):
        at = pl.ds(pl.multiple_of(which * half, half), half)
        heads = jnp.concatenate([out_l[:, at], out_r[:, at]], axis=0)
        return dot(heads, mixed, TN)

    send[...] = part(1 - here).astype(BF16)
    own[...] = part(here)


def project_call(core, out_l, out_r, w_l, w_r):
    half, dim = out_l.shape[1] // 2, w_l.shape[1]
    return pl.pallas_call(
        project_kernel,
        in_specs=[SMEM] + [pl.BlockSpec(memory_space=pltpu.VMEM)] * 4,
        out_shape=[sds((half, dim), F32), sds((half, dim), BF16)],
        compiler_params=params(),
        cost_estimate=cost(6e8, 5e6),
    )(core, out_l, out_r, w_l, w_r)


def norm2_kernel(tokens, own, received, gain, shift, hidden, out):
    total = tokens[...].astype(F32) + (own[...] + received[...].astype(F32))
    hidden[...] = total
    scaled, _ = normalize(total)
    out[...] = (scaled * gain[...] + shift[...]).astype(BF16)


def norm2_call(tokens, own, received, gain, shift):
    return pl.pallas_call(
        norm2_kernel,
        out_shape=[sds(tokens.shape, F32), sds(tokens.shape, BF16)],
        compiler_params=params(),
        cost_estimate=cost(0, 14 * tokens.size),
    )(tokens, own, received, gain, shift)


def mlp_kernel(first, steps, *refs):
    if first:
        n2_other, n2_own, g_other, g_own, w_up, w_down = refs[:6]
        rest = refs[6:]
        before = None
    else:
        n2_other, n2_own, g_other, g_own, w_up, w_down = refs[:6]
        before = refs[6:10]
        rest = refs[10:]
    mixed_send, mixed_own, back_send, back_own, w_grads, sums = rest
    step = pl.program_id(0)
    dim = w_up.shape[0]

    def work(n2, grad, mixed_out, back_out, mixed_in, back_in):
        rows = n2[...]
        grad_rows = grad[...]
        up_values = dot(rows, w_up[...], NN)
        active, slope = gelu_pair(up_values)
        active = active.astype(BF16)
        grad_up = (dot(grad_rows, w_down[...], NT) * slope).astype(BF16)
        back = dot(grad_up, w_up[...], NT)
        mixed = dot(active, w_down[...], NN)
        if mixed_in is not None:
            back = back + back_in[...]
            mixed = mixed + mixed_in[...]
        back_out[...] = back.astype(back_out.dtype)
        mixed_out[...] = mixed.astype(mixed_out.dtype)
        up_grad = dot(rows, grad_up, TN)
        down_grad = dot(active, grad_rows, TN)

        @pl.when(step == 0)
        def _():
            sums[:dim, :] = up_grad
            sums[dim:, :] = down_grad

        @pl.when(step > 0)
        def _():
            sums[:dim, :] += up_grad
            sums[dim:, :] += down_grad

    @pl.when(step < steps // 2)
    def _():
        ins = (None, None) if first else (before[0], before[2])
        work(n2_other, g_other, mixed_send, back_send, *ins)

    @pl.when(step >= steps // 2)
    def _():
        ins = (None, None) if first else (before[1], before[3])
        work(n2_own, g_own, mixed_own, back_own, *ins)

    @pl.when(step == steps - 1)
    def _():
        w_grads[...] = sums[...].astype(w_grads.dtype)


def mlp_call(n2_other, n2_own, g_other, g_own, w_up, w_down, before=None):
    half, dim = n2_own.shape
    units = w_up.shape[1]
    block = 256
    steps = 2 * half // block
    last = steps // 2 - 1
    sent = pl.BlockSpec((block, dim), lambda i: (jnp.minimum(i, last), 0))
    kept = pl.BlockSpec((block, dim), lambda i: (jnp.maximum(i - last - 1, 0), 0))
    first = before is None
    operands = (n2_other, n2_own, g_other, g_own, w_up, w_down) + (() if first else tuple(before))
    in_specs = [sent, kept, sent, kept, whole((dim, units)), whole((units, dim))]
    in_specs += [] if first else [sent, kept, sent, kept]
    sent_type = F32 if first else BF16
    return pl.pallas_call(
        functools.partial(mlp_kernel, first, steps),
        grid=(steps,),
        in_specs=in_specs,
        out_specs=[sent, kept, sent, kept, whole((dim + units, dim))],
        out_shape=[
            sds((half, dim), sent_type),
            sds((half, dim), F32),
            sds((half, dim), sent_type),
            sds((half, dim), F32),
            sds((dim + units, dim), F32 if first else BF16),
        ],
        scratch_shapes=[pltpu.VMEM((dim + units, dim), F32)],
        compiler_params=params(),
        cost_estimate=cost(7.2e9, 18e6),
    )(*operands)


def norm2_back_kernel(hidden, own, received, grad, gain, grad_hidden, low, sums):
    normed_grad = own[...] + received[...].astype(F32)
    scaled, inverse = normalize(hidden[...])
    total = grad[...].astype(F32) + norm_back(normed_grad, scaled, inverse, gain[...])
    grad_hidden[...] = total
    low[...] = total.astype(BF16)
    sums[...] = jnp.zeros(sums.shape, F32)
    sums[0:1, :] = jnp.sum(normed_grad * scaled, axis=0, keepdims=True)
    sums[1:2, :] = jnp.sum(normed_grad, axis=0, keepdims=True)


def norm2_back_call(hidden, own, received, grad, gain):
    return pl.pallas_call(
        norm2_back_kernel,
        out_shape=[
            sds(hidden.shape, F32),
            sds(hidden.shape, BF16),
            sds((8, hidden.shape[1]), F32),
        ],
        compiler_params=params(),
        cost_estimate=cost(0, 18 * hidden.size),
    )(hidden, own, received, grad, gain)


def backward_kernel(first, block, *refs):
    core, g_own, g_other, w_out, heads_out, qkv, lse, penalty = refs[:8]
    if first:
        before = None
        grads, w_grad, logit_sum, grad_full, grad_heads, key_sum, value_sum = refs[8:]
        low_sum = None
    else:
        before = refs[8]
        grads, w_grad, logit_sum, low_sum, grad_full, grad_heads, key_sum, value_sum = refs[9:]
    head = pl.program_id(0)
    third = qkv.shape[0] // 3
    seq = qkv.shape[1]
    half = seq // 2

    @pl.when(head == 0)
    def _():
        here = core[0]
        grad_full[pl.ds(pl.multiple_of(here * half, half), half), :] = g_own[...]
        grad_full[pl.ds(pl.multiple_of((1 - here) * half, half), half), :] = g_other[...]
        whole_grad = grad_full[...]
        grad_heads[...] = dot(w_out[...], whole_grad, NT).astype(BF16)
        w_grad[...] = dot(heads_out[...], whole_grad, NN).astype(w_grad.dtype)

    at = pl.multiple_of(head * HEAD_DIM, HEAD_DIM)
    query = qkv[pl.ds(at, HEAD_DIM), :]
    key = qkv[pl.ds(third + at, HEAD_DIM), :]
    value = qkv[pl.ds(2 * third + at, HEAD_DIM), :]
    grad = grad_heads[pl.ds(at, HEAD_DIM), :]
    for low in range(0, seq, block):
        high = low + block
        cols = slice(low, high)
        score = dot(key[:, :high], query[:, cols], TN)
        probs = jnp.exp(score - penalty[:high, cols] - lse[:, cols])
        grad_probs = dot(value[:, :high], grad[:, cols], TN)
        row_dot = jnp.sum(probs * grad_probs, axis=0, keepdims=True)
        grad_logits = probs * (grad_probs - row_dot)
        if first:

            @pl.when(head == 0)
            def _():
                logit_sum[:high, cols] = grad_logits

            @pl.when(head > 0)
            def _():
                logit_sum[:high, cols] += grad_logits

        else:

            @pl.when(head == 0)
            def _():
                logit_sum[:high, cols] = before[:high, cols] + grad_logits

            @pl.when(head > 0)
            def _():
                logit_sum[:high, cols] += grad_logits

        low_logits = grad_logits.astype(BF16)
        low_probs = probs.astype(BF16)
        grads[pl.ds(at, HEAD_DIM), cols] = (
            dot(key[:, :high], low_logits, NN) * 0.125
        ).astype(BF16)
        value_new = dot(grad[:, cols], low_probs, NT)
        key_new = dot(query[:, cols], low_logits, NT)
        if low:
            key_sum[:, :low] += key_new[:, :low]
            value_sum[:, :low] += value_new[:, :low]
        key_sum[:, cols] = key_new[:, low:]
        value_sum[:, cols] = value_new[:, low:]
    grads[pl.ds(third + at, HEAD_DIM), :] = key_sum[...].astype(BF16)
    grads[pl.ds(2 * third + at, HEAD_DIM), :] = value_sum[...].astype(BF16)
    if low_sum is not None:

        @pl.when(head == pl.num_programs(0) - 1)
        def _():
            for low in range(0, seq, block):
                high = low + block
                low_sum[:high, low:high] = logit_sum[:high, low:high].astype(BF16)


def backward_call(core, g_own, g_other, w_out, heads_out, qkv, lse, penalty, before=None):
    width, seq = qkv.shape
    heads = width // (3 * HEAD_DIM)
    half, dim = g_own.shape
    first = before is None
    square = whole((seq, seq))
    operands = (core, g_own, g_other, w_out, heads_out, qkv, lse, penalty)
    in_specs = [
        SMEM,
        whole((half, dim)),
        whole((half, dim)),
        whole(w_out.shape),
        whole(heads_out.shape),
        whole((width, seq)),
        pl.BlockSpec((None, 1, seq), lambda h: (h, 0, 0)),
        square,
    ]
    out_specs = [whole((width, seq)), whole(w_out.shape), square]
    out_shape = [sds((width, seq), BF16), sds(w_out.shape, F32), sds((seq, seq), F32)]
    if not first:
        operands += (before,)
        in_specs.append(square)
        out_specs.append(square)
        out_shape.append(sds((seq, seq), BF16))
    return pl.pallas_call(
        functools.partial(backward_kernel, first, 256),
        grid=(heads,),
        in_specs=in_specs,
        out_specs=out_specs,
        out_shape=out_shape,
        scratch_shapes=[
            pltpu.VMEM((seq, dim), BF16),
            pltpu.VMEM((width // 3, seq), BF16),
            pltpu.VMEM((HEAD_DIM, seq), F32),
            pltpu.VMEM((HEAD_DIM, seq), F32),
        ],
        compiler_params=params(),
        cost_estimate=cost(1e10, 16e6),
    )(*operands)


def halves(value):
    high = value.astype(BF16)
    return high, (value - high.astype(F32)).astype(BF16)


def select_back_kernel(block, own, received, qk0, seg_pad, out):
    seq = own.shape[0]
    q0 = qk0[:HEAD_DIM, :]
    k0 = qk0[HEAD_DIM:, :]
    seg_value = seg_pad[...]
    cols = seg_value.T
    later = lax.broadcasted_iota(jnp.int32, (block, block + 128), 0)
    earlier = lax.broadcasted_iota(jnp.int32, (block, block + 128), 1)
    sums = ((later > earlier) | (earlier >= block)).astype(F32).astype(BF16)
    carry = jnp.zeros((seq, 128), F32)
    out[...] = jnp.zeros(out.shape, F32)
    for low in range(seq - block, -1, -block):
        high = low + block
        logit_sum = own[:high, low:high] + received[:high, low:high].astype(F32)
        top, bottom = halves(logit_sum)
        total = dot(top, sums, NN) + dot(bottom, sums, NN)
        after = jnp.concatenate([carry[:high]] * (block // 128), axis=1)
        select_grad = -(total[:, :block] + after)
        carry = carry[:high] + total[:, block:]
        _, picked = masks(seg_value, cols, low, high)
        score = dot(k0[:, :high], q0[:, low:high], TN)
        through = jnp.where(picked, select_grad / (1.0 + jnp.exp(-score)), 0.0)
        top, bottom = halves(through)
        out[:HEAD_DIM, low:high] = 0.125 * (
            dot(k0[:, :high], top, NN) + dot(k0[:, :high], bottom, NN)
        )
        out[HEAD_DIM:, :high] += dot(q0[:, low:high], top, NT) + dot(q0[:, low:high], bottom, NT)


def select_back_call(own, received, qk0, seg_pad):
    return pl.pallas_call(
        functools.partial(select_back_kernel, 256),
        out_shape=sds(qk0.shape, F32),
        compiler_params=params(),
        cost_estimate=cost(4e9, 8e6),
    )(own, received, qk0, seg_pad)


def weights_kernel(core, flags, n1, grads_l, grads_r, extra, w_l, w_r, out_l, out_r, *rest):
    sum_l, sum_r, own, send, all_grads = rest
    width = grads_l.shape[0]
    third = width // 3
    half = own.shape[0]
    all_grads[:width, :] = grads_l[...]
    all_grads[width:, :] = grads_r[...]
    for place, flag in ((0, flags[0]), (width, flags[1])):

        @pl.when(flag > 0)
        def _():
            for at, source in ((place, 0), (place + third, HEAD_DIM)):
                rows = slice(at, at + HEAD_DIM)
                all_grads[rows, :] = (
                    all_grads[rows, :].astype(F32) + extra[source : source + HEAD_DIM, :]
                ).astype(BF16)

    here = core[0]
    both = jnp.concatenate([w_l[...], w_r[...]], axis=1)

    def part(which):
        at = pl.ds(pl.multiple_of(which * half, half), half)
        return dot(all_grads[:, at], both, TT)

    send[...] = part(1 - here).astype(BF16)
    own[...] = part(here)
    product = dot(all_grads[...], n1[...], NN)
    sum_l[:width, :] = product[:width]
    sum_l[width:, :] = out_l[...]
    sum_r[:width, :] = product[width:].astype(BF16)
    sum_r[width:, :] = out_r[...].astype(BF16)


def weights_call(core, flags, n1, grads_l, grads_r, extra, w_l, w_r, out_l, out_r):
    seq, dim = n1.shape
    width = grads_l.shape[0]
    rows = width + out_l.shape[0]
    return pl.pallas_call(
        weights_kernel,
        in_specs=[SMEM, SMEM] + [pl.BlockSpec(memory_space=pltpu.VMEM)] * 8,
        out_shape=[
            sds((rows, dim), F32),
            sds((rows, dim), BF16),
            sds((seq // 2, dim), F32),
            sds((seq // 2, dim), BF16),
        ],
        scratch_shapes=[pltpu.VMEM((2 * width, seq), BF16)],
        compiler_params=params(),
        cost_estimate=cost(4e9, 16e6),
    )(core, flags, n1, grads_l, grads_r, extra, w_l, w_r, out_l, out_r)


def norm1_back_kernel(tokens, own, received, grad_hidden, gain, out, sums):
    normed_grad = own[...] + received[...].astype(F32)
    scaled, inverse = normalize(tokens[...].astype(F32))
    total = grad_hidden[...] + norm_back(normed_grad, scaled, inverse, gain[...])
    out[...] = total.astype(BF16)
    sums[...] = jnp.zeros(sums.shape, F32)
    sums[0:1, :] = jnp.sum(normed_grad * scaled, axis=0, keepdims=True)
    sums[1:2, :] = jnp.sum(normed_grad, axis=0, keepdims=True)


def norm1_back_call(tokens, own, received, grad_hidden, gain):
    return pl.pallas_call(
        norm1_back_kernel,
        out_shape=[sds(tokens.shape, BF16), sds((8, tokens.shape[1]), F32)],
        compiler_params=params(),
        cost_estimate=cost(0, 14 * tokens.size),
    )(tokens, own, received, grad_hidden, gain)


def make_body(devices, parts):
    axes = ("dp", "tensor")
    chips = devices // 2
    masks_in_order = [1 << bit for bit in range(chips.bit_length() - 1)]
    turned = masks_in_order[1:] + masks_in_order[:1]

    def pairs(move):
        found = []
        for device in range(devices):
            for part in range(parts):
                to_chip, to_core, to_part = move(device // 2, device % 2, part)
                source = device * parts + part
                found.append((source, (to_chip * 2 + to_core) * parts + to_part))
        return found

    by_role = pairs(lambda chip, core, part: (chip, part, core))
    by_core = pairs(lambda chip, core, part: (chip, 1 - core, part))
    by_part = pairs(lambda chip, core, part: (chip, core, 1 - part))
    first_part = [pair for pair in by_part if pair[0] % parts == 0]
    first_core = [pair for pair in by_core if (pair[0] // parts) % 2 == 1]
    by_chip = [
        pairs(lambda chip, core, part: (chip ^ (turned[i] if core else masks_in_order[i]), core, part))
        for i in range(len(masks_in_order))
    ]

    def move(value, how):
        return lax.ppermute(value, axes, how)

    def body(
        tokens,
        segment_ids,
        pad_mask,
        norm1_gain,
        norm1_shift,
        w_query,
        w_key,
        w_value,
        w_out,
        norm2_gain,
        norm2_shift,
        w_up,
        w_down,
        cotangent,
    ):
        device = lax.axis_index("dp")
        part = lax.axis_index("tensor")
        core = device % 2
        chip = device // 2
        core_ref = jnp.reshape(core, (1,)).astype(jnp.int32)
        bits = [
            jnp.where(core == 1, (chip & turned[i]) != 0, (chip & masks_in_order[i]) != 0)
            for i in range(len(masks_in_order))
        ]
        gain1, shift1, gain2, shift2 = (
            vector[None, :] for vector in (norm1_gain, norm1_shift, norm2_gain, norm2_shift)
        )
        dim = tokens.shape[1]
        width = w_query.shape[1] // 2
        units = w_up.shape[1] // 2

        mine = move(tokens, by_role)
        first_heads = jnp.concatenate([w_query[:, :HEAD_DIM], w_key[:, :HEAD_DIM]], axis=1)
        first_moved = move(first_heads, first_part)
        wqk0 = jnp.where(part == 0, first_heads, first_moved)
        ints = jnp.concatenate([segment_ids, pad_mask], axis=0)
        ints = jnp.where(core == part, ints, move(ints, by_core)).astype(F32)
        seg_pad = jnp.concatenate([ints, jnp.zeros((6, ints.shape[1]), F32)], axis=0)

        def columns(weight, size):
            return lax.dynamic_slice_in_dim(weight, core * size, size, axis=1)

        def rows(weight, size):
            return lax.dynamic_slice_in_dim(weight, core * size, size, axis=0)

        qkv_l = jnp.concatenate(
            [columns(weight, width) for weight in (w_query, w_key, w_value)], axis=1
        )
        out_l = rows(w_out, width)
        up_l = columns(w_up, units)
        down_l = rows(w_down, units)
        qkv_r = move(qkv_l, by_part)
        out_r = move(out_l, by_part)
        grad_own = move(cotangent, by_role)
        up_r = move(up_l, by_part)
        down_r = move(down_l, by_part)

        n1_own = norm1(mine, gain1, shift1)
        n1_other = move(n1_own, by_core)
        grad_other = move(grad_own, by_core)
        n1, penalty, qk0 = penalty_call(core_ref, n1_own, n1_other, wqk0, seg_pad)
        qkvt_l, heads_l, lse_l = forward_call(n1, qkv_l, penalty)
        qkvt_r, heads_r, lse_r = forward_call(n1, qkv_r, penalty)
        own, send = project_call(core_ref, heads_l, heads_r, out_l, out_r)
        hidden, n2_own = norm2_call(mine, own, move(send, by_core), gain2, shift2)
        n2_other = move(n2_own, by_core)
        *before, ff_l = mlp_call(n2_other, n2_own, grad_other, grad_own, up_l, down_l)
        mixed_send, mixed_own, back_send, back_own, ff_r = mlp_call(
            n2_other, n2_own, grad_other, grad_own, up_r, down_r, before
        )
        grad_hidden, low_own, sums2 = norm2_back_call(
            hidden, back_own, move(back_send, by_core), grad_own, gain2
        )
        low_other = move(low_own, by_core)
        mixed = hidden + (mixed_own + move(mixed_send, by_core).astype(F32))
        mixed = move(mixed.astype(BF16), by_role)

        grads_r, wo_r, sum_r = backward_call(
            core_ref, low_own, low_other, out_r, heads_r, qkvt_r, lse_r, penalty
        )
        grads_l, wo_l, logit_sum, logit_low = backward_call(
            core_ref, low_own, low_other, out_l, heads_l, qkvt_l, lse_l, penalty, sum_r
        )
        extra = select_back_call(logit_sum, move(logit_low, first_core), qk0, seg_pad)
        flags = jnp.stack([(core == 0) & (part == 0), (core == 0) & (part == 1)])
        sum_l, sum_r, own, send = weights_call(
            core_ref, flags.astype(jnp.int32), n1, grads_l, grads_r, extra, qkv_l, qkv_r, wo_l, wo_r
        )
        tokens_grad, sums1 = norm1_back_call(
            mine, own, move(send, by_core), grad_hidden, gain1
        )
        tokens_grad = move(tokens_grad, by_role)

        def all_sum(mine_l, mine_r):
            value = mine_l + move(mine_r, by_part).astype(F32)
            for how, bit in zip(by_chip, bits):
                size = value.shape[0] // 2
                at = jnp.where(bit, size, 0)
                sent = lax.dynamic_slice_in_dim(value, size - at, size, axis=0).astype(BF16)
                kept = lax.dynamic_slice_in_dim(value, at, size, axis=0)
                value = kept + move(sent, how).astype(F32)
            value = value.astype(BF16)
            for how, bit in zip(by_chip[::-1], bits[::-1]):
                got = move(value, how)
                value = jnp.concatenate(
                    [jnp.where(bit, got, value), jnp.where(bit, value, got)], axis=0
                )
            other = move(value, by_core)
            return (
                jnp.where(core == 0, value, other).astype(F32),
                jnp.where(core == 0, other, value).astype(F32),
            )

        ff_0, ff_1 = all_sum(ff_l, ff_r)
        at_0, at_1 = all_sum(sum_l, sum_r)
        up_grad = jnp.concatenate([ff_0[:dim], ff_1[:dim]], axis=1)
        down_grad = jnp.concatenate([ff_0[dim:], ff_1[dim:]], axis=0)
        w_grads = []
        for i in range(3):
            piece = slice(i * width, (i + 1) * width)
            w_grads.append(jnp.concatenate([at_0[piece], at_1[piece]], axis=0).T)
        out_grad = jnp.concatenate([at_0[3 * width :], at_1[3 * width :]], axis=0)

        norms = jnp.concatenate([sums1[:2], sums2[:2], jnp.zeros((4, dim), F32)], axis=0)
        norms = norms + move(norms, by_core)
        norms = norms + move(norms, by_part)
        for how in by_chip:
            norms = norms + move(norms, how)
        return (
            mixed,
            tokens_grad,
            norms[0],
            norms[1],
            w_grads[0],
            w_grads[1],
            w_grads[2],
            out_grad,
            norms[2],
            norms[3],
            up_grad,
            down_grad,
        )

    return body


def solution(mesh):
    in_specs = (
        P(("dp", "tensor"), None),
        P("dp", None),
        P("dp", None),
        P(),
        P(),
        P(None, "tensor"),
        P(None, "tensor"),
        P(None, "tensor"),
        P("tensor", None),
        P(),
        P(),
        P(None, "tensor"),
        P("tensor", None),
        P(("dp", "tensor"), None),
    )
    out_specs = (
        P(("dp", "tensor"), None),
        P(("dp", "tensor"), None),
        P(),
        P(),
        P(None, "tensor"),
        P(None, "tensor"),
        P(None, "tensor"),
        P("tensor", None),
        P(),
        P(),
        P(None, "tensor"),
        P("tensor", None),
    )
    body = make_body(mesh.shape["dp"], mesh.shape["tensor"])
    return jax.shard_map(body, mesh=mesh, in_specs=in_specs, out_specs=out_specs, check_vma=False)
```

time: 888 us -> 413 us (0.47)
  the two profiles are of different devices: /device:TPU:1 before, /device:TPU:0 now
where the time goes in v1:
time: 413 us; the launch traced here: 409 us
  waiting for transfers between devices  136 us (33%)
  Pallas kernels  131 us (32%)
  starting transfers between devices  74 us (18%)
  local copies, waits for them, and re-layouts  34.9 us (8%)
  other arithmetic  31.1 us (8%)
    ppermute x40, waiting for transfers between devices, move(): return lax.ppermute(value, axes, how)  136 us
    ppermute x40, starting transfers between devices, move(): return lax.ppermute(value, axes, how)  74 us
    pallas_call x2, Pallas kernels, mlp_call(): pl.pallas_call(functools.partial(mlp_kernel, first, steps), grid=(steps,)...  35.8 us
    pallas_call x2, Pallas kernels, backward_call(): pl.pallas_call(functools.partial(backward_kernel, first, 256), grid=(head...  34.3 us
    pallas_call x2, Pallas kernels, forward_call(): pl.pallas_call(functools.partial(forward_kernel, FORWARD_BLOCK), grid=(he...  18.5 us
    unnamed x61, local copies, waits for them, and re-layouts  15.4 us
    pallas_call x1, Pallas kernels, weights_call(): pl.pallas_call(weights_kernel, in_specs=[SMEM, SMEM] + [pl.BlockSpec(memo...  9.98 us
  transfers between devices with their start and end apart: 40, of which 21 were waited for; matrix products, arithmetic and copies ran while one was open for 11% of the time, Pallas kernels for 27%

profile of v1, /device:TPU:0, one launch (start us, length us, event | category | flops | bytes accessed | tf_op | source)
XLA Modules:
  0.0 409.3 jit_solution(18184281412730239246)
XLA Ops:
  0.7 1.9 collective-permute-start
  3.8 1.6 constant_dynamic-slice_fusion.3
  6.7 2.2 copy.29
  8.9 3.2 collective-permute-start.4
  16.1 2.6 shard_map.229.n1_own
  20.9 4.6 %collective-permute-start.2 = (bf16[768,128]{1,0:T(8,128)(2,1)}, bf16[768,128]{1,0:T(8,128)(2,1)}, u32[]{:S(2)}, u32[]{:S(2)}) collective-permute-start(bf16[768,128]{1,0:T(8,128)(2,1)} %pad_maximum_fusion.10), channel_id=1, source_target_pairs={{0,1},{2,3},{4,5},{6,7},{8,9},{10,11},{12,13},{14,15},{16,17},{18,... | collective-permute-start | bytes 589832 | tf_op jit(solution)/shard_map/ppermute | solution.py:616
  26.7 2.0 collective-permute-start.8
  29.4 7.3 %collective-permute-done.2 = bf16[768,128]{1,0:T(8,128)(2,1)} collective-permute-done((bf16[768,128]{1,0:T(8,128)(2,1)}, bf16[768,128]{1,0:T(8,128)(2,1)}, u32[]{:S(2)}, u32[]{:S(2)}) %collective-permute-start.2) | collective-permute-done | bytes 196640 | tf_op jit(solution)/shard_map/ppermute | solution.py:616
  37.6 2.2 copy.30.weights.w_r
  39.8 6.3 %shard_map.230 = (bf16[1024,768]{1,0:T(8,128)(2,1)}, f32[1024,1024]{1,0:T(8,128)}, bf16[128,1024]{1,0:T(8,128)(2,1)}) custom-call(s32[1]{0:T(128)} %bitcast.core.refs_0_, bf16[512,768]{1,0:T(8,128)(2,1)} %shard_map.229.n1_own, bf16[512,768]{1,0:T(8,128)(2,1)} %collective-permute-done.1.n1_other, bf16[768,128]{1,0:T(8,128)(2,1)} %broadcast_select_fusion.10.wqk0, ...), custom_call_target="tpu_custom_call" | custom-call | flops 3000000000 | bytes 8000000 | tf_op jit(solution)/shard_map/pallas_call | solution.py:146
  46.1 9.3 %shard_map.231 = (bf16[576,1024]{1,0:T(8,128)(2,1)}, bf16[192,1024]{1,0:T(8,128)(2,1)}, f32[3,1,1024]{2,1,0:T(1,128)}) custom-call(bf16[1024,768]{1,0:T(8,128)(2,1)} %get-tuple-element.51.n1, bf16[768,576]{1,0:T(8,128)(2,1)} %pad_maximum_fusion.6.weights.w_l, f32[1024,1024]{1,0:T(8,128)} %get-tuple-element.52.penalty.refs_7_), custom_call_target="tpu_custom_call" | custom-call | flops 5000000000 | bytes 8000000 | tf_op jit(solution)/shard_map/pallas_call | solution.py:186
  55.4 9.3 %shard_map.232 = (bf16[576,1024]{1,0:T(8,128)(2,1)}, bf16[192,1024]{1,0:T(8,128)(2,1)}, f32[3,1,1024]{2,1,0:T(1,128)}) custom-call(bf16[1024,768]{1,0:T(8,128)(2,1)} %get-tuple-element.51.n1, bf16[768,576]{1,0:T(8,128)(2,1)} %copy.30.weights.w_r, f32[1024,1024]{1,0:T(8,128)} %get-tuple-element.52.penalty.refs_7_), custom_call_target="tpu_custom_call" | custom-call | flops 5000000000 | bytes 8000000 | tf_op jit(solution)/shard_map/pallas_call | solution.py:186
  64.7 3.5 shard_map.233
  68.1 2.7 collective-permute-start.6
  73.1 3.5 shard_map.234
  77.1 3.5 collective-permute-start.10
  80.7 1.6 collective-permute-start.11
  82.3 17.9 %shard_map.235 = (f32[512,768]{1,0:T(8,128)}, f32[512,768]{1,0:T(8,128)}, f32[512,768]{1,0:T(8,128)}, f32[512,768]{1,0:T(8,128)}, f32[1536,768]{1,0:T(8,128)}) custom-call(bf16[512,768]{1,0:T(8,128)(2,1)} %collective-permute-done.7.refs_0_, bf16[512,768]{1,0:T(8,128)(2,1)} %get-tuple-element.58.refs_1_, bf16[512,768]{1,0:T(8,128)(2,1)} %collective-permute-done.9.refs_2_, ...), custom_call_target="tpu_custom_call" | custom-call | flops 7200000000 | bytes 18000000 | tf_op jit(solution)/shard_map/pallas_call | solution.py:314
  100.2 7.1 %collective-permute-done.10.refs_4_ = bf16[768,768]{1,0:T(8,128)(2,1)S(1)} collective-permute-done((bf16[768,768]{1,0:T(8,128)(2,1)S(1)}, bf16[768,768]{1,0:T(8,128)(2,1)S(1)}, u32[]{:S(2)}, u32[]{:S(2)}) %collective-permute-start.10) | collective-permute-done | bytes 1179680 | tf_op jit(solution)/shard_map/ppermute | solution.py:616
  107.3 24.8 %collective-permute-done.11.refs_5_ = bf16[768,768]{1,0:T(8,128)(2,1)S(1)} collective-permute-done((bf16[768,768]{1,0:T(8,128)(2,1)S(1)}, bf16[768,768]{1,0:T(8,128)(2,1)S(1)}, u32[]{:S(2)}, u32[]{:S(2)}) %collective-permute-start.11) | collective-permute-done | bytes 1179680 | tf_op jit(solution)/shard_map/ppermute | solution.py:616
  133.1 18.0 %shard_map.236 = (bf16[512,768]{1,0:T(8,128)(2,1)}, f32[512,768]{1,0:T(8,128)}, bf16[512,768]{1,0:T(8,128)(2,1)}, f32[512,768]{1,0:T(8,128)}, bf16[1536,768]{1,0:T(8,128)(2,1)}) custom-call(bf16[512,768]{1,0:T(8,128)(2,1)} %collective-permute-done.7.refs_0_, bf16[512,768]{1,0:T(8,128)(2,1)} %get-tuple-element.58.refs_1_, ...), custom_call_target="tpu_custom_call" | custom-call | flops 7200000000 | bytes 18000000 | tf_op jit(solution)/shard_map/pallas_call | solution.py:314
  151.2 2.5 collective-permute-done.14.received
  154.5 4.9 %shard_map.237 = (f32[512,768]{1,0:T(8,128)}, bf16[512,768]{1,0:T(8,128)(2,1)}, f32[8,768]{1,0:T(8,128)}) custom-call(f32[512,768]{1,0:T(8,128)} %get-tuple-element.57.hidden, f32[512,768]{1,0:T(8,128)} %get-tuple-element.65.own, bf16[512,768]{1,0:T(8,128)(2,1)} %copy-done.12, bf16[512,768]{1,0:T(8,128)(2,1)} %copy-done.11, f32[1,768]{1,0:T(1,128)} %broadcast_in_dim.18.gain), custom_call_target="tpu_custom_call" | custom-call | bytes 7077888 | tf_op jit(solution)/shard_map/pallas_call | solution.py:344
  159.6 1.7 collective-permute-start.32
  162.9 15.7 %shard_map.238 = (bf16[576,1024]{1,0:T(8,128)(2,1)}, f32[192,768]{1,0:T(8,128)}, f32[1024,1024]{1,0:T(8,128)}) custom-call(s32[1]{0:T(128)} %bitcast.core.refs_0_, bf16[512,768]{1,0:T(8,128)(2,1)} %get-tuple-element.67.refs_1_, bf16[512,768]{1,0:T(8,128)(2,1)} %copy-done.27, bf16[192,768]{1,0:T(8,128)(2,1)} %collective-permute-done.5.w_r.refs_3_, ...), custom_call_target="tpu_custom_call" | custom-call | flops 10000000000 | bytes 16000000 | tf_op jit(solution)/shard_map/pallas_call | solution.py:459
  178.5 18.7 %shard_map.239 = (bf16[576,1024]{1,0:T(8,128)(2,1)}, f32[192,768]{1,0:T(8,128)}, f32[1024,1024]{1,0:T(8,128)}, bf16[1024,1024]{1,0:T(8,128)(2,1)}) custom-call(s32[1]{0:T(128)} %bitcast.core.refs_0_, bf16[512,768]{1,0:T(8,128)(2,1)} %get-tuple-element.67.refs_1_, bf16[512,768]{1,0:T(8,128)(2,1)} %copy-done.27, ...), custom_call_target="tpu_custom_call" | custom-call | flops 10000000000 | bytes 16000000 | tf_op jit(solution)/shard_map/pallas_call | solution.py:459
  199.1 14.2 %collective-permute-done.32 = bf16[1536,768]{1,0:T(8,128)(2,1)S(1)} collective-permute-done((bf16[1536,768]{1,0:T(8,128)(2,1)}, bf16[1536,768]{1,0:T(8,128)(2,1)S(1)}, u32[]{:S(2)}, u32[]{:S(2)}) %collective-permute-start.32) | collective-permute-done | bytes 2359328 | tf_op jit(solution)/shard_map/ppermute | solution.py:616
  213.4 2.8 convert_add_fusion
  216.2 2.2 copy-done.2
  218.4 1.6 collective-permute-start.33
  220.0 7.5 %shard_map.240.extra = f32[128,1024]{1,0:T(8,128)} custom-call(f32[1024,1024]{1,0:T(8,128)} %get-tuple-element.75.own, bf16[1024,1024]{1,0:T(8,128)(2,1)} %collective-permute-done.16.received, bf16[128,1024]{1,0:T(8,128)(2,1)} %get-tuple-element.77.qk0, f32[8,1024]{1,0:T(8,128)} %concatenate.53.seg_pad), custom_call_target="tpu_custom_call" | custom-call | flops 4000000000 | bytes 8000000 | tf_op jit(solution)/shard_map/pallas_call | solution.py:511
  227.5 10.0 %shard_map.241 = (f32[768,768]{1,0:T(8,128)}, bf16[768,768]{1,0:T(8,128)(2,1)}, f32[512,768]{1,0:T(8,128)}, bf16[512,768]{1,0:T(8,128)(2,1)}) custom-call(s32[1]{0:T(128)} %bitcast.core.refs_0_, s32[2]{0:T(128)} %add_convert_fusion.3.flags, bf16[1024,768]{1,0:T(8,128)(2,1)} %get-tuple-element.51.n1, bf16[576,1024]{1,0:T(8,128)(2,1)} %get-tuple-element.73.grads_l, ...), custom_call_target="tpu_custom_call" | custom-call | flops 4000000000 | bytes 16000000 | tf_op jit(solution)/shard_map/pallas_call | solution.py:556
  237.5 1.7 collective-permute-start.24
  239.3 2.0 convert_add_fusion.1
  241.4 1.6 collective-permute-start.34
  243.0 22.0 %collective-permute-done.24 = bf16[768,768]{1,0:T(8,128)(2,1)} collective-permute-done((bf16[768,768]{1,0:T(8,128)(2,1)}, bf16[768,768]{1,0:T(8,128)(2,1)}, u32[]{:S(2)}, u32[]{:S(2)}) %collective-permute-start.24) | collective-permute-done | bytes 1179680 | tf_op jit(solution)/shard_map/ppermute | solution.py:616
  265.1 1.6 convert_add_fusion.2
  269.0 1.5 collective-permute-start.25
  271.9 2.7 collective-permute-start.35
  274.5 7.3 %collective-permute-done.25 = bf16[384,768]{1,0:T(8,128)(2,1)} collective-permute-done((bf16[384,768]{1,0:T(8,128)(2,1)}, bf16[384,768]{1,0:T(8,128)(2,1)}, u32[]{:S(2)}, u32[]{:S(2)}) %collective-permute-start.25) | collective-permute-done | bytes 589856 | tf_op jit(solution)/shard_map/ppermute | solution.py:616
  284.1 2.7 collective-permute-start.36
  286.8 8.4 %collective-permute-done.26 = bf16[192,768]{1,0:T(8,128)(2,1)} collective-permute-done((bf16[192,768]{1,0:T(8,128)(2,1)S(1)}, bf16[192,768]{1,0:T(8,128)(2,1)}, u32[]{:S(2)}, u32[]{:S(2)}) %collective-permute-start.26) | collective-permute-done | bytes 294944 | tf_op jit(solution)/shard_map/ppermute | solution.py:616
  296.4 6.8 %collective-permute-done.36 = bf16[192,768]{1,0:T(8,128)(2,1)S(1)} collective-permute-done((bf16[192,768]{1,0:T(8,128)(2,1)S(1)}, bf16[192,768]{1,0:T(8,128)(2,1)S(1)}, u32[]{:S(2)}, u32[]{:S(2)}) %collective-permute-start.36) | collective-permute-done | bytes 294944 | tf_op jit(solution)/shard_map/ppermute | solution.py:616
  305.0 6.3 %collective-permute-start.12 = (bf16[512,768]{1,0:T(8,128)(2,1)S(1)}, bf16[512,768]{1,0:T(8,128)(2,1)S(1)}, u32[]{:S(2)}, u32[]{:S(2)}) collective-permute-start(bf16[512,768]{1,0:T(8,128)(2,1)S(1)} %copy-done.25), channel_id=1, source_target_pairs={{0,2},{1,3},{2,0},{3,1},{4,6},{5,7},{6,4},{7,5},{8,10},{9,11},{10,... | collective-permute-start | bytes 2359304 | tf_op jit(solution)/shard_map/ppermute | solution.py:616
  311.2 6.0 %collective-permute-done.28 = bf16[96,768]{1,0:T(8,128)(2,1)S(1)} collective-permute-done((bf16[96,768]{1,0:T(8,128)(2,1)S(1)}, bf16[96,768]{1,0:T(8,128)(2,1)S(1)}, u32[]{:S(2)}, u32[]{:S(2)}) %collective-permute-start.28) | collective-permute-done | bytes 147488 | tf_op jit(solution)/shard_map/ppermute | solution.py:616
  317.7 11.6 %collective-permute-start.38 = (bf16[768,768]{1,0:T(8,128)(2,1)S(1)}, bf16[768,768]{1,0:T(8,128)(2,1)S(1)}, u32[]{:S(2)}, u32[]{:S(2)}) collective-permute-start(bf16[768,768]{1,0:T(8,128)(2,1)S(1)} %pad_maximum_fusion.5), channel_id=1, source_target_pairs={{0,4},{1,5},{2,10},{3,11},{4,0},{5,1},{6,14},{7,15},{8,12},{9,13},... | collective-permute-start | bytes 3538952 | tf_op jit(solution)/shard_map/ppermute | solution.py:616
  329.3 2.1 collective-permute-done.29
  331.6 3.9 collective-permute-start.30
  336.7 7.4 %collective-permute-start.13 = (bf16[512,768]{1,0:T(8,128)(2,1)}, bf16[512,768]{1,0:T(8,128)(2,1)}, u32[]{:S(2)}, u32[]{:S(2)}) collective-permute-start(bf16[512,768]{1,0:T(8,128)(2,1)} %add_convert_fusion), channel_id=1, source_target_pairs={{0,0},{1,2},{2,1},{3,3},{4,4},{5,6},{6,5},{7,7},{8,8},{9,10},{10,9... | collective-permute-start | bytes 2359304 | tf_op jit(solution)/shard_map/ppermute | solution.py:616
  344.2 5.6 %collective-permute-done.30 = bf16[384,768]{1,0:T(8,128)(2,1)S(1)} collective-permute-done((bf16[384,768]{1,0:T(8,128)(2,1)S(1)}, bf16[384,768]{1,0:T(8,128)(2,1)S(1)}, u32[]{:S(2)}, u32[]{:S(2)}) %collective-permute-start.30) | collective-permute-done | bytes 589856 | tf_op jit(solution)/shard_map/ppermute | solution.py:616
  350.7 1.6 pad_maximum_fusion.2
  352.7 4.4 %shard_map.242 = (bf16[512,768]{1,0:T(8,128)(2,1)}, f32[8,768]{1,0:T(8,128)}) custom-call(bf16[512,768]{1,0:T(8,128)(2,1)} %copy-done.5, f32[512,768]{1,0:T(8,128)} %get-tuple-element.80.own, bf16[512,768]{1,0:T(8,128)(2,1)} %collective-permute-done.17.received, f32[512,768]{1,0:T(8,128)} %get-tuple-element.82.grad_hidden, f32[1,768]{1,0:T(1,128)} %broadcast_in_dim.16.gain), custom_call_target="tpu_custom_call" | custom-call | bytes 5505024 | tf_op jit(solution)/shard_map/pallas_call | solution.py:582
  357.2 2.0 collective-permute-start.18
  360.8 2.0 collective-permute-start.19
  364.0 7.5 %collective-permute-done.20 = f32[8,768]{1,0:T(8,128)S(1)} collective-permute-done((f32[8,768]{1,0:T(8,128)S(1)}, f32[8,768]{1,0:T(8,128)S(1)}, u32[]{:S(2)}, u32[]{:S(2)}) %collective-permute-start.20) | collective-permute-done | bytes 24608 | tf_op jit(solution)/shard_map/ppermute | solution.py:616
  371.5 2.0 collective-permute-start.21
  373.5 1.8 collective-permute-done.21
  375.4 3.8 collective-permute-done.22
  379.2 4.7 %collective-permute-done.23 = f32[8,768]{1,0:T(8,128)S(1)} collective-permute-done((f32[8,768]{1,0:T(8,128)S(1)}, f32[8,768]{1,0:T(8,128)S(1)}, u32[]{:S(2)}, u32[]{:S(2)}) %collective-permute-start.23) | collective-permute-done | bytes 24608 | tf_op jit(solution)/shard_map/ppermute | solution.py:616
  395.2 2.3 pad_maximum_fusion.4
  397.5 2.4 select_convert_fusion.1
  400.5 2.9 pad_maximum_fusion
  403.4 2.5 pad_maximum_fusion.1
  405.9 2.2 copy.37
  (161 shorter events, 47.4 us)
Async XLA Ops:
  0.6 76.4 %copy-start = (bf16[768,1536]{1,0:T(8,128)(2,1)S(1)}, bf16[768,1536]{1,0:T(8,128)(2,1)}, u32[]{:S(2)}) copy-start(bf16[768,1536]{1,0:T(8,128)(2,1)} %param.25) | copy-start | bytes 7077892
  0.7 14.5 %collective-permute-start = (bf16[512,768]{1,0:T(8,128)(2,1)}, bf16[512,768]{1,0:T(8,128)(2,1)S(1)}, u32[]{:S(2)}, u32[]{:S(2)}) collective-permute-start(bf16[512,768]{1,0:T(8,128)(2,1)} %param.14), channel_id=1, source_target_pairs={{0,0},{1,2},{2,1},{3,3},{4,4},{5,6},{6,5},{7,7},{8,8},{9,10},{10,9... | collective-permute-start | bytes 2359304 | tf_op jit(solution)/shard_map/ppermute | solution.py:616
  6.7 7.3 %copy-start.19 = (f32[768]{0:T(1024)S(1)}, f32[768]{0:T(1024)}, u32[]{:S(2)}) copy-start(f32[768]{0:T(1024)} %param.17) | copy-start | bytes 9220
  6.7 7.9 %copy-start.20 = (f32[768]{0:T(1024)S(1)}, f32[768]{0:T(1024)}, u32[]{:S(2)}) copy-start(f32[768]{0:T(1024)} %param.18) | copy-start | bytes 9220
  8.9 16.5 %copy-start.17 = (s32[1,1024]{1,0:T(1,128)S(1)}, s32[1,1024]{1,0:T(1,128)}, u32[]{:S(2)}) copy-start(s32[1,1024]{1,0:T(1,128)} %param.16) | copy-start | bytes 12292
  8.9 16.5 %copy-start.18 = (s32[1,1024]{1,0:T(1,128)S(1)}, s32[1,1024]{1,0:T(1,128)}, u32[]{:S(2)}) copy-start(s32[1,1024]{1,0:T(1,128)} %param.15) | copy-start | bytes 12292
  8.9 16.8 %copy-start.16 = (bf16[384,768]{1,0:T(8,128)(2,1)S(1)}, bf16[384,768]{1,0:T(8,128)(2,1)}, u32[]{:S(2)}) copy-start(bf16[384,768]{1,0:T(8,128)(2,1)} %param.22) | copy-start | bytes 1769476
  8.9 28.7 %collective-permute-start.4 = (bf16[768,576]{0,1:T(8,128)(2,1)}, bf16[768,576]{0,1:T(8,128)(2,1)}, u32[]{:S(2)}, u32[]{:S(2)}) collective-permute-start(bf16[768,576]{0,1:T(8,128)(2,1)} %copy.29), channel_id=1, source_target_pairs={{0,1},{1,0},{2,3},{3,2},{4,5},{5,4},{6,7},{7,6},{8,9},{9,8},{10,11... | collective-permute-start | bytes 2654216 | tf_op jit(solution)/shard_map/ppermute | solution.py:616
  18.7 21.2 %collective-permute-start.1 = (bf16[512,768]{1,0:T(8,128)(2,1)}, bf16[512,768]{1,0:T(8,128)(2,1)}, u32[]{:S(2)}, u32[]{:S(2)}) collective-permute-start(bf16[512,768]{1,0:T(8,128)(2,1)} %shard_map.229.n1_own), channel_id=1, source_target_pairs={{0,2},{1,3},{2,0},{3,1},{4,6},{5,7},{6,4},{7,5},{8,10},{9,11},{10,... | collective-permute-start | bytes 2359304 | tf_op jit(solution)/shard_map/ppermute | solution.py:616
  20.9 15.9 %collective-permute-start.2 = (bf16[768,128]{1,0:T(8,128)(2,1)}, bf16[768,128]{1,0:T(8,128)(2,1)}, u32[]{:S(2)}, u32[]{:S(2)}) collective-permute-start(bf16[768,128]{1,0:T(8,128)(2,1)} %pad_maximum_fusion.10), channel_id=1, source_target_pairs={{0,1},{2,3},{4,5},{6,7},{8,9},{10,11},{12,13},{14,15},{16,17},{18,... | collective-permute-start | bytes 589832 | tf_op jit(solution)/shard_map/ppermute | solution.py:616
  25.5 1.2 collective-permute-start.3
  26.5 38.1 %collective-permute-start.5 = (bf16[192,768]{1,0:T(8,128)(2,1)}, bf16[192,768]{1,0:T(8,128)(2,1)}, u32[]{:S(2)}, u32[]{:S(2)}) collective-permute-start(bf16[192,768]{1,0:T(8,128)(2,1)} %constant_dynamic-slice_fusion.2.w_l.refs_3_), channel_id=1, source_target_pairs={{0,1},{1,0},{2,3},{3,2},{4,5},{5,4},{6,7},{7,6},{8,9},{9,8},{10,11... | collective-permute-start | bytes 884744 | tf_op jit(solution)/shard_map/ppermute | solution.py:616
  26.7 45.3 %collective-permute-start.8 = (bf16[512,768]{1,0:T(8,128)(2,1)}, bf16[512,768]{1,0:T(8,128)(2,1)S(1)}, u32[]{:S(2)}, u32[]{:S(2)}) collective-permute-start(bf16[512,768]{1,0:T(8,128)(2,1)} %param.27), channel_id=1, source_target_pairs={{0,0},{1,2},{2,1},{3,3},{4,4},{5,6},{6,5},{7,7},{8,8},{9,10},{10,9... | collective-permute-start | bytes 2359304 | tf_op jit(solution)/shard_map/ppermute | solution.py:616
  64.6 6.2 %copy-start.21 = (f32[768]{0:T(1024)S(1)}, f32[768]{0:T(1024)}, u32[]{:S(2)}) copy-start(f32[768]{0:T(1024)} %param.23) | copy-start | bytes 9220
  64.6 6.8 %copy-start.22 = (f32[768]{0:T(1024)S(1)}, f32[768]{0:T(1024)}, u32[]{:S(2)}) copy-start(f32[768]{0:T(1024)} %param.24) | copy-start | bytes 9220
  68.1 5.0 %collective-permute-start.6 = (bf16[512,768]{1,0:T(8,128)(2,1)}, bf16[512,768]{1,0:T(8,128)(2,1)}, u32[]{:S(2)}, u32[]{:S(2)}) collective-permute-start(bf16[512,768]{1,0:T(8,128)(2,1)} %get-tuple-element.56), channel_id=1, source_target_pairs={{0,2},{1,3},{2,0},{3,1},{4,6},{5,7},{6,4},{7,5},{8,10},{9,11},{10,... | collective-permute-start | bytes 2359304 | tf_op jit(solution)/shard_map/ppermute | solution.py:616
  72.0 4.6 %copy-start.11 = (bf16[512,768]{1,0:T(8,128)(2,1)}, bf16[512,768]{1,0:T(8,128)(2,1)S(1)}, u32[]{:S(2)}) copy-start(bf16[512,768]{1,0:T(8,128)(2,1)S(1)} %collective-permute-done.8.refs_3_.grad) | copy-start | bytes 2359300
  72.0 10.3 %collective-permute-start.9 = (bf16[512,768]{1,0:T(8,128)(2,1)S(1)}, bf16[512,768]{1,0:T(8,128)(2,1)}, u32[]{:S(2)}, u32[]{:S(2)}) collective-permute-start(bf16[512,768]{1,0:T(8,128)(2,1)S(1)} %collective-permute-done.8.refs_3_.grad), channel_id=1, source_target_pairs={{0,2},{1,3},{2,0},{3,1},{4,6},{5,7},{6,4},{7,5},{8,10},{9,11},{10,... | collective-permute-start | bytes 2359304 | tf_op jit(solution)/shard_map/ppermute | solution.py:616
  76.6 3.9 copy-start.15
  76.6 5.7 %collective-permute-start.7 = (bf16[512,768]{1,0:T(8,128)(2,1)}, bf16[512,768]{1,0:T(8,128)(2,1)}, u32[]{:S(2)}, u32[]{:S(2)}) collective-permute-start(bf16[512,768]{1,0:T(8,128)(2,1)} %get-tuple-element.58.refs_1_), channel_id=1, source_target_pairs={{0,2},{1,3},{2,0},{3,1},{4,6},{5,7},{6,4},{7,5},{8,10},{9,11},{10,... | collective-permute-start | bytes 2359304 | tf_op jit(solution)/shard_map/ppermute | solution.py:616
  77.1 5.2 %copy-start.9 = (bf16[768,768]{1,0:T(8,128)(2,1)}, bf16[768,768]{1,0:T(8,128)(2,1)S(1)}, u32[]{:S(2)}) copy-start(bf16[768,768]{1,0:T(8,128)(2,1)S(1)} %constant_dynamic-slice_fusion.1.refs_4_) | copy-start | bytes 3538948
  77.1 30.2 %collective-permute-start.10 = (bf16[768,768]{1,0:T(8,128)(2,1)S(1)}, bf16[768,768]{1,0:T(8,128)(2,1)S(1)}, u32[]{:S(2)}, u32[]{:S(2)}) collective-permute-start(bf16[768,768]{1,0:T(8,128)(2,1)S(1)} %constant_dynamic-slice_fusion.1.refs_4_), channel_id=1, source_target_pairs={{0,1},{1,0},{2,3},{3,2},{4,5},{5,4},{6,7},{7,6},{8,9},{9,8},{10,11... | collective-permute-start | bytes 3538952 | tf_op jit(solution)/shard_map/ppermute | solution.py:616
  80.7 1.7 copy-start.10
  80.7 51.5 %collective-permute-start.11 = (bf16[768,768]{1,0:T(8,128)(2,1)S(1)}, bf16[768,768]{1,0:T(8,128)(2,1)S(1)}, u32[]{:S(2)}, u32[]{:S(2)}) collective-permute-start(bf16[768,768]{1,0:T(8,128)(2,1)S(1)} %constant_dynamic-slice_fusion.refs_5_), channel_id=1, source_target_pairs={{0,1},{1,0},{2,3},{3,2},{4,5},{5,4},{6,7},{7,6},{8,9},{9,8},{10,11... | collective-permute-start | bytes 3538952 | tf_op jit(solution)/shard_map/ppermute | solution.py:616
  107.3 24.8 %copy-start.23 = (bf16[768,768]{1,0:T(8,128)(2,1)}, bf16[768,768]{1,0:T(8,128)(2,1)S(1)}, u32[]{:S(2)}) copy-start(bf16[768,768]{1,0:T(8,128)(2,1)S(1)} %collective-permute-done.10.refs_4_) | copy-start | bytes 3538948
  132.1 1.0 copy-start.24
  151.1 2.6 collective-permute-start.14
  159.5 2.5 collective-permute-start.15
  159.6 53.7 %collective-permute-start.32 = (bf16[1536,768]{1,0:T(8,128)(2,1)}, bf16[1536,768]{1,0:T(8,128)(2,1)S(1)}, u32[]{:S(2)}, u32[]{:S(2)}) collective-permute-start(bf16[1536,768]{1,0:T(8,128)(2,1)} %get-tuple-element.89), channel_id=1, source_target_pairs={{0,1},{1,0},{2,3},{3,2},{4,5},{5,4},{6,7},{7,6},{8,9},{9,8},{10,11... | collective-permute-start | bytes 7077896 | tf_op jit(solution)/shard_map/ppermute | solution.py:616
  197.2 22.8 %collective-permute-start.16 = (bf16[1024,1024]{1,0:T(8,128)(2,1)}, bf16[1024,1024]{1,0:T(8,128)(2,1)}, u32[]{:S(2)}, u32[]{:S(2)}) collective-permute-start(bf16[1024,1024]{1,0:T(8,128)(2,1)} %get-tuple-element.76), channel_id=1, source_target_pairs={{2,0},{3,1},{6,4},{7,5},{10,8},{11,9},{14,12},{15,13},{18,16},{19,... | collective-permute-start | bytes 6291464 | tf_op jit(solution)/shard_map/ppermute | solution.py:616
  216.1 2.2 copy-start.2
  218.4 20.8 %collective-permute-start.33 = (bf16[768,768]{1,0:T(8,128)(2,1)S(1)}, bf16[768,768]{1,0:T(8,128)(2,1)S(1)}, u32[]{:S(2)}, u32[]{:S(2)}) collective-permute-start(bf16[768,768]{1,0:T(8,128)(2,1)S(1)} %dynamic-slice_convert_fusion), channel_id=1, source_target_pairs={{0,4},{1,5},{2,10},{3,11},{4,0},{5,1},{6,14},{7,15},{8,12},{9,13},... | collective-permute-start | bytes 3538952 | tf_op jit(solution)/shard_map/ppermute | solution.py:616
  237.5 27.5 %collective-permute-start.24 = (bf16[768,768]{1,0:T(8,128)(2,1)}, bf16[768,768]{1,0:T(8,128)(2,1)}, u32[]{:S(2)}, u32[]{:S(2)}) collective-permute-start(bf16[768,768]{1,0:T(8,128)(2,1)} %get-tuple-element.87), channel_id=1, source_target_pairs={{0,1},{1,0},{2,3},{3,2},{4,5},{5,4},{6,7},{7,6},{8,9},{9,8},{10,11... | collective-permute-start | bytes 3538952 | tf_op jit(solution)/shard_map/ppermute | solution.py:616
  239.3 25.8 %copy-start.7 = (f32[768,768]{1,0:T(8,128)S(1)}, f32[768,768]{1,0:T(8,128)}, u32[]{:S(2)}) copy-start(f32[768,768]{1,0:T(8,128)} %get-tuple-element.86) | copy-start | bytes 7077892
  241.4 29.1 %collective-permute-start.34 = (bf16[384,768]{1,0:T(8,128)(2,1)S(1)}, bf16[384,768]{1,0:T(8,128)(2,1)}, u32[]{:S(2)}, u32[]{:S(2)}) collective-permute-start(bf16[384,768]{1,0:T(8,128)(2,1)S(1)} %dynamic-slice_convert_fusion.1), channel_id=1, source_target_pairs={{0,8},{1,9},{2,18},{3,19},{4,12},{5,13},{6,22},{7,23},{8,0},{9,1},... | collective-permute-start | bytes 1769480 | tf_op jit(solution)/shard_map/ppermute | solution.py:616
  266.7 1.4 copy-start.3
  269.0 12.9 %collective-permute-start.25 = (bf16[384,768]{1,0:T(8,128)(2,1)}, bf16[384,768]{1,0:T(8,128)(2,1)}, u32[]{:S(2)}, u32[]{:S(2)}) collective-permute-start(bf16[384,768]{1,0:T(8,128)(2,1)} %dynamic-slice_convert_fusion.2), channel_id=1, source_target_pairs={{0,4},{1,5},{2,10},{3,11},{4,0},{5,1},{6,14},{7,15},{8,12},{9,13},... | collective-permute-start | bytes 1769480 | tf_op jit(solution)/shard_map/ppermute | solution.py:616
  270.5 11.4 %copy-start.4 = (f32[768,768]{1,0:T(8,128)S(1)}, f32[768,768]{1,0:T(8,128)}, u32[]{:S(2)}) copy-start(f32[768,768]{1,0:T(8,128)} %copy-done.3) | copy-start | bytes 7077892
  271.9 12.2 %collective-permute-start.35 = (bf16[192,768]{1,0:T(8,128)(2,1)S(1)}, bf16[192,768]{1,0:T(8,128)(2,1)S(1)}, u32[]{:S(2)}, u32[]{:S(2)}) collective-permute-start(bf16[192,768]{1,0:T(8,128)(2,1)S(1)} %dynamic-slice_convert_fusion.3), channel_id=1, source_target_pairs={{0,16},{1,17},{2,6},{3,7},{4,20},{5,21},{6,2},{7,3},{8,24},{9,25},... | collective-permute-start | bytes 884744 | tf_op jit(solution)/shard_map/ppermute | solution.py:616
  283.1 12.1 %collective-permute-start.26 = (bf16[192,768]{1,0:T(8,128)(2,1)S(1)}, bf16[192,768]{1,0:T(8,128)(2,1)}, u32[]{:S(2)}, u32[]{:S(2)}) collective-permute-start(bf16[192,768]{1,0:T(8,128)(2,1)S(1)} %dynamic-slice_convert_fusion.4), channel_id=1, source_target_pairs={{0,8},{1,9},{2,18},{3,19},{4,12},{5,13},{6,22},{7,23},{8,0},{9,1},... | collective-permute-start | bytes 884744 | tf_op jit(solution)/shard_map/ppermute | solution.py:616
  284.1 19.1 %collective-permute-start.36 = (bf16[192,768]{1,0:T(8,128)(2,1)S(1)}, bf16[192,768]{1,0:T(8,128)(2,1)S(1)}, u32[]{:S(2)}, u32[]{:S(2)}) collective-permute-start(bf16[192,768]{1,0:T(8,128)(2,1)S(1)} %add_convert_fusion.1), channel_id=1, source_target_pairs={{0,16},{1,17},{2,6},{3,7},{4,20},{5,21},{6,2},{7,3},{8,24},{9,25},... | collective-permute-start | bytes 884744 | tf_op jit(solution)/shard_map/ppermute | solution.py:616
  296.2 8.7 %copy-start.25 = (bf16[512,768]{1,0:T(8,128)(2,1)S(1)}, bf16[512,768]{1,0:T(8,128)(2,1)}, u32[]{:S(2)}) copy-start(bf16[512,768]{1,0:T(8,128)(2,1)} %get-tuple-element.64) | copy-start | bytes 2359300
  296.3 8.6 %collective-permute-start.27 = (bf16[96,768]{1,0:T(8,128)(2,1)S(1)}, bf16[96,768]{1,0:T(8,128)(2,1)S(1)}, u32[]{:S(2)}, u32[]{:S(2)}) collective-permute-start(bf16[96,768]{1,0:T(8,128)(2,1)S(1)} %dynamic-slice_convert_fusion.5), channel_id=1, source_target_pairs={{0,16},{1,17},{2,6},{3,7},{4,20},{5,21},{6,2},{7,3},{8,24},{9,25},... | collective-permute-start | bytes 442376 | tf_op jit(solution)/shard_map/ppermute | solution.py:616
  303.3 14.1 %collective-permute-start.37 = (bf16[384,768]{1,0:T(8,128)(2,1)S(1)}, bf16[384,768]{1,0:T(8,128)(2,1)S(1)}, u32[]{:S(2)}, u32[]{:S(2)}) collective-permute-start(bf16[384,768]{1,0:T(8,128)(2,1)S(1)} %pad_maximum_fusion.8), channel_id=1, source_target_pairs={{0,8},{1,9},{2,18},{3,19},{4,12},{5,13},{6,22},{7,23},{8,0},{9,1},... | collective-permute-start | bytes 1769480 | tf_op jit(solution)/shard_map/ppermute | solution.py:616
  304.9 12.4 %collective-permute-start.28 = (bf16[96,768]{1,0:T(8,128)(2,1)S(1)}, bf16[96,768]{1,0:T(8,128)(2,1)S(1)}, u32[]{:S(2)}, u32[]{:S(2)}) collective-permute-start(bf16[96,768]{1,0:T(8,128)(2,1)S(1)} %add_convert_fusion.2), channel_id=1, source_target_pairs={{0,16},{1,17},{2,6},{3,7},{4,20},{5,21},{6,2},{7,3},{8,24},{9,25},... | collective-permute-start | bytes 442376 | tf_op jit(solution)/shard_map/ppermute | solution.py:616
  305.0 30.5 %collective-permute-start.12 = (bf16[512,768]{1,0:T(8,128)(2,1)S(1)}, bf16[512,768]{1,0:T(8,128)(2,1)S(1)}, u32[]{:S(2)}, u32[]{:S(2)}) collective-permute-start(bf16[512,768]{1,0:T(8,128)(2,1)S(1)} %copy-done.25), channel_id=1, source_target_pairs={{0,2},{1,3},{2,0},{3,1},{4,6},{5,7},{6,4},{7,5},{8,10},{9,11},{10,... | collective-permute-start | bytes 2359304 | tf_op jit(solution)/shard_map/ppermute | solution.py:616
  317.3 14.1 %collective-permute-start.29 = (bf16[192,768]{1,0:T(8,128)(2,1)S(1)}, bf16[192,768]{1,0:T(8,128)(2,1)S(1)}, u32[]{:S(2)}, u32[]{:S(2)}) collective-permute-start(bf16[192,768]{1,0:T(8,128)(2,1)S(1)} %pad_maximum_fusion.9), channel_id=1, source_target_pairs={{0,8},{1,9},{2,18},{3,19},{4,12},{5,13},{6,22},{7,23},{8,0},{9,1},... | collective-permute-start | bytes 884744 | tf_op jit(solution)/shard_map/ppermute | solution.py:616
  317.6 17.8 %copy-start.8 = (f32[512,768]{1,0:T(8,128)S(1)}, f32[512,768]{1,0:T(8,128)}, u32[]{:S(2)}) copy-start(f32[512,768]{1,0:T(8,128)} %get-tuple-element.63) | copy-start | bytes 4718596
  317.7 17.8 %copy-start.6 = (f32[512,768]{1,0:T(8,128)S(1)}, f32[512,768]{1,0:T(8,128)}, u32[]{:S(2)}) copy-start(f32[512,768]{1,0:T(8,128)} %get-tuple-element.57.hidden) | copy-start | bytes 4718596
  317.7 32.5 %collective-permute-start.38 = (bf16[768,768]{1,0:T(8,128)(2,1)S(1)}, bf16[768,768]{1,0:T(8,128)(2,1)S(1)}, u32[]{:S(2)}, u32[]{:S(2)}) collective-permute-start(bf16[768,768]{1,0:T(8,128)(2,1)S(1)} %pad_maximum_fusion.5), channel_id=1, source_target_pairs={{0,4},{1,5},{2,10},{3,11},{4,0},{5,1},{6,14},{7,15},{8,12},{9,13},... | collective-permute-start | bytes 3538952 | tf_op jit(solution)/shard_map/ppermute | solution.py:616
  331.6 18.2 %collective-permute-start.30 = (bf16[384,768]{1,0:T(8,128)(2,1)S(1)}, bf16[384,768]{1,0:T(8,128)(2,1)S(1)}, u32[]{:S(2)}, u32[]{:S(2)}) collective-permute-start(bf16[384,768]{1,0:T(8,128)(2,1)S(1)} %pad_maximum_fusion.7), channel_id=1, source_target_pairs={{0,4},{1,5},{2,10},{3,11},{4,0},{5,1},{6,14},{7,15},{8,12},{9,13},... | collective-permute-start | bytes 1769480 | tf_op jit(solution)/shard_map/ppermute | solution.py:616
  335.5 8.7 %copy-start.26 = (bf16[512,768]{1,0:T(8,128)(2,1)S(1)}, bf16[512,768]{1,0:T(8,128)(2,1)}, u32[]{:S(2)}) copy-start(bf16[512,768]{1,0:T(8,128)(2,1)} %get-tuple-element.81) | copy-start | bytes 2359300
  336.7 42.4 %collective-permute-start.13 = (bf16[512,768]{1,0:T(8,128)(2,1)}, bf16[512,768]{1,0:T(8,128)(2,1)}, u32[]{:S(2)}, u32[]{:S(2)}) collective-permute-start(bf16[512,768]{1,0:T(8,128)(2,1)} %add_convert_fusion), channel_id=1, source_target_pairs={{0,0},{1,2},{2,1},{3,3},{4,4},{5,6},{6,5},{7,7},{8,8},{9,10},{10,9... | collective-permute-start | bytes 2359304 | tf_op jit(solution)/shard_map/ppermute | solution.py:616
  344.2 8.6 %collective-permute-start.17 = (bf16[512,768]{1,0:T(8,128)(2,1)S(1)}, bf16[512,768]{1,0:T(8,128)(2,1)}, u32[]{:S(2)}, u32[]{:S(2)}) collective-permute-start(bf16[512,768]{1,0:T(8,128)(2,1)S(1)} %copy-done.26), channel_id=1, source_target_pairs={{0,2},{1,3},{2,0},{3,1},{4,6},{5,7},{6,4},{7,5},{8,10},{9,11},{10,... | collective-permute-start | bytes 2359304 | tf_op jit(solution)/shard_map/ppermute | solution.py:616
  350.1 35.3 %collective-permute-start.31 = (bf16[768,768]{1,0:T(8,128)(2,1)S(1)}, bf16[768,768]{1,0:T(8,128)(2,1)S(1)}, u32[]{:S(2)}, u32[]{:S(2)}) collective-permute-start(bf16[768,768]{1,0:T(8,128)(2,1)S(1)} %pad_maximum_fusion.3), channel_id=1, source_target_pairs={{0,2},{1,3},{2,0},{3,1},{4,6},{5,7},{6,4},{7,5},{8,10},{9,11},{10,... | collective-permute-start | bytes 3538952 | tf_op jit(solution)/shard_map/ppermute | solution.py:616
  352.3 45.2 %collective-permute-start.39 = (bf16[1536,768]{1,0:T(8,128)(2,1)}, bf16[1536,768]{1,0:T(8,128)(2,1)}, u32[]{:S(2)}, u32[]{:S(2)}) collective-permute-start(bf16[1536,768]{1,0:T(8,128)(2,1)} %pad_maximum_fusion.2), channel_id=1, source_target_pairs={{0,2},{1,3},{2,0},{3,1},{4,6},{5,7},{6,4},{7,5},{8,10},{9,11},{10,... | collective-permute-start | bytes 7077896 | tf_op jit(solution)/shard_map/ppermute | solution.py:616
  357.2 27.4 %collective-permute-start.18 = (bf16[512,768]{1,0:T(8,128)(2,1)}, bf16[512,768]{1,0:T(8,128)(2,1)S(1)}, u32[]{:S(2)}, u32[]{:S(2)}) collective-permute-start(bf16[512,768]{1,0:T(8,128)(2,1)} %get-tuple-element.83), channel_id=1, source_target_pairs={{0,0},{1,2},{2,1},{3,3},{4,4},{5,6},{6,5},{7,7},{8,8},{9,10},{10,9... | collective-permute-start | bytes 2359304 | tf_op jit(solution)/shard_map/ppermute | solution.py:616
  360.8 2.8 collective-permute-start.19
  363.8 7.8 %collective-permute-start.20 = (f32[8,768]{1,0:T(8,128)S(1)}, f32[8,768]{1,0:T(8,128)S(1)}, u32[]{:S(2)}, u32[]{:S(2)}) collective-permute-start(f32[8,768]{1,0:T(8,128)S(1)} %fusion), channel_id=1, source_target_pairs={{0,1},{1,0},{2,3},{3,2},{4,5},{5,4},{6,7},{7,6},{8,9},{9,8},{10,11... | collective-permute-start | bytes 73736 | tf_op jit(solution)/shard_map/ppermute | solution.py:616
  371.5 3.8 collective-permute-start.21
  375.4 3.8 collective-permute-start.22
  379.2 4.7 %collective-permute-start.23 = (f32[8,768]{1,0:T(8,128)S(1)}, f32[8,768]{1,0:T(8,128)S(1)}, u32[]{:S(2)}, u32[]{:S(2)}) collective-permute-start(f32[8,768]{1,0:T(8,128)S(1)} %add.100), channel_id=1, source_target_pairs={{0,16},{1,17},{2,6},{3,7},{4,20},{5,21},{6,2},{7,3},{8,24},{9,25},... | collective-permute-start | bytes 73736 | tf_op jit(solution)/shard_map/ppermute | solution.py:616
  405.9 2.2 copy-start.14
  405.9 3.1 copy-start.1
  (4 other events, 3.5 us)

commit v2 on v1

v2 whole, which is shorter than its diff:
```python
import functools

import jax
import jax.numpy as jnp
from jax import lax
from jax.experimental import pallas as pl
from jax.experimental.pallas import tpu as pltpu
from jax.sharding import PartitionSpec as P

HEAD_DIM = 64
EPS = 1e-05
FAR = 1e30
FORWARD_BLOCK = 512
BF16 = jnp.bfloat16
F32 = jnp.float32
TN = (((0,), (0,)), ((), ()))
NT = (((1,), (1,)), ((), ()))
NN = (((1,), (0,)), ((), ()))
TT = (((0,), (1,)), ((), ()))
ERF_C = (
    1.5897294934128858e-07,
    -5.985900079472216e-06,
    8.971378204617447e-05,
    -0.0006257225011275588,
    -0.0001843806018428344,
    0.10276548023357895,
    1.1283797055884355,
)
ERF_X = tuple(c * 0.5 ** (6 - i) * 0.7071067811865476 for i, c in enumerate(ERF_C))


def dot(left, right, dims):
    return lax.dot_general(left, right, dims, preferred_element_type=F32)


def sds(shape, dtype):
    return jax.ShapeDtypeStruct(shape, dtype)


SMEM = pl.BlockSpec(memory_space=pltpu.SMEM)
VMEM = pl.BlockSpec(memory_space=pltpu.VMEM)
ANY = pl.BlockSpec(memory_space=pl.ANY)


WEIGHT = 20.0


class Order:
    def __init__(self):
        self.last = None

    def run(self, us, kernel, operands, out_shape, in_specs=None, after=(), **rest):
        after = tuple(after) + (() if self.last is None else (self.last,))
        count, extra = len(operands), len(after)
        in_specs = list(in_specs or [VMEM] * count) + [ANY] * extra

        def body(*refs):
            kernel(*refs[:count], *refs[count + extra :])

        out = pl.pallas_call(
            body,
            out_shape=out_shape,
            in_specs=in_specs,
            compiler_params=pltpu.CompilerParams(vmem_limit_bytes=58 << 20),
            cost_estimate=pl.CostEstimate(
                flops=int(us * WEIGHT * 1.15e9), bytes_accessed=0, transcendentals=0
            ),
            **rest,
        )(*operands, *after)
        self.last = out[-1] if isinstance(out, (list, tuple)) else out
        return out


def hold(value, after):
    def kernel(*refs):
        pass

    return pl.pallas_call(
        kernel,
        out_shape=sds(value.shape, value.dtype),
        in_specs=[ANY] * (1 + len(after)),
        out_specs=ANY,
        input_output_aliases={0: 0},
        compiler_params=pltpu.CompilerParams(has_side_effects=True),
        cost_estimate=pl.CostEstimate(flops=0, bytes_accessed=0, transcendentals=0),
    )(value, *after)


def whole(shape):
    return pl.BlockSpec(shape, lambda *_: (0,) * len(shape))


def normalize(values):
    center = values - jnp.mean(values, axis=-1, keepdims=True)
    inverse = lax.rsqrt(jnp.mean(center * center, axis=-1, keepdims=True) + EPS)
    return center * inverse, inverse


def norm_back(grad_normed, scaled, inverse, gain):
    grad_scaled = grad_normed * gain
    return inverse * (
        grad_scaled
        - jnp.mean(grad_scaled, axis=-1, keepdims=True)
        - scaled * jnp.mean(grad_scaled * scaled, axis=-1, keepdims=True)
    )


def gelu_pair(x):
    square = x * x
    near = jnp.minimum(square, 64.0)
    poly = ERF_X[0]
    for coefficient in ERF_X[1:]:
        poly = poly * near + coefficient
    phi = 0.5 * jnp.tanh(x * poly) + 0.5
    bell = jnp.exp(square * -0.5)
    return x * phi, phi + x * (bell * 0.3989422804014327)


def pack_first_kernel(place, w_query, w_key, w_value, qkv, qkv_send, first):
    width = qkv.shape[1] // 3
    half = qkv_send.shape[0]
    first[:, :HEAD_DIM] = w_query[:, :HEAD_DIM]
    first[:, HEAD_DIM:] = w_key[:, :HEAD_DIM]
    for core in range(2):

        @pl.when(place[0] == core)
        def _():
            narrow = slice(core * width, (core + 1) * width)
            for i, weight in enumerate((w_query, w_key, w_value)):
                qkv[:, i * width : (i + 1) * width] = weight[:, narrow]

    qkv_send[...] = qkv[pl.ds(pl.multiple_of(place[2] * half, half), half), :]


def pack_first_call(order, place, w_query, w_key, w_value):
    dim, width = w_query.shape[0], w_query.shape[1] // 2
    return order.run(
        4,
        pack_first_kernel,
        (place, w_query, w_key, w_value),
        [
            sds((dim, 3 * width), BF16),
            sds((dim // 2, 3 * width), BF16),
            sds((dim, 2 * HEAD_DIM), BF16),
        ],
        [SMEM] + [VMEM] * 3,
    )


def pack_last_kernel(place, w_out, w_up, w_down, grad, out, up, up_send, down, down_send, grad_out):
    width = out.shape[0]
    units = down.shape[0]
    half = units // 2
    grad_out[...] = grad[...]
    for core in range(2):

        @pl.when(place[0] == core)
        def _():
            wide = slice(core * units, (core + 1) * units)
            out[...] = w_out[core * width : (core + 1) * width, :]
            up[...] = w_up[:, wide]
            down[...] = w_down[wide, :]

    rows = pl.ds(pl.multiple_of(place[2] * half, half), half)
    up_send[...] = up[rows, :]
    down_send[...] = down[rows, :]


def pack_last_call(order, place, w_out, w_up, w_down, grad):
    width, dim = w_out.shape[0] // 2, w_out.shape[1]
    units = w_up.shape[1] // 2
    return order.run(
        5,
        pack_last_kernel,
        (place, w_out, w_up, w_down, grad),
        [
            sds((width, dim), BF16),
            sds((dim, units), BF16),
            sds((dim // 2, units), BF16),
            sds((units, dim), BF16),
            sds((units // 2, dim), BF16),
            sds(grad.shape, BF16),
        ],
        [SMEM] + [VMEM] * 4,
    )


def norm1_kernel(tokens, gain, shift, out):
    scaled, _ = normalize(tokens[...].astype(F32))
    out[...] = (scaled * gain[...] + shift[...]).astype(BF16)


def rows_spec(block, dim):
    return pl.BlockSpec((block, dim), lambda i: (i, 0))


def norm1_call(order, tokens, gain, shift):
    return order.run(2.5, norm1_kernel, (tokens, gain, shift), sds(tokens.shape, BF16))


def masks(seg_pad, cols, low, high):
    width = high - low
    seg_row = seg_pad[0:1, low:high]
    pad_row = seg_pad[1:2, low:high]
    row_key = jnp.where(pad_row > 0, seg_row, -2.0)
    col_seg = cols[:high, 0:1]
    col_pad = cols[:high, 1:2]
    col_key = jnp.where(col_pad > 0, col_seg, -1.0)
    key_at = lax.broadcasted_iota(jnp.int32, (high, width), 0)
    query_at = lax.broadcasted_iota(jnp.int32, (high, width), 1) + low
    allowed = ((col_key == seg_row) & (key_at <= query_at)) | (key_at == query_at)
    picked = (col_key == row_key) & (key_at < query_at)
    return allowed, picked


def penalty_kernel(
    block, place, n1_own, n1_other, first, first_moved, seg_pad, n1_out, penalty, qk0, first_out
):
    seq = n1_out.shape[0]
    half = seq // 2
    core = place[0]
    n1_out[pl.ds(pl.multiple_of(core * half, half), half), :] = n1_own[...]
    n1_out[pl.ds(pl.multiple_of((1 - core) * half, half), half), :] = n1_other[...]

    @pl.when(place[1] == 0)
    def _():
        first_out[...] = first[...]

    @pl.when(place[1] != 0)
    def _():
        first_out[...] = first_moved[...]

    qk = dot(first_out[...], n1_out[...], TT)
    q0 = (qk[:HEAD_DIM].astype(BF16) * 0.125).astype(BF16)
    k0 = qk[HEAD_DIM:].astype(BF16)
    qk0[:HEAD_DIM, :] = q0
    qk0[HEAD_DIM:, :] = k0
    seg_value = seg_pad[...]
    cols = seg_value.T
    earlier = lax.broadcasted_iota(jnp.int32, (block, block + 128), 0)
    later = lax.broadcasted_iota(jnp.int32, (block, block + 128), 1)
    sums = ((earlier < later) | (later >= block)).astype(F32).astype(BF16)
    carry = jnp.zeros((seq, 128), F32)
    for low in range(0, seq, block):
        high = low + block
        allowed, picked = masks(seg_value, cols, low, high)
        score = dot(k0[:, :high], q0[:, low:high], TN)
        small = jnp.exp(-jnp.abs(score))
        log1p = jnp.where(small < 1e-3, small - 0.5 * small * small, jnp.log(1.0 + small))
        select = jnp.where(picked, jnp.maximum(score, 0.0) + log1p, 0.0).astype(BF16)
        total = dot(select, sums, NN)
        before = jnp.concatenate([carry[:high]] * (block // 128), axis=1)
        penalty[:high, low:high] = jnp.where(allowed, total[:, :block] + before, FAR)
        if high % FORWARD_BLOCK:
            edge = high + FORWARD_BLOCK - high % FORWARD_BLOCK
            penalty[high:edge, low:high] = jnp.full((edge - high, block), FAR, F32)
        carry = jnp.concatenate([carry[:high] + total[:, block:], carry[high:]], axis=0)


def penalty_call(order, place, n1_own, n1_other, first, first_moved, seg_pad, after=()):
    half, dim = n1_own.shape
    seq = 2 * half
    return order.run(
        6.5,
        functools.partial(penalty_kernel, 256),
        (place, n1_own, n1_other, first, first_moved, seg_pad),
        [
            sds((seq, dim), BF16),
            sds((seq, seq), F32),
            sds((2 * HEAD_DIM, seq), BF16),
            sds(first.shape, BF16),
        ],
        [SMEM] + [VMEM] * 5,
        after,
    )


def forward_kernel(block, split, *refs):
    if split:
        place, n1, near, far, penalty, qkv, out, lse, weights = refs
    else:
        n1, weights, penalty, qkv, out, lse = refs
    head = pl.program_id(0)
    third = qkv.shape[0] // 3
    seq = qkv.shape[1]

    @pl.when(head == 0)
    def _():
        if split:
            join(place[2], weights, near, far)
        product = dot(weights[...], n1[...], TT).astype(BF16)
        qkv[:third, :] = (product[:third] * 0.125).astype(BF16)
        qkv[third:, :] = product[third:]

    at = pl.multiple_of(head * HEAD_DIM, HEAD_DIM)
    query = qkv[pl.ds(at, HEAD_DIM), :]
    key = qkv[pl.ds(third + at, HEAD_DIM), :]
    value = qkv[pl.ds(2 * third + at, HEAD_DIM), :]
    value = jnp.concatenate([value, jnp.ones((16, seq), BF16)], axis=0)
    for low in range(0, seq, block):
        high = low + block
        logits = dot(key[:, :high], query[:, low:high], TN) - penalty[:high, low:high]
        largest = jnp.max(logits, axis=0, keepdims=True)
        weight = jnp.exp(logits - largest).astype(BF16)
        result = dot(value[:, :high], weight, NN)
        total = result[HEAD_DIM : HEAD_DIM + 1, :]
        out[:, low:high] = (result[:HEAD_DIM] / total).astype(BF16)
        lse[:, low:high] = largest + jnp.log(total)


def join(bit, out, near, far):
    half = near.shape[0]
    out[pl.ds(pl.multiple_of(bit * half, half), half), :] = near[...]
    out[pl.ds(pl.multiple_of((1 - bit) * half, half), half), :] = far[...]


def forward_call(order, n1, weights, penalty, place=None, after=()):
    seq, dim = n1.shape
    split = place is not None
    width = weights[0].shape[1]
    heads = width // (3 * HEAD_DIM)
    operands = ((place,) if split else ()) + (n1,) + tuple(weights) + (penalty,)
    in_specs = [SMEM] if split else []
    in_specs += [whole(x.shape) for x in operands if x is not place]
    out_specs = [
        whole((width, seq)),
        pl.BlockSpec((HEAD_DIM, seq), lambda h: (h, 0)),
        pl.BlockSpec((None, 1, seq), lambda h: (h, 0, 0)),
    ]
    out_shape = [
        sds((width, seq), BF16),
        sds((heads * HEAD_DIM, seq), BF16),
        sds((heads, 1, seq), F32),
    ]
    if split:
        out_specs.append(whole((dim, width)))
        out_shape.append(sds((dim, width), BF16))
    return order.run(
        9.3,
        functools.partial(forward_kernel, FORWARD_BLOCK, split),
        operands,
        out_shape,
        in_specs,
        after,
        grid=(heads,),
        out_specs=out_specs,
    )


def project_kernel(place, out_l, out_r, w_l, w_r, own, send):
    half = own.shape[0]
    core = place[0]
    mixed = jnp.concatenate([w_l[...], w_r[...]], axis=0)

    def part(which):
        at = pl.ds(pl.multiple_of(which * half, half), half)
        heads = jnp.concatenate([out_l[:, at], out_r[:, at]], axis=0)
        return dot(heads, mixed, TN)

    send[...] = part(1 - core).astype(BF16)
    own[...] = part(core)


def project_call(order, place, out_l, out_r, w_l, w_r, after=()):
    half, dim = out_l.shape[1] // 2, w_l.shape[1]
    return order.run(
        3.5,
        project_kernel,
        (place, out_l, out_r, w_l, w_r),
        [sds((half, dim), F32), sds((half, dim), BF16)],
        [SMEM] + [VMEM] * 4,
        after,
    )


def norm2_kernel(tokens, own, received, gain, shift, hidden, out):
    total = tokens[...].astype(F32) + (own[...] + received[...].astype(F32))
    hidden[...] = total
    scaled, _ = normalize(total)
    out[...] = (scaled * gain[...] + shift[...]).astype(BF16)


def norm2_call(order, tokens, own, received, gain, shift, after=()):
    size, dim = tokens.shape
    rows = rows_spec(size // 4, dim)
    vector = whole((1, dim))
    return order.run(
        4,
        norm2_kernel,
        (tokens, own, received, gain, shift),
        [sds(tokens.shape, F32), sds(tokens.shape, BF16)],
        [rows] * 3 + [vector] * 2,
        after,
        grid=(4,),
        out_specs=[rows, rows],
    )


def mlp_kernel(first, steps, *refs):
    if first:
        n2_other, n2_own, g_other, g_own, w_up, w_down, *refs = refs
        mixed_send, mixed_own, back_send, back_own, up_grad, down_grad, *refs = refs
    else:
        place, n2_other, n2_own, g_other, g_own, *refs = refs
        up_near, up_far, down_near, down_far, *refs = refs
        mixed_in_send, mixed_in_own, back_in_send, back_in_own, down_l, *refs = refs
        mixed_send, mixed_own, back_send, back_own, up_grad, down_send, down_keep, *refs = refs
        w_up, w_down, *refs = refs
    rows, grads, actives, grad_ups = refs
    step = pl.program_id(0)
    block = n2_own.shape[0]
    early = step < steps // 2

    if not first:

        @pl.when(step == 0)
        def _():
            join(place[2], w_up, up_near, up_far)
            join(place[2], w_down, down_near, down_far)

    here = pl.ds(pl.multiple_of(step * block, block), block)
    row = jnp.where(early, n2_other[...], n2_own[...])
    grad = jnp.where(early, g_other[...], g_own[...])
    rows[here, :] = row
    grads[here, :] = grad
    active, slope = gelu_pair(dot(row, w_up[...], NN))
    active = active.astype(BF16)
    grad_up = (dot(grad, w_down[...], NT) * slope).astype(BF16)
    actives[here, :] = active
    grad_ups[here, :] = grad_up
    back = dot(grad_up, w_up[...], NT)
    mixed = dot(active, w_down[...], NN)

    @pl.when(early)
    def _():
        if first:
            back_send[...] = back.astype(back_send.dtype)
            mixed_send[...] = mixed.astype(mixed_send.dtype)
        else:
            back_send[...] = (back + back_in_send[...]).astype(back_send.dtype)
            mixed_send[...] = (mixed + mixed_in_send[...]).astype(mixed_send.dtype)

    @pl.when(jnp.logical_not(early))
    def _():
        if first:
            back_own[...] = back
            mixed_own[...] = mixed
        else:
            back_own[...] = back + back_in_own[...]
            mixed_own[...] = mixed + mixed_in_own[...]

    @pl.when(step == steps - 1)
    def _():
        up_grad[...] = dot(rows[...], grad_ups[...], TN).astype(BF16)
        down = dot(actives[...], grads[...], TN).astype(BF16)
        if first:
            down_grad[...] = down
        else:
            half = down.shape[0] // 2
            for bit in range(2):

                @pl.when(place[2] == bit)
                def _():
                    kept = slice(bit * half, (bit + 1) * half)
                    sent = slice((1 - bit) * half, (2 - bit) * half)
                    down_send[0] = down_l[sent, :]
                    down_send[1] = down[sent, :]
                    down_keep[0] = down_l[kept, :]
                    down_keep[1] = down[kept, :]


def mlp_call(order, n2_other, n2_own, g_other, g_own, weights, place=None, before=None, after=()):
    size, dim = n2_own.shape
    first = before is None
    units = weights[0].shape[1]
    block = min(256, size // 2)
    steps = 2 * size // block
    last = steps // 2 - 1
    sent = pl.BlockSpec((block, dim), lambda i: (jnp.minimum(i, last), 0))
    kept = pl.BlockSpec((block, dim), lambda i: (jnp.maximum(i - last - 1, 0), 0))
    operands = () if first else (place,)
    operands += (n2_other, n2_own, g_other, g_own) + tuple(weights)
    in_specs = [] if first else [SMEM]
    in_specs += [sent, kept, sent, kept] + [whole(weight.shape) for weight in weights]
    sent_type = F32 if first else BF16
    square = whole((dim, units))
    out_specs = [sent, kept, sent, kept, square]
    out_shape = [
        sds((size, dim), sent_type),
        sds((size, dim), F32),
        sds((size, dim), sent_type),
        sds((size, dim), F32),
        sds((dim, units), BF16),
    ]
    scratch = []
    if first:
        out_specs.append(whole((units, dim)))
        out_shape.append(sds((units, dim), BF16))
    else:
        operands += tuple(before)
        in_specs += [sent, kept, sent, kept, whole((units, dim))]
        out_specs += [whole((2, units // 2, dim))] * 2
        out_shape += [sds((2, units // 2, dim), BF16)] * 2
        scratch = [pltpu.VMEM((dim, units), BF16), pltpu.VMEM((units, dim), BF16)]
    tall = pltpu.VMEM((2 * size, dim), BF16)
    flat = pltpu.VMEM((2 * size, units), BF16)
    return order.run(
        14.6,
        functools.partial(mlp_kernel, first, steps),
        operands,
        out_shape,
        in_specs,
        after,
        grid=(steps,),
        out_specs=out_specs,
        scratch_shapes=scratch + [tall, tall, flat, flat],
    )


def norm2_back_kernel(hidden, own, received, grad, gain, grad_hidden, low, sums):
    normed_grad = own[...] + received[...].astype(F32)
    scaled, inverse = normalize(hidden[...])
    total = grad[...].astype(F32) + norm_back(normed_grad, scaled, inverse, gain[...])
    grad_hidden[...] = total
    low[...] = total.astype(BF16)
    add_sums(sums, normed_grad, scaled)


def add_sums(sums, normed_grad, scaled):
    @pl.when(pl.program_id(0) == 0)
    def _():
        sums[...] = jnp.zeros(sums.shape, F32)

    sums[0:1, :] += jnp.sum(normed_grad * scaled, axis=0, keepdims=True)
    sums[1:2, :] += jnp.sum(normed_grad, axis=0, keepdims=True)


def norm2_back_call(order, hidden, own, received, grad, gain, after=()):
    size, dim = hidden.shape
    rows = rows_spec(size // 4, dim)
    return order.run(
        5,
        norm2_back_kernel,
        (hidden, own, received, grad, gain),
        [sds(hidden.shape, F32), sds(hidden.shape, BF16), sds((8, dim), F32)],
        [rows] * 4 + [whole((1, dim))],
        after,
        grid=(4,),
        out_specs=[rows, rows, whole((8, dim))],
    )


def mixed_kernel(hidden, own, received, out):
    out[...] = (hidden[...] + (own[...] + received[...].astype(F32))).astype(BF16)


def mixed_call(order, hidden, own, received, after=()):
    size, dim = hidden.shape
    rows = rows_spec(size // 2, dim)
    return order.run(
        3,
        mixed_kernel,
        (hidden, own, received),
        sds(hidden.shape, BF16),
        [rows] * 3,
        after,
        grid=(2,),
        out_specs=rows,
    )


def backward_kernel(start, heads, first, final, wide, block, *refs):
    place, g_own, g_other, w_out, *refs = refs
    if wide:
        heads_out, *refs = refs
    qkv, lse, penalty, *refs = refs
    if not first:
        before, *refs = refs
    grads, *refs = refs
    if wide:
        w_grad, *refs = refs
    logit_sum, grad_full, grad_heads, key_sum, value_sum, *refs = refs
    head = pl.program_id(0)
    third = qkv.shape[0] // 3
    seq = qkv.shape[1]
    half = seq // 2
    total = refs[0] if final and heads > 1 else logit_sum

    @pl.when(head == 0)
    def _():
        core = place[0]
        grad_full[pl.ds(pl.multiple_of(core * half, half), half), :] = g_own[...]
        grad_full[pl.ds(pl.multiple_of((1 - core) * half, half), half), :] = g_other[...]
        whole_grad = grad_full[...]
        rows = slice(start * HEAD_DIM, (start + heads) * HEAD_DIM)
        grad_heads[...] = dot(w_out[rows, :], whole_grad, NT).astype(BF16)
        if wide:
            w_grad[...] = dot(heads_out[...], whole_grad, NN).astype(BF16)

    out_at = pl.multiple_of(head * HEAD_DIM, HEAD_DIM)
    at = pl.multiple_of((start + head) * HEAD_DIM, HEAD_DIM)
    size = heads * HEAD_DIM
    query = qkv[pl.ds(at, HEAD_DIM), :]
    key = qkv[pl.ds(third + at, HEAD_DIM), :]
    value = qkv[pl.ds(2 * third + at, HEAD_DIM), :]
    grad = grad_heads[pl.ds(out_at, HEAD_DIM), :]
    for low in range(0, seq, block):
        high = low + block
        cols = slice(low, high)
        score = dot(key[:, :high], query[:, cols], TN)
        probs = jnp.exp(score - penalty[:high, cols] - lse[:, cols])
        grad_probs = dot(value[:, :high], grad[:, cols], TN)
        row_dot = jnp.sum(probs * grad_probs, axis=0, keepdims=True)
        grad_logits = probs * (grad_probs - row_dot)
        if final and heads == 1:
            if first:
                logit_sum[:high, cols] = grad_logits.astype(logit_sum.dtype)
            else:
                logit_sum[:high, cols] = (before[:high, cols] + grad_logits).astype(BF16)
        else:

            @pl.when(head == 0)
            def _():
                if first:
                    total[:high, cols] = grad_logits
                else:
                    total[:high, cols] = before[:high, cols] + grad_logits

            @pl.when(head > 0)
            def _():
                total[:high, cols] += grad_logits

        low_logits = grad_logits.astype(BF16)
        low_probs = probs.astype(BF16)
        grads[pl.ds(out_at, HEAD_DIM), cols] = (
            dot(key[:, :high], low_logits, NN) * 0.125
        ).astype(BF16)
        value_new = dot(grad[:, cols], low_probs, NT)
        key_new = dot(query[:, cols], low_logits, NT)
        if low:
            key_sum[:, :low] += key_new[:, :low]
            value_sum[:, :low] += value_new[:, :low]
        key_sum[:, cols] = key_new[:, low:]
        value_sum[:, cols] = value_new[:, low:]
    grads[pl.ds(size + out_at, HEAD_DIM), :] = key_sum[...].astype(BF16)
    grads[pl.ds(2 * size + out_at, HEAD_DIM), :] = value_sum[...].astype(BF16)
    if final and heads > 1:

        @pl.when(head == heads - 1)
        def _():
            for low in range(0, seq, block):
                high = low + block
                logit_sum[:high, low:high] = total[:high, low:high].astype(BF16)


def backward_call(
    order, place, g_own, g_other, w_out, heads_out, qkv, lse, penalty, start, heads, before, final
):
    width, seq = qkv.shape
    half, dim = g_own.shape
    first, wide = before is None, heads_out is not None
    square = whole((seq, seq))
    operands = (place, g_own, g_other, w_out) + ((heads_out,) if wide else ())
    in_specs = [SMEM] + [whole(x.shape) for x in operands[1:]]
    operands += (qkv, lse, penalty)
    in_specs += [
        whole((width, seq)),
        pl.BlockSpec((None, 1, seq), lambda h: (h + start, 0, 0)),
        square,
    ]
    if not first:
        operands += (before,)
        in_specs.append(square)
    size = heads * HEAD_DIM
    out_specs = [whole((3 * size, seq))]
    out_shape = [sds((3 * size, seq), BF16)]
    if wide:
        out_specs.append(whole(w_out.shape))
        out_shape.append(sds(w_out.shape, BF16))
    out_specs.append(square)
    out_shape.append(sds((seq, seq), BF16 if final else F32))
    scratch = [
        pltpu.VMEM((seq, dim), BF16),
        pltpu.VMEM((size, seq), BF16),
        pltpu.VMEM((HEAD_DIM, seq), F32),
        pltpu.VMEM((HEAD_DIM, seq), F32),
    ]
    if final and heads > 1:
        scratch.append(pltpu.VMEM((seq, seq), F32))
    return order.run(
        5.5 * heads,
        functools.partial(backward_kernel, start, heads, first, final, wide, 256),
        operands,
        out_shape,
        in_specs,
        grid=(heads,),
        out_specs=out_specs,
        scratch_shapes=scratch,
    )


def halves(value):
    high = value.astype(BF16)
    return high, (value - high.astype(F32)).astype(BF16)


def select_back_kernel(block, place, own, received, qk0, seg_pad, n1, out, w_grad, total_grad):
    seq = own.shape[0]
    q0 = qk0[:HEAD_DIM, :]
    k0 = qk0[HEAD_DIM:, :]
    seg_value = seg_pad[...]
    cols = seg_value.T
    later = lax.broadcasted_iota(jnp.int32, (block, block + 128), 0)
    earlier = lax.broadcasted_iota(jnp.int32, (block, block + 128), 1)
    sums = ((later > earlier) | (earlier >= block)).astype(F32).astype(BF16)
    carry = jnp.zeros((seq, 128), F32)
    total_grad[...] = jnp.zeros(total_grad.shape, F32)
    for low in range(seq - block, -1, -block):
        high = low + block
        logit_sum = own[:high, low:high].astype(F32) + received[:high, low:high].astype(F32)
        top, bottom = halves(logit_sum)
        total = dot(top, sums, NN) + dot(bottom, sums, NN)
        after = jnp.concatenate([carry[:high]] * (block // 128), axis=1)
        select_grad = -(total[:, :block] + after)
        carry = carry[:high] + total[:, block:]
        _, picked = masks(seg_value, cols, low, high)
        score = dot(k0[:, :high], q0[:, low:high], TN)
        through = jnp.where(picked, select_grad / (1.0 + jnp.exp(-score)), 0.0)
        top, bottom = halves(through)
        total_grad[:HEAD_DIM, low:high] = 0.125 * (
            dot(k0[:, :high], top, NN) + dot(k0[:, :high], bottom, NN)
        )
        total_grad[HEAD_DIM:, :high] += dot(q0[:, low:high], top, NT) + dot(
            q0[:, low:high], bottom, NT
        )
    out[...] = jnp.where(place[0] == 0, total_grad[...], 0.0).astype(BF16)
    w_grad[...] = dot(out[...], n1[...], NN).astype(BF16)


def select_back_call(order, place, own, received, qk0, seg_pad, n1, after=()):
    return order.run(
        8.4,
        functools.partial(select_back_kernel, 256),
        (place, own, received, qk0, seg_pad, n1),
        [sds(qk0.shape, BF16), sds((qk0.shape[0], n1.shape[1]), BF16)],
        [SMEM] + [VMEM] * 5,
        after,
        scratch_shapes=[pltpu.VMEM(qk0.shape, F32)],
    )


def weights_first_kernel(place, n1, grads, weights, w_out, back, send, keep, late):
    width = grads.shape[0]
    third = width // 3
    half = keep.shape[0]
    early_out = 2 * half - 2 * (width // 3 - HEAD_DIM) - (third - HEAD_DIM)
    product = dot(grads[...], n1[...], NN).astype(BF16)
    tail = w_out[...]
    early = [product[i * third + HEAD_DIM : (i + 1) * third] for i in range(3)]
    early = jnp.concatenate(early + [tail[:early_out]], axis=0)
    for i in range(3):
        late[i * HEAD_DIM : (i + 1) * HEAD_DIM, :] = product[i * third : i * third + HEAD_DIM]
    late[3 * HEAD_DIM :, :] = tail[early_out:]
    for bit in range(2):

        @pl.when(place[2] == bit)
        def _():
            keep[...] = early[bit * half : (bit + 1) * half]
            send[...] = early[(1 - bit) * half : (2 - bit) * half]

    back[...] = dot(grads[...], weights[...], TT)


def weights_first_call(order, place, n1, grads, weights, w_out):
    seq, dim = n1.shape
    late = 4 * HEAD_DIM
    half = (grads.shape[0] + w_out.shape[0] - late) // 2
    return order.run(
        6,
        weights_first_kernel,
        (place, n1, grads, weights, w_out),
        [
            sds((seq, dim), F32),
            sds((half, dim), BF16),
            sds((half, dim), BF16),
            sds((late, dim), BF16),
        ],
        [SMEM] + [VMEM] * 4,
    )


def weights_middle_kernel(place, n1, grads, w_out, send, keep):
    half = keep.shape[0]
    product = dot(grads[...], n1[...], NN).astype(BF16)
    early = jnp.concatenate([product, w_out[: 2 * half - product.shape[0], :]], axis=0)
    for bit in range(2):

        @pl.when(place[2] == bit)
        def _():
            keep[...] = early[bit * half : (bit + 1) * half]
            send[...] = early[(1 - bit) * half : (2 - bit) * half]


def weights_middle_call(order, place, n1, grads, w_out):
    dim = n1.shape[1]
    half = (grads.shape[0] + w_out.shape[0] - HEAD_DIM) // 2
    return order.run(
        3,
        weights_middle_kernel,
        (place, n1, grads, w_out),
        [sds((half, dim), BF16)] * 2,
        [SMEM] + [VMEM] * 3,
    )


def weights_last_kernel(
    place, n1, grads_one, grads_rest, extra, weights, first, before, w_out, own, send, late
):
    half = own.shape[0]
    core = place[0]
    rest = grads_rest.shape[0] // 3
    pieces = []
    for i in range(3):
        pieces.append(grads_one[i * HEAD_DIM : (i + 1) * HEAD_DIM, :])
        pieces.append(grads_rest[i * rest : (i + 1) * rest, :])
    grads = jnp.concatenate(pieces, axis=0)
    late[: 3 * HEAD_DIM, :] = dot(grads_one[...], n1[...], NN)
    late[3 * HEAD_DIM :, :] = w_out[w_out.shape[0] - HEAD_DIM :, :].astype(F32)
    total = before[...] + dot(grads, weights[...], TT) + dot(extra[...], first[...], TT)

    for which in range(2):

        @pl.when(core == which)
        def _():
            own[...] = total[which * half : (which + 1) * half]
            send[...] = total[(1 - which) * half : (2 - which) * half].astype(BF16)


def weights_last_call(order, place, n1, grads_one, grads_rest, extra, weights, first, before, w_out):
    seq, dim = n1.shape
    return order.run(
        7,
        weights_last_kernel,
        (place, n1, grads_one, grads_rest, extra, weights, first, before, w_out),
        [
            sds((seq // 2, dim), F32),
            sds((seq // 2, dim), BF16),
            sds((4 * HEAD_DIM, dim), F32),
        ],
        [SMEM] + [VMEM] * 8,
    )


def norm1_back_kernel(tokens, own, received, grad_hidden, gain, out, sums):
    normed_grad = own[...] + received[...].astype(F32)
    scaled, inverse = normalize(tokens[...].astype(F32))
    total = grad_hidden[...] + norm_back(normed_grad, scaled, inverse, gain[...])
    out[...] = total.astype(BF16)
    add_sums(sums, normed_grad, scaled)


def norm1_back_call(order, tokens, own, received, grad_hidden, gain, after=()):
    size, dim = tokens.shape
    rows = rows_spec(size // 4, dim)
    return order.run(
        4.6,
        norm1_back_kernel,
        (tokens, own, received, grad_hidden, gain),
        [sds(tokens.shape, BF16), sds((8, dim), F32)],
        [rows] * 4 + [whole((1, dim))],
        after,
        grid=(4,),
        out_specs=[rows, whole((8, dim))],
    )


def low_sum(*terms):
    total = terms[0].astype(F32)
    for term in terms[1:]:
        total = total + term.astype(F32)
    return total.astype(BF16)


def split(place, bit, terms, keep, send):
    half = keep.shape[1]
    for out, which in ((keep, place[2 + bit]), (send, 1 - place[2 + bit])):
        rows = pl.ds(pl.multiple_of(which * half, half), half)
        out[...] = low_sum(*(term[:, rows, :] for term in terms))


def merge(place, bit, near, far, out):
    half = near.shape[1]
    for part, which in ((near, place[2 + bit]), (far, 1 - place[2 + bit])):
        out[:, pl.ds(pl.multiple_of(which * half, half), half), :] = part[...]


def step1_kernel(place, down_keep, down_got, up_l, up_got, down_near, down_move, up_keep, up_send):
    total = low_sum(down_keep[...], down_got[...])
    down_near[...] = total[0]
    down_move[...] = total[1]
    split(place, 0, (up_l, up_got), up_keep, up_send)


def step1_call(order, place, down_keep, down_got, up_l, up_got):
    _, half, dim = down_keep.shape
    return order.run(
        3,
        step1_kernel,
        (place, down_keep, down_got, up_l, up_got),
        [sds((half, dim), BF16)] * 2 + [sds((1, half, dim), BF16)] * 2,
        [SMEM] + [VMEM] * 4,
    )


def step2_kernel(place, at_keep, at_got, up_keep, up_got, near, got, at_move, ff_keep, ff_send, total):
    at_move[...] = low_sum(at_keep[...], at_got[...])
    total[0] = low_sum(up_keep[0], up_got[0])
    total[1] = low_sum(near[...], got[...])
    split(place, 1, (total,), ff_keep, ff_send)


def step2_call(order, place, at_keep, at_got, up_keep, up_got, near, got):
    half, dim = near.shape
    return order.run(
        3,
        step2_kernel,
        (place, at_keep, at_got, up_keep, up_got, near, got),
        [sds(at_keep.shape, BF16)] + [sds((2, half // 2, dim), BF16)] * 2,
        [SMEM] + [VMEM] * 6,
        scratch_shapes=[pltpu.VMEM((2, half, dim), BF16)],
    )


def step3_kernel(at_keep, at_got, at_got_r, ff_keep, ff_got, at, ff):
    at[...] = low_sum(at_keep[...], at_got[...], at_got_r[...])
    ff[...] = low_sum(ff_keep[...], ff_got[...])


def step3_call(order, at_terms, ff_terms):
    return order.run(
        3,
        step3_kernel,
        (*at_terms, *ff_terms),
        [sds(at_terms[0].shape, BF16), sds(ff_terms[0].shape, BF16)],
    )


def step4_kernel(place, late, late_got, extra_own, extra_moved, at_own, at_got, ff_own, ff_got, *outs):
    late_out, at, ff = outs
    at[...] = low_sum(at_own[...], at_got[...])
    ff[...] = low_sum(ff_own[...], ff_got[...])
    rows = extra_own.shape[0]
    ours = ((place[0] == 0) & (place[1] == 0)).astype(F32)
    total = late[...] + late_got[...].astype(F32)
    extra = extra_own[...].astype(F32) + extra_moved[...].astype(F32)
    late_out[:rows, :] = (total[:rows] + ours * extra).astype(BF16)
    late_out[rows:, :] = total[rows:].astype(BF16)


def step4_call(order, place, late, late_got, extra_own, extra_moved, at_terms, ff_terms):
    return order.run(
        3.5,
        step4_kernel,
        (place, late, late_got, extra_own, extra_moved, *at_terms, *ff_terms),
        [sds(late.shape, BF16), sds(at_terms[0].shape, BF16), sds(ff_terms[0].shape, BF16)],
        [SMEM] + [VMEM] * 8,
    )


def step5_kernel(place, late_own, late_got, norms_own, norms_got, at_own, at_got, ff_near, ff_far, *outs):
    late, at, ff = outs
    rows = late_own.shape[0]
    late[:rows, :] = low_sum(late_own[...], late_got[...])
    high, low = halves(norms_own[...] + norms_got[...])
    late[rows : rows + 8, :] = high
    late[rows + 8 :, :] = low
    at[...] = low_sum(at_own[...], at_got[...])
    merge(place, 1, ff_near, ff_far, ff)


def step5_call(order, place, late_terms, norms_terms, at_terms, ff_near, ff_far):
    rows, dim = late_terms[0].shape
    groups, size, _ = ff_near.shape
    return order.run(
        3.5,
        step5_kernel,
        (place, *late_terms, *norms_terms, *at_terms, ff_near, ff_far),
        [
            sds((rows + 16, dim), BF16),
            sds(at_terms[0].shape, BF16),
            sds((groups, 2 * size, dim), BF16),
        ],
        [SMEM] + [VMEM] * 8,
    )


def add_late(own, got, out):
    rows = own.shape[0] - 16
    out[:rows, :] = low_sum(own[:rows, :], got[:rows, :])

    def norms(ref):
        return ref[rows : rows + 8, :].astype(F32) + ref[rows + 8 :, :].astype(F32)

    high, low = halves(norms(own) + norms(got))
    out[rows : rows + 8, :] = high
    out[rows + 8 :, :] = low


def step6_kernel(place, late_own, late_got, at_near, at_far, ff_near, ff_far, late, at, ff):
    add_late(late_own, late_got, late)
    merge(place, 0, at_near, at_far, at)
    merge(place, 0, ff_near, ff_far, ff)


def step6_call(order, place, late_terms, at_near, at_far, ff_near, ff_far):
    dim = at_near.shape[2]
    groups, size, _ = ff_near.shape
    return order.run(
        3.5,
        step6_kernel,
        (place, *late_terms, at_near, at_far, ff_near, ff_far),
        [
            sds(late_terms[0].shape, BF16),
            sds((1, 2 * at_near.shape[1], dim), BF16),
            sds((groups, 2 * size, dim), BF16),
        ],
        [SMEM] + [VMEM] * 6,
    )


def step7_kernel(late_own, late_got, mixed, grad, late, mixed_out, grad_out):
    add_late(late_own, late_got, late)
    mixed_out[...] = mixed[...]
    grad_out[...] = grad[...]


def step7_call(order, late_terms, mixed, grad):
    shape = sds(mixed.shape, BF16)
    return order.run(
        2.5,
        step7_kernel,
        (*late_terms, mixed, grad),
        [sds(late_terms[0].shape, BF16), shape, shape],
    )


def finish_attention_kernel(place, near, far, late_near, late_far, w_query, w_key, w_value, w_out, norms):
    width = w_out.shape[0] // 2
    early = near.shape[0]
    pair = width - HEAD_DIM
    rows = 4 * HEAD_DIM
    total = jnp.zeros(norms.shape, F32)
    for ref in (late_near, late_far):
        total = total + (ref[rows : rows + 8, :].astype(F32) + ref[rows + 8 :, :].astype(F32))
    norms[...] = total
    for core in range(2):

        @pl.when(place[0] == core)
        def _():
            low, high = ((near, late_near), (far, late_far))[:: 1 if core == 0 else -1]
            for i, out in enumerate((w_query, w_key, w_value)):
                one = slice(i * HEAD_DIM, (i + 1) * HEAD_DIM)
                rest = slice(i * pair, (i + 1) * pair)
                both = [low[1][one, :], low[0][rest, :], high[1][one, :], high[0][rest, :]]
                out[...] = jnp.concatenate(both, axis=0).astype(F32).T
            for at, (most, last) in ((0, low), (width, high)):
                edge = at + early - 3 * pair
                w_out[at:edge, :] = most[3 * pair :, :].astype(F32)
                w_out[edge : at + width, :] = last[3 * HEAD_DIM : rows, :].astype(F32)


def finish_attention_call(order, place, near, far, late_near, late_far):
    rows, dim = near.shape
    width = (rows + 4 * HEAD_DIM) // 4
    return order.run(
        4.5,
        finish_attention_kernel,
        (place, near, far, late_near, late_far),
        [sds((dim, 2 * width), F32)] * 3 + [sds((2 * width, dim), F32), sds((8, dim), F32)],
        [SMEM] + [VMEM] * 4,
    )


def finish_mlp_kernel(place, near, far, w_up, w_down):
    units = near.shape[1]
    for core in range(2):

        @pl.when(place[0] == core)
        def _():
            low, high = (near, far) if core == 0 else (far, near)
            w_up[:, :units] = low[0].astype(F32)
            w_up[:, units:] = high[0].astype(F32)
            w_down[:units, :] = low[1].astype(F32)
            w_down[units:, :] = high[1].astype(F32)


def finish_mlp_call(order, place, near, far):
    _, units, dim = near.shape
    return order.run(
        6.8,
        finish_mlp_kernel,
        (place, near, far),
        [sds((dim, 2 * units), F32), sds((2 * units, dim), F32)],
        [SMEM] + [VMEM] * 2,
    )


def make_body(devices, parts):
    axes = ("dp", "tensor")
    chips = devices // 2
    in_order = [1 << bit for bit in range(chips.bit_length() - 1)]
    turned = in_order[1:] + in_order[:1]
    rounds = len(in_order)
    rounds_more = range(3, rounds)

    def pairs(move):
        found = []
        for device in range(devices):
            for part in range(parts):
                to_chip, to_core, to_part = move(device // 2, device % 2, part)
                source = device * parts + part
                found.append((source, (to_chip * 2 + to_core) * parts + to_part))
        return found

    def by_bit(bit):
        return pairs(
            lambda chip, core, part: (chip ^ (turned if core else in_order)[bit], core, part)
        )

    by_role = pairs(lambda chip, core, part: (chip, part, core))
    by_core = pairs(lambda chip, core, part: (chip, 1 - core, part))
    by_part = pairs(lambda chip, core, part: (chip, core, 1 - part))
    from_first_part = [pair for pair in by_part if pair[0] % parts == 0]
    extra_to_first = [
        pair for pair in by_part if pair[0] % parts == 1 and (pair[0] // parts) % 2 == 0
    ]
    to_first_core = [pair for pair in by_core if (pair[0] // parts) % 2 == 1]
    by_chip = [by_bit(bit) for bit in range(rounds)]

    def move(value, how):
        return lax.ppermute(value, axes, how)

    def add_more(value):
        for bit in rounds_more:
            other = move(value, by_chip[bit])
            value = (value.astype(F32) + other.astype(F32)).astype(value.dtype)
        return value

    def body(
        tokens,
        segment_ids,
        pad_mask,
        norm1_gain,
        norm1_shift,
        w_query,
        w_key,
        w_value,
        w_out,
        norm2_gain,
        norm2_shift,
        w_up,
        w_down,
        cotangent,
    ):
        order = Order()
        device = lax.axis_index("dp")
        part = lax.axis_index("tensor")
        core = device % 2
        chip = device // 2
        bits = [
            jnp.where(core == 1, (chip & turned[i]) != 0, (chip & in_order[i]) != 0)
            for i in range(rounds)
        ]
        place = jnp.stack([core, part] + bits).astype(jnp.int32)
        gain1, shift1, gain2, shift2 = (
            vector[None, :] for vector in (norm1_gain, norm1_shift, norm2_gain, norm2_shift)
        )

        mine = move(tokens, by_role)
        ints = jnp.concatenate([segment_ids, pad_mask], axis=0)
        ints = jnp.where(core == part, ints, move(ints, by_core)).astype(F32)
        seg_pad = jnp.concatenate([ints, jnp.zeros((6, ints.shape[1]), F32)], axis=0)

        qkv_l, qkv_s, first = pack_first_call(order, place, w_query, w_key, w_value)
        first_moved = move(first, from_first_part)
        qkv_near = move(qkv_s, by_part)
        n1_own = norm1_call(order, mine, gain1, shift1)
        n1_other = move(n1_own, by_core)
        out_l, up_l, up_s, down_l, down_s, grad = pack_last_call(
            order, place, w_out, w_up, w_down, cotangent
        )
        out_r = move(out_l, by_part)
        up_near = move(up_s, by_part)
        grad_own = move(grad, by_role)
        down_near = move(down_s, by_part)
        n1, penalty, qk0, first = penalty_call(
            order, place, n1_own, n1_other, first, first_moved, seg_pad
        )
        qkv_near = hold(qkv_near, (penalty,))
        qkv_far = move(qkv_near, by_chip[0])
        qkvt_l, heads_l, lse_l = forward_call(order, n1, (qkv_l,), penalty)
        qkvt_r, heads_r, lse_r, qkv_r = forward_call(
            order, n1, (qkv_near, qkv_far), penalty, place, after=(up_near,)
        )
        up_near = hold(up_near, (lse_r,))
        up_far = move(up_near, by_chip[0])
        grad_own = hold(grad_own, (lse_r,))
        grad_other = move(grad_own, by_core)
        own, send = project_call(order, place, heads_l, heads_r, out_l, out_r, after=(down_near,))
        down_near = hold(down_near, (send,))
        down_far = move(down_near, by_chip[0])
        hidden, n2_own = norm2_call(order, mine, own, move(send, by_core), gain2, shift2)
        n2_other = move(n2_own, by_core)
        mixed_send, mixed_own, back_send, back_own, up_sum_l, down_sum_l = mlp_call(
            order, n2_other, n2_own, grad_other, grad_own, (up_l, down_l)
        )
        before = (mixed_send, mixed_own, back_send, back_own, down_sum_l)
        mixed_send, mixed_own, back_send, back_own, up_sum_r, down_send, down_keep = mlp_call(
            order,
            n2_other,
            n2_own,
            grad_other,
            grad_own,
            (up_near, up_far, down_near, down_far),
            place,
            before,
        )
        down_got = move(down_send, by_chip[0])
        up_got = move(up_sum_r, by_part)

        grad_hidden, low_own, sums2 = norm2_back_call(
            order, hidden, back_own, move(back_send, by_core), grad_own, gain2
        )
        low_other = move(low_own, by_core)
        mixed = mixed_call(order, hidden, mixed_own, move(mixed_send, by_core))
        mixed = move(mixed, by_role)

        low = (low_own, low_other)
        grads_r, wo_r, logit_sum = backward_call(
            order, place, *low, out_r, heads_r, qkvt_r, lse_r, penalty, 0, 3, None, False
        )
        back, at_send_r, at_keep_r, late_r = weights_first_call(
            order, place, n1, grads_r, qkv_r, wo_r
        )
        late_got = move(late_r, by_part)
        at_got_r = move(at_send_r, by_chip[0])
        down_near, down_move, up_keep, up_send = step1_call(
            order, place, down_keep, down_got, up_sum_l[None], up_got[None]
        )
        down_got = move(down_move, by_part)
        up_got = move(up_send, by_chip[0])
        grads_rest, wo_l, logit_sum = backward_call(
            order, place, *low, out_l, heads_l, qkvt_l, lse_l, penalty, 1, 2, logit_sum, False
        )
        at_send, at_keep = weights_middle_call(order, place, n1, grads_rest, wo_l)
        at_got = move(at_send, by_chip[0])
        at_r, ff, ff_send = step2_call(
            order, place, at_keep_r, at_got_r, up_keep, up_got, down_near, down_got
        )
        at_got_r = move(at_r, by_part)
        ff_got = move(ff_send, by_chip[1])
        grads_one, logit_sum = backward_call(
            order, place, *low, out_l, None, qkvt_l, lse_l, penalty, 0, 1, logit_sum, True
        )
        logit_got = move(logit_sum, to_first_core)
        at, ff = step3_call(order, (at_keep[None], at_got[None], at_got_r[None]), (ff, ff_got))
        at_got = move(at, by_chip[1])
        ff_got = move(ff, by_chip[2])
        extra, extra_w = select_back_call(order, place, logit_sum, logit_got, qk0, seg_pad, n1)
        extra_moved = move(extra_w, extra_to_first)
        own, send, late = weights_last_call(
            order, place, n1, grads_one, grads_rest, extra, qkv_l, first, back, wo_l
        )
        received = move(send, by_core)
        late, at, ff = step4_call(
            order, place, late, late_got, extra_w, extra_moved, (at, at_got), (ff, ff_got)
        )
        late_got = move(late, by_chip[0])
        at_got = move(at, by_chip[2])
        ff = add_more(ff)
        ff_far = move(ff, by_chip[1])
        tokens_grad, sums1 = norm1_back_call(order, mine, own, received, grad_hidden, gain1)
        tokens_grad = move(tokens_grad, by_role)
        norms = jnp.concatenate([sums1[:2], sums2[:2], sums1[4:]], axis=0)
        norms = norms + move(norms, by_part)
        norms_got = move(norms, by_chip[0])
        late, at, ff = step5_call(
            order, place, (late, late_got), (norms, norms_got), (at, at_got), ff, ff_far
        )
        late_got = move(late, by_chip[1])
        at = add_more(at)
        at_far = move(at, by_chip[0])
        ff_far = move(ff, by_chip[0])
        late, at, ff = step6_call(order, place, (late, late_got), at, at_far, ff, ff_far)
        late_got = move(late, by_chip[2])
        at_far = move(at, by_core)
        ff_far = move(ff, by_core)
        up_grad, down_grad = finish_mlp_call(order, place, ff, ff_far)
        late, mixed, tokens_grad = step7_call(order, (late, late_got), mixed, tokens_grad)
        late = add_more(late)
        query_grad, key_grad, value_grad, out_grad, norms = finish_attention_call(
            order, place, at[0], at_far[0], late, move(late, by_core)
        )
        return (
            mixed,
            tokens_grad,
            norms[0],
            norms[1],
            query_grad,
            key_grad,
            value_grad,
            out_grad,
            norms[2],
            norms[3],
            up_grad,
            down_grad,
        )

    return body


def solution(mesh):
    in_specs = (
        P(("dp", "tensor"), None),
        P("dp", None),
        P("dp", None),
        P(),
        P(),
        P(None, "tensor"),
        P(None, "tensor"),
        P(None, "tensor"),
        P("tensor", None),
        P(),
        P(),
        P(None, "tensor"),
        P("tensor", None),
        P(("dp", "tensor"), None),
    )
    out_specs = (
        P(("dp", "tensor"), None),
        P(("dp", "tensor"), None),
        P(),
        P(),
        P(None, "tensor"),
        P(None, "tensor"),
        P(None, "tensor"),
        P("tensor", None),
        P(),
        P(),
        P(None, "tensor"),
        P("tensor", None),
    )
    body = make_body(mesh.shape["dp"], mesh.shape["tensor"])
    return jax.shard_map(body, mesh=mesh, in_specs=in_specs, out_specs=out_specs, check_vma=False)
```

time: 413 us -> 333 us (0.81)
  the two profiles are of different devices: /device:TPU:0 before, /device:TPU:1 now
where the time goes in v2:
time: 333 us; the launch traced here: 328 us
  Pallas kernels  186 us (56%)
  starting transfers between devices  70.8 us (21%)
  waiting for transfers between devices  47.6 us (14%)
  local copies, waits for them, and re-layouts  21.7 us (7%)
    pallas_call x29, Pallas kernels, run(): pl.pallas_call(body, out_shape=out_shape, in_specs=in_specs, compiler_par...  186 us
    ppermute x46, starting transfers between devices, move(): return lax.ppermute(value, axes, how)  70.8 us
    ppermute x46, waiting for transfers between devices, move(): return lax.ppermute(value, axes, how)  47.6 us
    unnamed x58, local copies, waits for them, and re-layouts  13.8 us
  transfers between devices with their start and end apart: 46, of which 10 were waited for; matrix products, arithmetic and copies ran while one was open for 2% of the time, Pallas kernels for 48%

profile of v2, /device:TPU:1, one launch (start us, length us, event | category | flops | bytes accessed | tf_op | source)
XLA Modules:
  0.0 328.1 jit_solution(10971641057817959276)
XLA Ops:
  1.5 4.5 %collective-permute-start = (bf16[512,768]{1,0:T(8,128)(2,1)}, bf16[512,768]{1,0:T(8,128)(2,1)S(1)}, u32[]{:S(2)}, u32[]{:S(2)}) collective-permute-start(bf16[512,768]{1,0:T(8,128)(2,1)} %param.14), channel_id=1, source_target_pairs={{0,0},{1,2},{2,1},{3,3},{4,4},{5,6},{6,5},{7,7},{8,8},{9,10},{10,9... | collective-permute-start | bytes 2359304 | tf_op jit(solution)/shard_map/ppermute | solution.py:1141
  6.7 3.1 shard_map.229
  9.8 2.5 collective-permute-start.2
  14.1 3.3 %collective-permute-done.refs_0_ = bf16[512,768]{1,0:T(8,128)(2,1)S(1)} collective-permute-done((bf16[512,768]{1,0:T(8,128)(2,1)}, bf16[512,768]{1,0:T(8,128)(2,1)S(1)}, u32[]{:S(2)}, u32[]{:S(2)}) %collective-permute-start) | collective-permute-done | bytes 786464 | tf_op jit(solution)/shard_map/ppermute | solution.py:1141
  18.3 2.6 shard_map.230.refs_5_.refs_1_
  20.9 5.1 %shard_map.231 = (bf16[192,768]{1,0:T(8,128)(2,1)}, bf16[768,768]{1,0:T(8,128)(2,1)}, bf16[384,768]{1,0:T(8,128)(2,1)}, bf16[768,768]{1,0:T(8,128)(2,1)}, bf16[3...) custom-call(s32[5]{0:T(128)} %stack.35.refs_0_, bf16[384,768]{1,0:T(8,128)(2,1)} %refs_1_.3, bf16[768,1536]{1,0:T(8,128)(2,1)} %refs_2_.3, ...), custom_call_target="tpu_custom_call" | custom-call | flops 115000000512 | tf_op jit(solution)/shard_map/pallas_call | solution.py:60
  26.0 2.5 collective-permute-start.7
  28.5 1.4 collective-permute-start.8
  30.0 2.4 collective-permute-start.11
  32.4 6.6 %shard_map.232 = (bf16[1024,768]{1,0:T(8,128)(2,1)}, f32[1024,1024]{1,0:T(8,128)}, bf16[128,1024]{1,0:T(8,128)(2,1)}, bf16[768,128]{1,0:T(8,128)(2,1)}) custom-call(s32[5]{0:T(128)} %stack.35.refs_0_, bf16[512,768]{1,0:T(8,128)(2,1)} %shard_map.230.refs_5_.refs_1_, bf16[512,768]{1,0:T(8,128)(2,1)} %copy-done.16, ...), custom_call_target="tpu_custom_call" | custom-call | flops 149500002304 | tf_op jit(solution)/shard_map/pallas_call | solution.py:60
  38.9 1.5 collective-permute-start.5
  40.5 9.2 %shard_map.233 = (bf16[576,1024]{1,0:T(8,128)(2,1)}, bf16[192,1024]{1,0:T(8,128)(2,1)}, f32[3,1,1024]{2,1,0:T(1,128)}) custom-call(bf16[1024,768]{1,0:T(8,128)(2,1)} %get-tuple-element.103.refs_0_.refs_1_.refs_5_, bf16[768,576]{1,0:T(8,128)(2,1)} %get-tuple-element.104.refs_1_.refs_5_, ...), custom_call_target="tpu_custom_call" | custom-call | flops 213900001280 | tf_op jit(solution)/shard_map/pallas_call | solution.py:60
  49.7 9.4 %shard_map.235 = (bf16[576,1024]{1,0:T(8,128)(2,1)}, bf16[192,1024]{1,0:T(8,128)(2,1)}, f32[3,1,1024]{2,1,0:T(1,128)}, bf16[768,576]{1,0:T(8,128)(2,1)}) custom-call(s32[5]{0:T(128)} %stack.35.refs_0_, bf16[1024,768]{1,0:T(8,128)(2,1)} %get-tuple-element.103.refs_0_.refs_1_.refs_5_, bf16[384,576]{1,0:T(8,128)(2,1)} %shard_map.234.refs_2_, ...), custom_call_target="tpu_custom_call" | custom-call | flops 213900001280 | tf_op jit(solution)/shard_map/pallas_call | solution.py:60
  59.2 2.4 collective-permute-done.8.refs_5_.refs_0_
  61.6 3.5 %shard_map.236 = (f32[512,768]{1,0:T(8,128)}, bf16[512,768]{1,0:T(8,128)(2,1)}) custom-call(s32[5]{0:T(128)} %stack.35.refs_0_, bf16[192,1024]{1,0:T(8,128)(2,1)} %get-tuple-element.107.refs_1_.refs_4_, bf16[192,1024]{1,0:T(8,128)(2,1)} %get-tuple-element.111.refs_2_.refs_4_, bf16[192,768]{1,0:T(8,128)(2,1)} %get-tuple-element.112.refs_3_, ...), custom_call_target="tpu_custom_call" | custom-call | flops 80499998720 | tf_op jit(solution)/shard_map/pallas_call | solution.py:60
  65.0 2.9 collective-permute-start.9
  71.0 4.2 %shard_map.237 = (f32[512,768]{1,0:T(8,128)}, bf16[512,768]{1,0:T(8,128)(2,1)}) custom-call(bf16[512,768]{1,0:T(8,128)(2,1)} %copy-done.11, f32[512,768]{1,0:T(8,128)} %get-tuple-element.115.refs_1_, bf16[512,768]{1,0:T(8,128)(2,1)} %copy-done.19, f32[1,768]{1,0:T(1,128)} %broadcast_in_dim.30.refs_3_.refs_4_, f32[1,768]{1,0:T(1,128)} %broadcast_in_dim.31.refs_4_, ...), custom_call_target="tpu_custom_call" | custom-call | flops 92000002048 | tf_op jit(solution)/shard_map/pallas_call | solution.py:60
  75.6 1.3 collective-permute-start.13
  78.6 14.5 %shard_map.241 = (f32[512,768]{1,0:T(8,128)}, f32[512,768]{1,0:T(8,128)}, f32[512,768]{1,0:T(8,128)}, f32[512,768]{1,0:T(8,128)}, bf16[768,768]{1,0:T(8,128)(2,1)}, /*index=5*/bf16[768,768]{1,0:T(8,128)(2,1)}) custom-call(bf16[512,768]{1,0:T(8,128)(2,1)} %copy-done.15, bf16[512,768]{1,0:T(8,128)(2,1)} %get-tuple-element.118.refs_1_.refs_6_.refs_2_, ...), custom_call_target="tpu_custom_call" | custom-call | flops 335800008704 | tf_op jit(solution)/shard_map/pallas_call | solution.py:60
  93.1 16.8 %shard_map.242 = (bf16[512,768]{1,0:T(8,128)(2,1)}, f32[512,768]{1,0:T(8,128)}, bf16[512,768]{1,0:T(8,128)(2,1)}, f32[512,768]{1,0:T(8,128)}, bf16[768,768]{1,0:...) custom-call(s32[5]{0:T(128)} %stack.35.refs_0_, bf16[512,768]{1,0:T(8,128)(2,1)} %copy-done.15, ...), custom_call_target="tpu_custom_call" | custom-call | flops 335800008704 | tf_op jit(solution)/shard_map/pallas_call | solution.py:60
  110.5 1.3 collective-permute-start.18
  111.8 2.5 collective-permute-start.19
  115.1 5.0 %shard_map.243 = (f32[512,768]{1,0:T(8,128)}, bf16[512,768]{1,0:T(8,128)(2,1)}, f32[8,768]{1,0:T(8,128)}) custom-call(f32[512,768]{1,0:T(8,128)} %get-tuple-element.117.refs_0_, f32[512,768]{1,0:T(8,128)} %get-tuple-element.127.refs_1_, bf16[512,768]{1,0:T(8,128)(2,1)} %copy-done.18, bf16[512,768]{1,0:T(8,128)(2,1)} %shard_map.238.refs_3_.refs_4_, ...), custom_call_target="tpu_custom_call" | custom-call | flops 115000000512 | tf_op jit(solution)/shard_map/pallas_call | solution.py:60
  121.9 2.9 shard_map.244.refs_8_
  124.8 1.3 slice.22
  127.0 15.6 %shard_map.245 = (bf16[576,1024]{1,0:T(8,128)(2,1)}, bf16[192,768]{1,0:T(8,128)(2,1)}, f32[1024,1024]{1,0:T(8,128)}) custom-call(s32[5]{0:T(128)} %stack.35.refs_0_, bf16[512,768]{1,0:T(8,128)(2,1)} %get-tuple-element.130.refs_1_, bf16[512,768]{1,0:T(8,128)(2,1)} %copy-done.12, bf16[192,768]{1,0:T(8,128)(2,1)} %collective-permute-done.7.refs_4_.refs_3_, ...), custom_call_target="tpu_custom_call" | custom-call | flops 379500003328 | tf_op jit(solution)/shard_map/pallas_call | solution.py:60
  142.6 7.2 %shard_map.246 = (f32[1024,768]{1,0:T(8,128)}, bf16[256,768]{1,0:T(8,128)(2,1)}, bf16[256,768]{1,0:T(8,128)(2,1)}, bf16[256,768]{1,0:T(8,128)(2,1)}) custom-call(s32[5]{0:T(128)} %stack.35.refs_0_, bf16[1024,768]{1,0:T(8,128)(2,1)} %get-tuple-element.103.refs_0_.refs_1_.refs_5_, bf16[576,1024]{1,0:T(8,128)(2,1)} %get-tuple-element.140.refs_2_, ...), custom_call_target="tpu_custom_call" | custom-call | flops 138000007168 | tf_op jit(solution)/shard_map/pallas_call | solution.py:60
  149.8 1.3 collective-permute-start.20
  151.3 4.0 %shard_map.247 = (bf16[384,768]{1,0:T(8,128)(2,1)}, bf16[384,768]{1,0:T(8,128)(2,1)}, bf16[1,384,768]{2,1,0:T(8,128)(2,1)}, bf16[1,384,768]{2,1,0:T(8,128)(2,1)}) custom-call(s32[5]{0:T(128)} %stack.35.refs_0_, bf16[2,384,768]{2,1,0:T(8,128)(2,1)} %get-tuple-element.129.refs_5_.refs_1_, bf16[2,384,768]{2,1,0:T(8,128)(2,1)} %collective-permute-done.18.refs_2_, ...), custom_call_target="tpu_custom_call" | custom-call | flops 69000003584 | tf_op jit(solution)/shard_map/pallas_call | solution.py:60
  156.7 14.1 %shard_map.248 = (bf16[384,1024]{1,0:T(8,128)(2,1)}, bf16[192,768]{1,0:T(8,128)(2,1)}, f32[1024,1024]{1,0:T(8,128)}) custom-call(s32[5]{0:T(128)} %stack.35.refs_0_, bf16[512,768]{1,0:T(8,128)(2,1)} %get-tuple-element.130.refs_1_, bf16[512,768]{1,0:T(8,128)(2,1)} %copy-done.12, bf16[192,768]{1,0:T(8,128)(2,1)} %get-tuple-element.112.refs_3_, ...), custom_call_target="tpu_custom_call" | custom-call | flops 253000007680 | tf_op jit(solution)/shard_map/pallas_call | solution.py:60
  170.8 3.4 %shard_map.249 = (bf16[256,768]{1,0:T(8,128)(2,1)}, bf16[256,768]{1,0:T(8,128)(2,1)}) custom-call(s32[5]{0:T(128)} %stack.35.refs_0_, bf16[1024,768]{1,0:T(8,128)(2,1)} %get-tuple-element.103.refs_0_.refs_1_.refs_5_, bf16[384,1024]{1,0:T(8,128)(2,1)} %get-tuple-element.150.refs_2_.refs_3_, bf16[192,768]{1,0:T(8,128)(2,1)} %get-tuple-element.151.refs_3_.refs_8_, ...), custom_call_target="tpu_custom_call" | custom-call | flops 69000003584 | tf_op jit(solution)/shard_map/pallas_call | solution.py:60
  174.2 1.3 collective-permute-start.24
  175.5 3.6 %shard_map.250 = (bf16[256,768]{1,0:T(8,128)(2,1)}, bf16[2,192,768]{2,1,0:T(8,128)(2,1)}, bf16[2,192,768]{2,1,0:T(8,128)(2,1)}) custom-call(s32[5]{0:T(128)} %stack.35.refs_0_, bf16[256,768]{1,0:T(8,128)(2,1)} %get-tuple-element.145.refs_1_, bf16[256,768]{1,0:T(8,128)(2,1)} %collective-permute-done.20.refs_2_, ...), custom_call_target="tpu_custom_call" | custom-call | flops 69000003584 | tf_op jit(solution)/shard_map/pallas_call | solution.py:60
  179.4 2.3 collective-permute-start.26
  181.7 8.6 %shard_map.251 = (bf16[192,1024]{1,0:T(8,128)(2,1)}, bf16[1024,1024]{1,0:T(8,128)(2,1)}) custom-call(s32[5]{0:T(128)} %stack.35.refs_0_, bf16[512,768]{1,0:T(8,128)(2,1)} %get-tuple-element.130.refs_1_, bf16[512,768]{1,0:T(8,128)(2,1)} %copy-done.12, bf16[192,768]{1,0:T(8,128)(2,1)} %get-tuple-element.112.refs_3_, ...), custom_call_target="tpu_custom_call" | custom-call | flops 126500003840 | tf_op jit(solution)/shard_map/pallas_call | solution.py:60
  190.3 3.3 collective-permute-start.23
  193.6 2.0 collective-permute-done.26.refs_4_
  196.5 2.7 shard_map.252
  200.2 2.1 collective-permute-start.30
  202.3 1.3 copy-done.9
  203.6 7.8 %shard_map.253 = (bf16[128,1024]{1,0:T(8,128)(2,1)}, bf16[128,768]{1,0:T(8,128)(2,1)}) custom-call(s32[5]{0:T(128)} %stack.35.refs_0_, bf16[1024,1024]{1,0:T(8,128)(2,1)} %get-tuple-element.155.refs_5_.refs_1_, bf16[1024,1024]{1,0:T(8,128)(2,1)} %copy-done.9, bf16[128,1024]{1,0:T(8,128)(2,1)} %get-tuple-element.156.refs_3_, ...), custom_call_target="tpu_custom_call" | custom-call | flops 193199996928 | tf_op jit(solution)/shard_map/pallas_call | solution.py:60
  211.4 1.3 collective-permute-start.28
  212.7 7.2 %shard_map.254 = (f32[512,768]{1,0:T(8,128)}, bf16[512,768]{1,0:T(8,128)(2,1)}, f32[256,768]{1,0:T(8,128)}) custom-call(s32[5]{0:T(128)} %stack.35.refs_0_, bf16[1024,768]{1,0:T(8,128)(2,1)} %get-tuple-element.103.refs_0_.refs_1_.refs_5_, bf16[192,1024]{1,0:T(8,128)(2,1)} %get-tuple-element.154.refs_2_, ...), custom_call_target="tpu_custom_call" | custom-call | flops 160999997440 | tf_op jit(solution)/shard_map/pallas_call | solution.py:60
  219.9 1.7 collective-permute-start.32
  221.6 3.2 shard_map.255
  225.1 1.7 collective-permute-start.36
  227.7 4.7 %shard_map.256 = (bf16[512,768]{1,0:T(8,128)(2,1)}, f32[8,768]{1,0:T(8,128)}) custom-call(bf16[512,768]{1,0:T(8,128)(2,1)} %copy-done.11, f32[512,768]{1,0:T(8,128)} %get-tuple-element.167.refs_1_, bf16[512,768]{1,0:T(8,128)(2,1)} %copy-done.14, f32[512,768]{1,0:T(8,128)} %get-tuple-element.169.refs_3_, f32[1,768]{1,0:T(1,128)} %broadcast_in_dim.28.refs_1_.refs_4_, ...), custom_call_target="tpu_custom_call" | custom-call | flops 105799999488 | tf_op jit(solution)/shard_map/pallas_call | solution.py:60
  233.9 2.7 collective-permute-start.33
  236.6 1.5 collective-permute-done.33
  239.3 9.6 %collective-permute-done.36.refs_8_ = bf16[2,192,768]{2,1,0:T(8,128)(2,1)S(1)} collective-permute-done((bf16[2,192,768]{2,1,0:T(8,128)(2,1)}, bf16[2,192,768]{2,1,0:T(8,128)(2,1)S(1)}, u32[]{:S(2)}, u32[]{:S(2)}) %collective-permute-start.36) | collective-permute-done | bytes 589856 | tf_op jit(solution)/shard_map/ppermute | solution.py:1141
  250.2 3.1 shard_map.257
  253.4 2.9 collective-permute-start.37
  256.3 25.5 %collective-permute-done.38.refs_4_ = bf16[1,256,768]{2,1,0:T(8,128)(2,1)S(1)} collective-permute-done((bf16[1,256,768]{2,1,0:T(8,128)(2,1)}, bf16[1,256,768]{2,1,0:T(8,128)(2,1)S(1)}, u32[]{:S(2)}, u32[]{:S(2)}) %collective-permute-start.38) | collective-permute-done | bytes 393248 | tf_op jit(solution)/shard_map/ppermute | solution.py:1141
  283.7 4.1 %shard_map.258 = (bf16[272,768]{1,0:T(8,128)(2,1)}, bf16[1,512,768]{2,1,0:T(8,128)(2,1)}, bf16[2,768,768]{2,1,0:T(8,128)(2,1)}) custom-call(s32[5]{0:T(128)} %stack.35.refs_0_, bf16[272,768]{1,0:T(8,128)(2,1)} %get-tuple-element.173.refs_1_, bf16[272,768]{1,0:T(8,128)(2,1)} %copy-done.22, bf16[1,256,768]{2,1,0:T(8,128)(2,1)} %get-tuple-element.174.refs_3_, ...), custom_call_target="tpu_custom_call" | custom-call | flops 80499998720 | tf_op jit(solution)/shard_map/pallas_call | solution.py:60
  287.8 6.3 %collective-permute-start.41 = (bf16[512,768]{1,0:T(8,128)(2,1)}, bf16[512,768]{1,0:T(8,128)(2,1)}, u32[]{:S(2)}, u32[]{:S(2)}) collective-permute-start(bf16[512,768]{1,0:T(8,128)(2,1)} %shard_map.244.refs_8_), channel_id=1, source_target_pairs={{0,0},{1,2},{2,1},{3,3},{4,4},{5,6},{6,5},{7,7},{8,8},{9,10},{10,9... | collective-permute-start | bytes 2359304 | tf_op jit(solution)/shard_map/ppermute | solution.py:1141
  294.1 1.9 collective-permute-start.42
  297.2 7.5 %collective-permute-start.44 = (bf16[1,512,768]{2,1,0:T(8,128)(2,1)}, bf16[1,512,768]{2,1,0:T(8,128)(2,1)}, u32[]{:S(2)}, u32[]{:S(2)}) collective-permute-start(bf16[1,512,768]{2,1,0:T(8,128)(2,1)} %get-tuple-element.182), channel_id=1, source_target_pairs={{0,2},{1,3},{2,0},{3,1},{4,6},{5,7},{6,4},{7,5},{8,10},{9,11},{10,... | collective-permute-start | bytes 2359304 | tf_op jit(solution)/shard_map/ppermute | solution.py:1141
  304.8 1.4 copy-done.8
  306.2 6.7 %shard_map.259 = (f32[768,1536]{1,0:T(8,128)}, f32[1536,768]{1,0:T(8,128)}) custom-call(s32[5]{0:T(128)} %stack.35.refs_0_, bf16[2,768,768]{2,1,0:T(8,128)(2,1)} %get-tuple-element.178.refs_1_.refs_3_, bf16[2,768,768]{2,1,0:T(8,128)(2,1)} %copy-done.8, bf16[2,768,768]{2,1,0:T(8,128)(2,1)} %get-tuple-element.178.refs_1_.refs_3_), custom_call_target="tpu_custom_call" | custom-call | flops 156399992832 | tf_op jit(solution)/shard_map/pallas_call | solution.py:60
  312.9 2.9 shard_map.260
  315.9 3.8 %collective-permute-start.45 = (bf16[272,768]{1,0:T(8,128)(2,1)}, bf16[272,768]{1,0:T(8,128)(2,1)S(1)}, u32[]{:S(2)}, u32[]{:S(2)}) collective-permute-start(bf16[272,768]{1,0:T(8,128)(2,1)} %get-tuple-element.183.refs_3_), channel_id=1, source_target_pairs={{0,2},{1,3},{2,0},{3,1},{4,6},{5,7},{6,4},{7,5},{8,10},{9,11},{10,... | collective-permute-start | bytes 1253384 | tf_op jit(solution)/shard_map/ppermute | solution.py:1141
  319.7 1.6 collective-permute-done.45.refs_4_
  322.0 4.4 %shard_map.261 = (f32[768,384]{1,0:T(8,128)}, f32[768,384]{1,0:T(8,128)}, f32[768,384]{1,0:T(8,128)}, f32[384,768]{1,0:T(8,128)}, f32[8,768]{1,0:T(8,128)}) custom-call(s32[5]{0:T(128)} %stack.35.refs_0_, bf16[512,768]{1,0:T(8,128)(2,1)} %bitcast.12, bf16[512,768]{1,0:T(8,128)(2,1)} %bitcast.11.refs_2_, bf16[272,768]{1,0:T(8,128)(2,1)} %get-tuple-element.183.refs_3_, ...), custom_call_target="tpu_custom_call" | custom-call | flops 103499997184 | tf_op jit(solution)/shard_map/pallas_call | solution.py:60
  326.4 1.5 slice_reduce_fusion
  (133 shorter events, 26.4 us)
Async XLA Ops:
  1.4 12.1 %collective-permute-start.3 = (s32[2,1024]{1,0:T(2,128)S(1)}, s32[2,1024]{1,0:T(2,128)S(1)}, u32[]{:S(2)}, u32[]{:S(2)}) collective-permute-start(s32[2,1024]{1,0:T(2,128)S(1)} %pad_add_fusion), channel_id=1, source_target_pairs={{0,2},{1,3},{2,0},{3,1},{4,6},{5,7},{6,4},{7,5},{8,10},{9,11},{10,... | collective-permute-start | bytes 24584 | tf_op jit(solution)/shard_map/ppermute | solution.py:1141
  1.5 15.9 %collective-permute-start = (bf16[512,768]{1,0:T(8,128)(2,1)}, bf16[512,768]{1,0:T(8,128)(2,1)S(1)}, u32[]{:S(2)}, u32[]{:S(2)}) collective-permute-start(bf16[512,768]{1,0:T(8,128)(2,1)} %param.14), channel_id=1, source_target_pairs={{0,0},{1,2},{2,1},{3,3},{4,4},{5,6},{6,5},{7,7},{8,8},{9,10},{10,9... | collective-permute-start | bytes 2359304 | tf_op jit(solution)/shard_map/ppermute | solution.py:1141
  6.7 5.6 %copy-start.4 = (f32[768]{0:T(1024)S(1)}, f32[768]{0:T(1024)}, u32[]{:S(2)}) copy-start(f32[768]{0:T(1024)} %param.17) | copy-start | bytes 9220
  6.7 6.2 %copy-start.5 = (f32[768]{0:T(1024)S(1)}, f32[768]{0:T(1024)}, u32[]{:S(2)}) copy-start(f32[768]{0:T(1024)} %param.18) | copy-start | bytes 9220
  6.7 6.8 %copy-start.2 = (s32[1,1024]{1,0:T(1,128)S(1)}, s32[1,1024]{1,0:T(1,128)}, u32[]{:S(2)}) copy-start(s32[1,1024]{1,0:T(1,128)} %param.16) | copy-start | bytes 12292
  6.7 6.8 %copy-start.3 = (s32[1,1024]{1,0:T(1,128)S(1)}, s32[1,1024]{1,0:T(1,128)}, u32[]{:S(2)}) copy-start(s32[1,1024]{1,0:T(1,128)} %param.15) | copy-start | bytes 12292
  9.8 18.7 %collective-permute-start.2 = (bf16[768,128]{1,0:T(8,128)(2,1)}, bf16[768,128]{1,0:T(8,128)(2,1)}, u32[]{:S(2)}, u32[]{:S(2)}) collective-permute-start(bf16[768,128]{1,0:T(8,128)(2,1)} %get-tuple-element.101.refs_3_), channel_id=1, source_target_pairs={{0,1},{2,3},{4,5},{6,7},{8,9},{10,11},{12,13},{14,15},{16,17},{18,... | collective-permute-start | bytes 589832 | tf_op jit(solution)/shard_map/ppermute | solution.py:1141
  12.3 26.6 %collective-permute-start.4 = (bf16[384,576]{1,0:T(8,128)(2,1)}, bf16[384,576]{1,0:T(8,128)(2,1)}, u32[]{:S(2)}, u32[]{:S(2)}) collective-permute-start(bf16[384,576]{1,0:T(8,128)(2,1)} %get-tuple-element.108), channel_id=1, source_target_pairs={{0,1},{1,0},{2,3},{3,2},{4,5},{5,4},{6,7},{7,6},{8,9},{9,8},{10,11... | collective-permute-start | bytes 1327112 | tf_op jit(solution)/shard_map/ppermute | solution.py:1141
  20.9 9.1 %collective-permute-start.1 = (bf16[512,768]{1,0:T(8,128)(2,1)}, bf16[512,768]{1,0:T(8,128)(2,1)S(1)}, u32[]{:S(2)}, u32[]{:S(2)}) collective-permute-start(bf16[512,768]{1,0:T(8,128)(2,1)} %shard_map.230.refs_5_.refs_1_), channel_id=1, source_target_pairs={{0,2},{1,3},{2,0},{3,1},{4,6},{5,7},{6,4},{7,5},{8,10},{9,11},{10,... | collective-permute-start | bytes 2359304 | tf_op jit(solution)/shard_map/ppermute | solution.py:1141
  26.0 33.2 %collective-permute-start.7 = (bf16[192,768]{1,0:T(8,128)(2,1)}, bf16[192,768]{1,0:T(8,128)(2,1)}, u32[]{:S(2)}, u32[]{:S(2)}) collective-permute-start(bf16[192,768]{1,0:T(8,128)(2,1)} %get-tuple-element.112.refs_3_), channel_id=1, source_target_pairs={{0,1},{1,0},{2,3},{3,2},{4,5},{5,4},{6,7},{7,6},{8,9},{9,8},{10,11... | collective-permute-start | bytes 884744 | tf_op jit(solution)/shard_map/ppermute | solution.py:1141
  28.5 21.3 %collective-permute-start.6 = (bf16[384,768]{1,0:T(8,128)(2,1)}, bf16[384,768]{1,0:T(8,128)(2,1)}, u32[]{:S(2)}, u32[]{:S(2)}) collective-permute-start(bf16[384,768]{1,0:T(8,128)(2,1)} %get-tuple-element.109), channel_id=1, source_target_pairs={{0,1},{1,0},{2,3},{3,2},{4,5},{5,4},{6,7},{7,6},{8,9},{9,8},{10,11... | collective-permute-start | bytes 1769480 | tf_op jit(solution)/shard_map/ppermute | solution.py:1141
  28.5 33.0 %collective-permute-start.8 = (bf16[384,768]{1,0:T(8,128)(2,1)}, bf16[384,768]{1,0:T(8,128)(2,1)}, u32[]{:S(2)}, u32[]{:S(2)}) collective-permute-start(bf16[384,768]{1,0:T(8,128)(2,1)} %get-tuple-element.113), channel_id=1, source_target_pairs={{0,1},{1,0},{2,3},{3,2},{4,5},{5,4},{6,7},{7,6},{8,9},{9,8},{10,11... | collective-permute-start | bytes 1769480 | tf_op jit(solution)/shard_map/ppermute | solution.py:1141
  30.0 2.4 copy-start.16
  30.0 40.0 %collective-permute-start.11 = (bf16[512,768]{1,0:T(8,128)(2,1)}, bf16[512,768]{1,0:T(8,128)(2,1)}, u32[]{:S(2)}, u32[]{:S(2)}) collective-permute-start(bf16[512,768]{1,0:T(8,128)(2,1)} %get-tuple-element.102.refs_6_), channel_id=1, source_target_pairs={{0,0},{1,2},{2,1},{3,3},{4,4},{5,6},{6,5},{7,7},{8,8},{9,10},{10,9... | collective-permute-start | bytes 2359304 | tf_op jit(solution)/shard_map/ppermute | solution.py:1141
  38.9 10.8 %collective-permute-start.5 = (bf16[384,576]{1,0:T(8,128)(2,1)}, bf16[384,576]{1,0:T(8,128)(2,1)}, u32[]{:S(2)}, u32[]{:S(2)}) collective-permute-start(bf16[384,576]{1,0:T(8,128)(2,1)} %shard_map.234.refs_2_), channel_id=1, source_target_pairs={{0,4},{1,5},{2,10},{3,11},{4,0},{5,1},{6,14},{7,15},{8,12},{9,13},... | collective-permute-start | bytes 1327112 | tf_op jit(solution)/shard_map/ppermute | solution.py:1141
  61.6 6.4 %copy-start.6 = (f32[768]{0:T(1024)S(1)}, f32[768]{0:T(1024)}, u32[]{:S(2)}) copy-start(f32[768]{0:T(1024)} %param.23) | copy-start | bytes 9220
  61.6 7.0 %copy-start.7 = (f32[768]{0:T(1024)S(1)}, f32[768]{0:T(1024)}, u32[]{:S(2)}) copy-start(f32[768]{0:T(1024)} %param.24) | copy-start | bytes 9220
  65.0 5.0 %collective-permute-start.9 = (bf16[512,768]{1,0:T(8,128)(2,1)}, bf16[512,768]{1,0:T(8,128)(2,1)S(1)}, u32[]{:S(2)}, u32[]{:S(2)}) collective-permute-start(bf16[512,768]{1,0:T(8,128)(2,1)} %get-tuple-element.116.refs_5_.refs_1_), channel_id=1, source_target_pairs={{0,2},{1,3},{2,0},{3,1},{4,6},{5,7},{6,4},{7,5},{8,10},{9,11},{10,... | collective-permute-start | bytes 2359304 | tf_op jit(solution)/shard_map/ppermute | solution.py:1141
  70.0 7.0 %collective-permute-start.12 = (bf16[512,768]{1,0:T(8,128)(2,1)}, bf16[512,768]{1,0:T(8,128)(2,1)S(1)}, u32[]{:S(2)}, u32[]{:S(2)}) collective-permute-start(bf16[512,768]{1,0:T(8,128)(2,1)} %shard_map.238.refs_3_.refs_4_), channel_id=1, source_target_pairs={{0,2},{1,3},{2,0},{3,1},{4,6},{5,7},{6,4},{7,5},{8,10},{9,11},{10,... | collective-permute-start | bytes 2359304 | tf_op jit(solution)/shard_map/ppermute | solution.py:1141
  70.1 0.9 copy-start.19
  75.1 2.6 collective-permute-start.10
  75.6 17.5 %collective-permute-start.13 = (bf16[384,768]{1,0:T(8,128)(2,1)}, bf16[384,768]{1,0:T(8,128)(2,1)}, u32[]{:S(2)}, u32[]{:S(2)}) collective-permute-start(bf16[384,768]{1,0:T(8,128)(2,1)} %shard_map.239.refs_5_), channel_id=1, source_target_pairs={{0,4},{1,5},{2,10},{3,11},{4,0},{5,1},{6,14},{7,15},{8,12},{9,13},... | collective-permute-start | bytes 1769480 | tf_op jit(solution)/shard_map/ppermute | solution.py:1141
  76.9 16.2 %collective-permute-start.14 = (bf16[384,768]{1,0:T(8,128)(2,1)}, bf16[384,768]{1,0:T(8,128)(2,1)}, u32[]{:S(2)}, u32[]{:S(2)}) collective-permute-start(bf16[384,768]{1,0:T(8,128)(2,1)} %shard_map.240.refs_7_), channel_id=1, source_target_pairs={{0,4},{1,5},{2,10},{3,11},{4,0},{5,1},{6,14},{7,15},{8,12},{9,13},... | collective-permute-start | bytes 1769480 | tf_op jit(solution)/shard_map/ppermute | solution.py:1141
  77.0 0.9 copy-start.13
  109.9 4.3 %collective-permute-start.15 = (bf16[512,768]{1,0:T(8,128)(2,1)}, bf16[512,768]{1,0:T(8,128)(2,1)S(1)}, u32[]{:S(2)}, u32[]{:S(2)}) collective-permute-start(bf16[512,768]{1,0:T(8,128)(2,1)} %get-tuple-element.128), channel_id=1, source_target_pairs={{0,2},{1,3},{2,0},{3,1},{4,6},{5,7},{6,4},{7,5},{8,10},{9,11},{10,... | collective-permute-start | bytes 2359304 | tf_op jit(solution)/shard_map/ppermute | solution.py:1141
  110.4 10.6 %collective-permute-start.17 = (bf16[512,768]{1,0:T(8,128)(2,1)}, bf16[512,768]{1,0:T(8,128)(2,1)S(1)}, u32[]{:S(2)}, u32[]{:S(2)}) collective-permute-start(bf16[512,768]{1,0:T(8,128)(2,1)} %get-tuple-element.134), channel_id=1, source_target_pairs={{0,2},{1,3},{2,0},{3,1},{4,6},{5,7},{6,4},{7,5},{8,10},{9,11},{10,... | collective-permute-start | bytes 2359304 | tf_op jit(solution)/shard_map/ppermute | solution.py:1141
  110.5 40.8 %collective-permute-start.18 = (bf16[2,384,768]{2,1,0:T(8,128)(2,1)}, bf16[2,384,768]{2,1,0:T(8,128)(2,1)}, u32[]{:S(2)}, u32[]{:S(2)}) collective-permute-start(bf16[2,384,768]{2,1,0:T(8,128)(2,1)} %get-tuple-element.137), channel_id=1, source_target_pairs={{0,4},{1,5},{2,10},{3,11},{4,0},{5,1},{6,14},{7,15},{8,12},{9,13},... | collective-permute-start | bytes 3538952 | tf_op jit(solution)/shard_map/ppermute | solution.py:1141
  111.8 39.5 %collective-permute-start.19 = (bf16[768,768]{1,0:T(8,128)(2,1)}, bf16[768,768]{1,0:T(8,128)(2,1)}, u32[]{:S(2)}, u32[]{:S(2)}) collective-permute-start(bf16[768,768]{1,0:T(8,128)(2,1)} %get-tuple-element.139), channel_id=1, source_target_pairs={{0,1},{1,0},{2,3},{3,2},{4,5},{5,4},{6,7},{7,6},{8,9},{9,8},{10,11... | collective-permute-start | bytes 3538952 | tf_op jit(solution)/shard_map/ppermute | solution.py:1141
  114.2 0.9 copy-start.18
  120.2 6.0 %collective-permute-start.16 = (bf16[512,768]{1,0:T(8,128)(2,1)}, bf16[512,768]{1,0:T(8,128)(2,1)S(1)}, u32[]{:S(2)}, u32[]{:S(2)}) collective-permute-start(bf16[512,768]{1,0:T(8,128)(2,1)} %get-tuple-element.130.refs_1_), channel_id=1, source_target_pairs={{0,2},{1,3},{2,0},{3,1},{4,6},{5,7},{6,4},{7,5},{8,10},{9,11},{10,... | collective-permute-start | bytes 2359304 | tf_op jit(solution)/shard_map/ppermute | solution.py:1141
  149.8 25.7 %collective-permute-start.20 = (bf16[256,768]{1,0:T(8,128)(2,1)}, bf16[256,768]{1,0:T(8,128)(2,1)}, u32[]{:S(2)}, u32[]{:S(2)}) collective-permute-start(bf16[256,768]{1,0:T(8,128)(2,1)} %get-tuple-element.146), channel_id=1, source_target_pairs={{0,4},{1,5},{2,10},{3,11},{4,0},{5,1},{6,14},{7,15},{8,12},{9,13},... | collective-permute-start | bytes 1179656 | tf_op jit(solution)/shard_map/ppermute | solution.py:1141
  151.1 70.6 %collective-permute-start.27 = (bf16[256,768]{1,0:T(8,128)(2,1)}, bf16[256,768]{1,0:T(8,128)(2,1)}, u32[]{:S(2)}, u32[]{:S(2)}) collective-permute-start(bf16[256,768]{1,0:T(8,128)(2,1)} %get-tuple-element.142.refs_5_), channel_id=1, source_target_pairs={{0,1},{1,0},{2,3},{3,2},{4,5},{5,4},{6,7},{7,6},{8,9},{9,8},{10,11... | collective-permute-start | bytes 1179656 | tf_op jit(solution)/shard_map/ppermute | solution.py:1141
  155.3 20.2 %collective-permute-start.22 = (bf16[384,768]{1,0:T(8,128)(2,1)}, bf16[384,768]{1,0:T(8,128)(2,1)}, u32[]{:S(2)}, u32[]{:S(2)}) collective-permute-start(bf16[384,768]{1,0:T(8,128)(2,1)} %get-tuple-element.149), channel_id=1, source_target_pairs={{0,1},{1,0},{2,3},{3,2},{4,5},{5,4},{6,7},{7,6},{8,9},{9,8},{10,11... | collective-permute-start | bytes 1769480 | tf_op jit(solution)/shard_map/ppermute | solution.py:1141
  156.6 18.9 %collective-permute-start.21 = (bf16[1,384,768]{2,1,0:T(8,128)(2,1)}, bf16[1,384,768]{2,1,0:T(8,128)(2,1)}, u32[]{:S(2)}, u32[]{:S(2)}) collective-permute-start(bf16[1,384,768]{2,1,0:T(8,128)(2,1)} %get-tuple-element.143.refs_9_), channel_id=1, source_target_pairs={{0,4},{1,5},{2,10},{3,11},{4,0},{5,1},{6,14},{7,15},{8,12},{9,13},... | collective-permute-start | bytes 1769480 | tf_op jit(solution)/shard_map/ppermute | solution.py:1141
  174.2 19.4 %collective-permute-start.24 = (bf16[256,768]{1,0:T(8,128)(2,1)}, bf16[256,768]{1,0:T(8,128)(2,1)}, u32[]{:S(2)}, u32[]{:S(2)}) collective-permute-start(bf16[256,768]{1,0:T(8,128)(2,1)} %get-tuple-element.157), channel_id=1, source_target_pairs={{0,4},{1,5},{2,10},{3,11},{4,0},{5,1},{6,14},{7,15},{8,12},{9,13},... | collective-permute-start | bytes 1179656 | tf_op jit(solution)/shard_map/ppermute | solution.py:1141
  179.1 14.4 %collective-permute-start.25 = (bf16[256,768]{1,0:T(8,128)(2,1)}, bf16[256,768]{1,0:T(8,128)(2,1)S(1)}, u32[]{:S(2)}, u32[]{:S(2)}) collective-permute-start(bf16[256,768]{1,0:T(8,128)(2,1)} %get-tuple-element.158), channel_id=1, source_target_pairs={{0,1},{1,0},{2,3},{3,2},{4,5},{5,4},{6,7},{7,6},{8,9},{9,8},{10,11... | collective-permute-start | bytes 1179656 | tf_op jit(solution)/shard_map/ppermute | solution.py:1141
  179.4 16.3 %collective-permute-start.26 = (bf16[2,192,768]{2,1,0:T(8,128)(2,1)}, bf16[2,192,768]{2,1,0:T(8,128)(2,1)S(1)}, u32[]{:S(2)}, u32[]{:S(2)}) collective-permute-start(bf16[2,192,768]{2,1,0:T(8,128)(2,1)} %get-tuple-element.153.refs_8_), channel_id=1, source_target_pairs={{0,8},{1,9},{2,18},{3,19},{4,12},{5,13},{6,22},{7,23},{8,0},{9,1},... | collective-permute-start | bytes 1769480 | tf_op jit(solution)/shard_map/ppermute | solution.py:1141
  190.3 12.0 %collective-permute-start.23 = (bf16[1024,1024]{1,0:T(8,128)(2,1)}, bf16[1024,1024]{1,0:T(8,128)(2,1)S(1)}, u32[]{:S(2)}, u32[]{:S(2)}) collective-permute-start(bf16[1024,1024]{1,0:T(8,128)(2,1)} %get-tuple-element.155.refs_5_.refs_1_), channel_id=1, source_target_pairs={{2,0},{3,1},{6,4},{7,5},{10,8},{11,9},{14,12},{15,13},{18,16},{19,... | collective-permute-start | bytes 6291464 | tf_op jit(solution)/shard_map/ppermute | solution.py:1141
  193.6 2.1 copy-start.26
  199.2 22.5 %collective-permute-start.29 = (bf16[1,256,768]{2,1,0:T(8,128)(2,1)}, bf16[1,256,768]{2,1,0:T(8,128)(2,1)}, u32[]{:S(2)}, u32[]{:S(2)}) collective-permute-start(bf16[1,256,768]{2,1,0:T(8,128)(2,1)} %get-tuple-element.165.refs_5_), channel_id=1, source_target_pairs={{0,8},{1,9},{2,18},{3,19},{4,12},{5,13},{6,22},{7,23},{8,0},{9,1},... | collective-permute-start | bytes 1179656 | tf_op jit(solution)/shard_map/ppermute | solution.py:1141
  200.2 21.5 %collective-permute-start.30 = (bf16[2,192,768]{2,1,0:T(8,128)(2,1)}, bf16[2,192,768]{2,1,0:T(8,128)(2,1)}, u32[]{:S(2)}, u32[]{:S(2)}) collective-permute-start(bf16[2,192,768]{2,1,0:T(8,128)(2,1)} %get-tuple-element.160.refs_6_.refs_7_), channel_id=1, source_target_pairs={{0,16},{1,17},{2,6},{3,7},{4,20},{5,21},{6,2},{7,3},{8,24},{9,25},... | collective-permute-start | bytes 1769480 | tf_op jit(solution)/shard_map/ppermute | solution.py:1141
  202.3 1.3 copy-start.9
  211.4 10.3 %collective-permute-start.28 = (bf16[128,768]{1,0:T(8,128)(2,1)}, bf16[128,768]{1,0:T(8,128)(2,1)}, u32[]{:S(2)}, u32[]{:S(2)}) collective-permute-start(bf16[128,768]{1,0:T(8,128)(2,1)} %get-tuple-element.163.refs_9_.refs_3_), channel_id=1, source_target_pairs={{1,0},{5,4},{9,8},{13,12},{17,16},{21,20},{25,24},{29,28}} | collective-permute-start | bytes 589832 | tf_op jit(solution)/shard_map/ppermute | solution.py:1141
  219.9 7.0 %collective-permute-start.32 = (bf16[512,768]{1,0:T(8,128)(2,1)}, bf16[512,768]{1,0:T(8,128)(2,1)S(1)}, u32[]{:S(2)}, u32[]{:S(2)}) collective-permute-start(bf16[512,768]{1,0:T(8,128)(2,1)} %get-tuple-element.168), channel_id=1, source_target_pairs={{0,2},{1,3},{2,0},{3,1},{4,6},{5,7},{6,4},{7,5},{8,10},{9,11},{10,... | collective-permute-start | bytes 2359304 | tf_op jit(solution)/shard_map/ppermute | solution.py:1141
  224.8 14.4 %collective-permute-start.31 = (bf16[256,768]{1,0:T(8,128)(2,1)}, bf16[256,768]{1,0:T(8,128)(2,1)S(1)}, u32[]{:S(2)}, u32[]{:S(2)}) collective-permute-start(bf16[256,768]{1,0:T(8,128)(2,1)} %get-tuple-element.166.refs_1_), channel_id=1, source_target_pairs={{0,4},{1,5},{2,10},{3,11},{4,0},{5,1},{6,14},{7,15},{8,12},{9,13},... | collective-permute-start | bytes 1179656 | tf_op jit(solution)/shard_map/ppermute | solution.py:1141
  224.8 14.4 %collective-permute-start.35 = (bf16[1,256,768]{2,1,0:T(8,128)(2,1)}, bf16[1,256,768]{2,1,0:T(8,128)(2,1)S(1)}, u32[]{:S(2)}, u32[]{:S(2)}) collective-permute-start(bf16[1,256,768]{2,1,0:T(8,128)(2,1)} %get-tuple-element.172.refs_5_), channel_id=1, source_target_pairs={{0,16},{1,17},{2,6},{3,7},{4,20},{5,21},{6,2},{7,3},{8,24},{9,25},... | collective-permute-start | bytes 1179656 | tf_op jit(solution)/shard_map/ppermute | solution.py:1141
  225.1 23.7 %collective-permute-start.36 = (bf16[2,192,768]{2,1,0:T(8,128)(2,1)}, bf16[2,192,768]{2,1,0:T(8,128)(2,1)S(1)}, u32[]{:S(2)}, u32[]{:S(2)}) collective-permute-start(bf16[2,192,768]{2,1,0:T(8,128)(2,1)} %get-tuple-element.170.refs_5_.refs_7_), channel_id=1, source_target_pairs={{0,8},{1,9},{2,18},{3,19},{4,12},{5,13},{6,22},{7,23},{8,0},{9,1},... | collective-permute-start | bytes 1769480 | tf_op jit(solution)/shard_map/ppermute | solution.py:1141
  227.7 6.1 %copy-start = (f32[2,768]{1,0:T(2,128)S(1)}, f32[2,768]{1,0:T(2,128)}, u32[]{:S(2)}) copy-start(f32[2,768]{1,0:T(2,128)} %slice.22) | copy-start | bytes 18436
  233.9 4.2 %collective-permute-start.33 = (f32[8,768]{1,0:T(8,128)S(1)}, f32[8,768]{1,0:T(8,128)S(1)}, u32[]{:S(2)}, u32[]{:S(2)}) collective-permute-start(f32[8,768]{1,0:T(8,128)S(1)} %pad_maximum_fusion), channel_id=1, source_target_pairs={{0,1},{1,0},{2,3},{3,2},{4,5},{5,4},{6,7},{7,6},{8,9},{9,8},{10,11... | collective-permute-start | bytes 73736 | tf_op jit(solution)/shard_map/ppermute | solution.py:1141
  238.1 10.7 %copy-start.1 = (f32[8,768]{1,0:T(8,128)}, f32[8,768]{1,0:T(8,128)S(1)}, u32[]{:S(2)}) copy-start(f32[8,768]{1,0:T(8,128)S(1)} %fusion.refs_3_) | copy-start | bytes 73732
  238.1 10.7 %collective-permute-start.34 = (f32[8,768]{1,0:T(8,128)S(1)}, f32[8,768]{1,0:T(8,128)S(1)}, u32[]{:S(2)}, u32[]{:S(2)}) collective-permute-start(f32[8,768]{1,0:T(8,128)S(1)} %fusion.refs_3_), channel_id=1, source_target_pairs={{0,4},{1,5},{2,10},{3,11},{4,0},{5,1},{6,14},{7,15},{8,12},{9,13},... | collective-permute-start | bytes 73736 | tf_op jit(solution)/shard_map/ppermute | solution.py:1141
  239.2 9.6 %copy-start.24 = (bf16[256,768]{1,0:T(8,128)(2,1)}, bf16[256,768]{1,0:T(8,128)(2,1)S(1)}, u32[]{:S(2)}) copy-start(bf16[256,768]{1,0:T(8,128)(2,1)S(1)} %collective-permute-done.31.refs_2_) | copy-start | bytes 1179652
  239.2 9.6 %copy-start.25 = (bf16[1,256,768]{2,1,0:T(8,128)(2,1)}, bf16[1,256,768]{2,1,0:T(8,128)(2,1)S(1)}, u32[]{:S(2)}) copy-start(bf16[1,256,768]{2,1,0:T(8,128)(2,1)S(1)} %collective-permute-done.35.refs_6_) | copy-start | bytes 1179652
  253.4 28.4 %collective-permute-start.39 = (bf16[2,384,768]{2,1,0:T(8,128)(2,1)}, bf16[2,384,768]{2,1,0:T(8,128)(2,1)S(1)}, u32[]{:S(2)}, u32[]{:S(2)}) collective-permute-start(bf16[2,384,768]{2,1,0:T(8,128)(2,1)} %get-tuple-element.175.refs_5_.refs_7_), channel_id=1, source_target_pairs={{0,4},{1,5},{2,10},{3,11},{4,0},{5,1},{6,14},{7,15},{8,12},{9,13},... | collective-permute-start | bytes 3538952 | tf_op jit(solution)/shard_map/ppermute | solution.py:1141
  253.4 28.4 %collective-permute-start.37 = (bf16[272,768]{1,0:T(8,128)(2,1)}, bf16[272,768]{1,0:T(8,128)(2,1)S(1)}, u32[]{:S(2)}, u32[]{:S(2)}) collective-permute-start(bf16[272,768]{1,0:T(8,128)(2,1)} %get-tuple-element.173.refs_1_), channel_id=1, source_target_pairs={{0,8},{1,9},{2,18},{3,19},{4,12},{5,13},{6,22},{7,23},{8,0},{9,1},... | collective-permute-start | bytes 1253384 | tf_op jit(solution)/shard_map/ppermute | solution.py:1141
  256.2 25.6 %collective-permute-start.38 = (bf16[1,256,768]{2,1,0:T(8,128)(2,1)}, bf16[1,256,768]{2,1,0:T(8,128)(2,1)S(1)}, u32[]{:S(2)}, u32[]{:S(2)}) collective-permute-start(bf16[1,256,768]{2,1,0:T(8,128)(2,1)} %get-tuple-element.174.refs_3_), channel_id=1, source_target_pairs={{0,4},{1,5},{2,10},{3,11},{4,0},{5,1},{6,14},{7,15},{8,12},{9,13},... | collective-permute-start | bytes 1179656 | tf_op jit(solution)/shard_map/ppermute | solution.py:1141
  282.7 1.0 copy-start.10
  287.7 17.0 %collective-permute-start.43 = (bf16[2,768,768]{2,1,0:T(8,128)(2,1)}, bf16[2,768,768]{2,1,0:T(8,128)(2,1)S(1)}, u32[]{:S(2)}, u32[]{:S(2)}) collective-permute-start(bf16[2,768,768]{2,1,0:T(8,128)(2,1)} %get-tuple-element.178.refs_1_.refs_3_), channel_id=1, source_target_pairs={{0,2},{1,3},{2,0},{3,1},{4,6},{5,7},{6,4},{7,5},{8,10},{9,11},{10,... | collective-permute-start | bytes 7077896 | tf_op jit(solution)/shard_map/ppermute | solution.py:1141
  287.8 25.2 %collective-permute-start.41 = (bf16[512,768]{1,0:T(8,128)(2,1)}, bf16[512,768]{1,0:T(8,128)(2,1)}, u32[]{:S(2)}, u32[]{:S(2)}) collective-permute-start(bf16[512,768]{1,0:T(8,128)(2,1)} %shard_map.244.refs_8_), channel_id=1, source_target_pairs={{0,0},{1,2},{2,1},{3,3},{4,4},{5,6},{6,5},{7,7},{8,8},{9,10},{10,9... | collective-permute-start | bytes 2359304 | tf_op jit(solution)/shard_map/ppermute | solution.py:1141
  294.1 18.9 %collective-permute-start.42 = (bf16[512,768]{1,0:T(8,128)(2,1)}, bf16[512,768]{1,0:T(8,128)(2,1)}, u32[]{:S(2)}, u32[]{:S(2)}) collective-permute-start(bf16[512,768]{1,0:T(8,128)(2,1)} %get-tuple-element.177), channel_id=1, source_target_pairs={{0,0},{1,2},{2,1},{3,3},{4,4},{5,6},{6,5},{7,7},{8,8},{9,10},{10,9... | collective-permute-start | bytes 2359304 | tf_op jit(solution)/shard_map/ppermute | solution.py:1141
  296.0 16.9 %collective-permute-start.40 = (bf16[272,768]{1,0:T(8,128)(2,1)}, bf16[272,768]{1,0:T(8,128)(2,1)}, u32[]{:S(2)}, u32[]{:S(2)}) collective-permute-start(bf16[272,768]{1,0:T(8,128)(2,1)} %get-tuple-element.176.refs_0_), channel_id=1, source_target_pairs={{0,16},{1,17},{2,6},{3,7},{4,20},{5,21},{6,2},{7,3},{8,24},{9,25},... | collective-permute-start | bytes 1253384 | tf_op jit(solution)/shard_map/ppermute | solution.py:1141
  297.2 22.5 %collective-permute-start.44 = (bf16[1,512,768]{2,1,0:T(8,128)(2,1)}, bf16[1,512,768]{2,1,0:T(8,128)(2,1)}, u32[]{:S(2)}, u32[]{:S(2)}) collective-permute-start(bf16[1,512,768]{2,1,0:T(8,128)(2,1)} %get-tuple-element.182), channel_id=1, source_target_pairs={{0,2},{1,3},{2,0},{3,1},{4,6},{5,7},{6,4},{7,5},{8,10},{9,11},{10,... | collective-permute-start | bytes 2359304 | tf_op jit(solution)/shard_map/ppermute | solution.py:1141
  304.8 1.4 copy-start.8
  315.9 5.4 %collective-permute-start.45 = (bf16[272,768]{1,0:T(8,128)(2,1)}, bf16[272,768]{1,0:T(8,128)(2,1)S(1)}, u32[]{:S(2)}, u32[]{:S(2)}) collective-permute-start(bf16[272,768]{1,0:T(8,128)(2,1)} %get-tuple-element.183.refs_3_), channel_id=1, source_target_pairs={{0,2},{1,3},{2,0},{3,1},{4,6},{5,7},{6,4},{7,5},{8,10},{9,11},{10,... | collective-permute-start | bytes 1253384 | tf_op jit(solution)/shard_map/ppermute | solution.py:1141
  (11 other events, 9.0 us)

commit v3 on v2

v3 whole, which is shorter than its diff:
```python
import functools

import jax
import jax.numpy as jnp
from jax import lax
from jax.experimental import pallas as pl
from jax.experimental.pallas import tpu as pltpu
from jax.sharding import PartitionSpec as P

HEAD_DIM = 64
EPS = 1e-05
FAR = 1e30
FORWARD_BLOCK = 512
BF16 = jnp.bfloat16
F32 = jnp.float32
TN = (((0,), (0,)), ((), ()))
NT = (((1,), (1,)), ((), ()))
NN = (((1,), (0,)), ((), ()))
TT = (((0,), (1,)), ((), ()))
ERF_C = (
    1.5897294934128858e-07,
    -5.985900079472216e-06,
    8.971378204617447e-05,
    -0.0006257225011275588,
    -0.0001843806018428344,
    0.10276548023357895,
    1.1283797055884355,
)
ERF_X = tuple(c * 0.5 ** (6 - i) * 0.7071067811865476 for i, c in enumerate(ERF_C))


def dot(left, right, dims):
    return lax.dot_general(left, right, dims, preferred_element_type=F32)


def sds(shape, dtype):
    return jax.ShapeDtypeStruct(shape, dtype)


SMEM = pl.BlockSpec(memory_space=pltpu.SMEM)
VMEM = pl.BlockSpec(memory_space=pltpu.VMEM)
ANY = pl.BlockSpec(memory_space=pl.ANY)


WEIGHT = 20.0


class Order:
    def __init__(self):
        self.last = None

    def run(self, us, kernel, operands, out_shape, in_specs=None, after=(), **rest):
        after = tuple(after) + (() if self.last is None else (self.last,))
        count, extra = len(operands), len(after)
        in_specs = list(in_specs or [VMEM] * count) + [ANY] * extra

        def body(*refs):
            kernel(*refs[:count], *refs[count + extra :])

        out = pl.pallas_call(
            body,
            out_shape=out_shape,
            in_specs=in_specs,
            compiler_params=pltpu.CompilerParams(vmem_limit_bytes=58 << 20),
            cost_estimate=pl.CostEstimate(
                flops=int(us * WEIGHT * 1.15e9), bytes_accessed=0, transcendentals=0
            ),
            **rest,
        )(*operands, *after)
        self.last = out[-1] if isinstance(out, (list, tuple)) else out
        return out

    def hold(self, values, after):
        count = len(values)

        def kernel(*refs):
            pass

        held = pl.pallas_call(
            kernel,
            out_shape=[sds(value.shape, value.dtype) for value in values],
            in_specs=[ANY] * (count + len(after)),
            out_specs=[ANY] * count,
            input_output_aliases={i: i for i in range(count)},
            compiler_params=pltpu.CompilerParams(has_side_effects=True),
            cost_estimate=pl.CostEstimate(flops=0, bytes_accessed=0, transcendentals=0),
        )(*values, *after)
        for value, same in zip(values, held):
            if self.last is value:
                self.last = same
        return held


def whole(shape):
    return pl.BlockSpec(shape, lambda *_: (0,) * len(shape))


def low_sum(*terms):
    total = terms[0].astype(F32)
    for term in terms[1:]:
        total = total + term.astype(F32)
    return total.astype(BF16)


def part_rows(index, size):
    return pl.ds(pl.multiple_of(index * size, size), size)


def split(place, bit, source, keep, send):
    half = keep.shape[1]
    keep[...] = source[:, part_rows(place[2 + bit], half), :]
    send[...] = source[:, part_rows(1 - place[2 + bit], half), :]


def quarter(place):
    return 2 * place[2] + place[3]


def scatter(place, source, outs):
    for partner, out in enumerate(outs):
        out[...] = source[:, part_rows(quarter(place) ^ partner, out.shape[1]), :]


def gather(place, pieces, out):
    for partner, piece in enumerate(pieces):
        out[:, part_rows(quarter(place) ^ partner, piece.shape[1]), :] = piece[...]


def normalize(values):
    center = values - jnp.mean(values, axis=-1, keepdims=True)
    inverse = lax.rsqrt(jnp.mean(center * center, axis=-1, keepdims=True) + EPS)
    return center * inverse, inverse


def norm_back(grad_normed, scaled, inverse, gain):
    grad_scaled = grad_normed * gain
    return inverse * (
        grad_scaled
        - jnp.mean(grad_scaled, axis=-1, keepdims=True)
        - scaled * jnp.mean(grad_scaled * scaled, axis=-1, keepdims=True)
    )


def gelu_pair(x):
    square = x * x
    near = jnp.minimum(square, 64.0)
    poly = ERF_X[0]
    for coefficient in ERF_X[1:]:
        poly = poly * near + coefficient
    phi = 0.5 * jnp.tanh(x * poly) + 0.5
    bell = jnp.exp(square * -0.5)
    return x * phi, phi + x * (bell * 0.3989422804014327)


def pack_first_kernel(place, w_query, w_key, w_value, qkv, qkv_send, first):
    width = qkv.shape[1] // 3
    half = qkv_send.shape[0]
    first[:, :HEAD_DIM] = w_query[:, :HEAD_DIM]
    first[:, HEAD_DIM:] = w_key[:, :HEAD_DIM]
    for core in range(2):

        @pl.when(place[0] == core)
        def _():
            narrow = slice(core * width, (core + 1) * width)
            for i, weight in enumerate((w_query, w_key, w_value)):
                qkv[:, i * width : (i + 1) * width] = weight[:, narrow]

    qkv_send[...] = qkv[pl.ds(pl.multiple_of(place[2] * half, half), half), :]


def pack_first_call(order, place, w_query, w_key, w_value):
    dim, width = w_query.shape[0], w_query.shape[1] // 2
    return order.run(
        4,
        pack_first_kernel,
        (place, w_query, w_key, w_value),
        [
            sds((dim, 3 * width), BF16),
            sds((dim // 2, 3 * width), BF16),
            sds((dim, 2 * HEAD_DIM), BF16),
        ],
        [SMEM] + [VMEM] * 3,
    )


def pack_last_kernel(place, w_out, w_up, w_down, grad, out, up, up_send, down, down_send, grad_out):
    width = out.shape[0]
    units = down.shape[0]
    half = units // 2
    grad_out[...] = grad[...]
    for core in range(2):

        @pl.when(place[0] == core)
        def _():
            wide = slice(core * units, (core + 1) * units)
            out[...] = w_out[core * width : (core + 1) * width, :]
            up[...] = w_up[:, wide]
            down[...] = w_down[wide, :]

    rows = pl.ds(pl.multiple_of(place[2] * half, half), half)
    up_send[...] = up[rows, :]
    down_send[...] = down[rows, :]


def pack_last_call(order, place, w_out, w_up, w_down, grad):
    width, dim = w_out.shape[0] // 2, w_out.shape[1]
    units = w_up.shape[1] // 2
    return order.run(
        5,
        pack_last_kernel,
        (place, w_out, w_up, w_down, grad),
        [
            sds((width, dim), BF16),
            sds((dim, units), BF16),
            sds((dim // 2, units), BF16),
            sds((units, dim), BF16),
            sds((units // 2, dim), BF16),
            sds(grad.shape, BF16),
        ],
        [SMEM] + [VMEM] * 4,
    )


def norm1_kernel(tokens, gain, shift, out):
    scaled, _ = normalize(tokens[...].astype(F32))
    out[...] = (scaled * gain[...] + shift[...]).astype(BF16)


def rows_spec(block, dim):
    return pl.BlockSpec((block, dim), lambda i: (i, 0))


def norm1_call(order, tokens, gain, shift):
    return order.run(2.5, norm1_kernel, (tokens, gain, shift), sds(tokens.shape, BF16))


def masks(seg_pad, cols, low, high):
    width = high - low
    seg_row = seg_pad[0:1, low:high]
    pad_row = seg_pad[1:2, low:high]
    row_key = jnp.where(pad_row > 0, seg_row, -2.0)
    col_seg = cols[:high, 0:1]
    col_pad = cols[:high, 1:2]
    col_key = jnp.where(col_pad > 0, col_seg, -1.0)
    key_at = lax.broadcasted_iota(jnp.int32, (high, width), 0)
    query_at = lax.broadcasted_iota(jnp.int32, (high, width), 1) + low
    allowed = ((col_key == seg_row) & (key_at <= query_at)) | (key_at == query_at)
    picked = (col_key == row_key) & (key_at < query_at)
    return allowed, picked


def penalty_kernel(
    block, place, n1_own, n1_other, first, first_moved, seg_pad, n1_out, penalty, qk0, first_out
):
    seq = n1_out.shape[0]
    half = seq // 2
    core = place[0]
    n1_out[pl.ds(pl.multiple_of(core * half, half), half), :] = n1_own[...]
    n1_out[pl.ds(pl.multiple_of((1 - core) * half, half), half), :] = n1_other[...]

    @pl.when(place[1] == 0)
    def _():
        first_out[...] = first[...]

    @pl.when(place[1] != 0)
    def _():
        first_out[...] = first_moved[...]

    qk = dot(first_out[...], n1_out[...], TT)
    q0 = (qk[:HEAD_DIM].astype(BF16) * 0.125).astype(BF16)
    k0 = qk[HEAD_DIM:].astype(BF16)
    qk0[:HEAD_DIM, :] = q0
    qk0[HEAD_DIM:, :] = k0
    seg_value = seg_pad[...]
    cols = seg_value.T
    earlier = lax.broadcasted_iota(jnp.int32, (block, block + 128), 0)
    later = lax.broadcasted_iota(jnp.int32, (block, block + 128), 1)
    sums = ((earlier < later) | (later >= block)).astype(F32).astype(BF16)
    carry = jnp.zeros((seq, 128), F32)
    for low in range(0, seq, block):
        high = low + block
        allowed, picked = masks(seg_value, cols, low, high)
        score = dot(k0[:, :high], q0[:, low:high], TN)
        small = jnp.exp(-jnp.abs(score))
        log1p = jnp.where(small < 1e-3, small - 0.5 * small * small, jnp.log(1.0 + small))
        select = jnp.where(picked, jnp.maximum(score, 0.0) + log1p, 0.0).astype(BF16)
        total = dot(select, sums, NN)
        before = jnp.concatenate([carry[:high]] * (block // 128), axis=1)
        penalty[:high, low:high] = jnp.where(allowed, total[:, :block] + before, FAR)
        if high % FORWARD_BLOCK:
            edge = high + FORWARD_BLOCK - high % FORWARD_BLOCK
            penalty[high:edge, low:high] = jnp.full((edge - high, block), FAR, F32)
        carry = jnp.concatenate([carry[:high] + total[:, block:], carry[high:]], axis=0)


def penalty_call(order, place, n1_own, n1_other, first, first_moved, seg_pad, after=()):
    half, dim = n1_own.shape
    seq = 2 * half
    return order.run(
        6.5,
        functools.partial(penalty_kernel, 256),
        (place, n1_own, n1_other, first, first_moved, seg_pad),
        [
            sds((seq, dim), BF16),
            sds((seq, seq), F32),
            sds((2 * HEAD_DIM, seq), BF16),
            sds(first.shape, BF16),
        ],
        [SMEM] + [VMEM] * 5,
        after,
    )


def forward_kernel(block, split, *refs):
    if split:
        place, n1, near, far, penalty, qkv, out, lse, weights = refs
    else:
        n1, weights, penalty, qkv, out, lse = refs
    head = pl.program_id(0)
    third = qkv.shape[0] // 3
    seq = qkv.shape[1]

    @pl.when(head == 0)
    def _():
        if split:
            join(place[2], weights, near, far)
        product = dot(weights[...], n1[...], TT).astype(BF16)
        qkv[:third, :] = (product[:third] * 0.125).astype(BF16)
        qkv[third:, :] = product[third:]

    at = pl.multiple_of(head * HEAD_DIM, HEAD_DIM)
    query = qkv[pl.ds(at, HEAD_DIM), :]
    key = qkv[pl.ds(third + at, HEAD_DIM), :]
    value = qkv[pl.ds(2 * third + at, HEAD_DIM), :]
    value = jnp.concatenate([value, jnp.ones((16, seq), BF16)], axis=0)
    for low in range(0, seq, block):
        high = low + block
        logits = dot(key[:, :high], query[:, low:high], TN) - penalty[:high, low:high]
        largest = jnp.max(logits, axis=0, keepdims=True)
        weight = jnp.exp(logits - largest).astype(BF16)
        result = dot(value[:, :high], weight, NN)
        total = result[HEAD_DIM : HEAD_DIM + 1, :]
        out[:, low:high] = (result[:HEAD_DIM] / total).astype(BF16)
        lse[:, low:high] = largest + jnp.log(total)


def join(bit, out, near, far):
    half = near.shape[0]
    out[pl.ds(pl.multiple_of(bit * half, half), half), :] = near[...]
    out[pl.ds(pl.multiple_of((1 - bit) * half, half), half), :] = far[...]


def forward_call(order, n1, weights, penalty, place=None, after=()):
    seq, dim = n1.shape
    split = place is not None
    width = weights[0].shape[1]
    heads = width // (3 * HEAD_DIM)
    operands = ((place,) if split else ()) + (n1,) + tuple(weights) + (penalty,)
    in_specs = [SMEM] if split else []
    in_specs += [whole(x.shape) for x in operands if x is not place]
    out_specs = [
        whole((width, seq)),
        pl.BlockSpec((HEAD_DIM, seq), lambda h: (h, 0)),
        pl.BlockSpec((None, 1, seq), lambda h: (h, 0, 0)),
    ]
    out_shape = [
        sds((width, seq), BF16),
        sds((heads * HEAD_DIM, seq), BF16),
        sds((heads, 1, seq), F32),
    ]
    if split:
        out_specs.append(whole((dim, width)))
        out_shape.append(sds((dim, width), BF16))
    return order.run(
        9.3,
        functools.partial(forward_kernel, FORWARD_BLOCK, split),
        operands,
        out_shape,
        in_specs,
        after,
        grid=(heads,),
        out_specs=out_specs,
    )


def project_kernel(place, out_l, out_r, w_l, w_r, own, send):
    half = own.shape[0]
    core = place[0]
    mixed = jnp.concatenate([w_l[...], w_r[...]], axis=0)

    def part(which):
        at = pl.ds(pl.multiple_of(which * half, half), half)
        heads = jnp.concatenate([out_l[:, at], out_r[:, at]], axis=0)
        return dot(heads, mixed, TN)

    send[...] = part(1 - core).astype(BF16)
    own[...] = part(core)


def project_call(order, place, out_l, out_r, w_l, w_r, after=()):
    half, dim = out_l.shape[1] // 2, w_l.shape[1]
    return order.run(
        3.5,
        project_kernel,
        (place, out_l, out_r, w_l, w_r),
        [sds((half, dim), F32), sds((half, dim), BF16)],
        [SMEM] + [VMEM] * 4,
        after,
    )


def norm2_kernel(tokens, own, received, gain, shift, hidden, out):
    total = tokens[...].astype(F32) + (own[...] + received[...].astype(F32))
    hidden[...] = total
    scaled, _ = normalize(total)
    out[...] = (scaled * gain[...] + shift[...]).astype(BF16)


def norm2_call(order, tokens, own, received, gain, shift, after=()):
    size, dim = tokens.shape
    rows = rows_spec(size // 4, dim)
    vector = whole((1, dim))
    return order.run(
        4,
        norm2_kernel,
        (tokens, own, received, gain, shift),
        [sds(tokens.shape, F32), sds(tokens.shape, BF16)],
        [rows] * 3 + [vector] * 2,
        after,
        grid=(4,),
        out_specs=[rows, rows],
    )


def mlp_kernel(first, steps, *refs):
    if first:
        place, n2_other, n2_own, g_other, g_own, w_up, w_down, *refs = refs
        mixed_send, mixed_own, back_send, back_own, keep, send, *refs = refs
    else:
        place, n2_other, n2_own, g_other, g_own, *refs = refs
        up_near, up_far, down_near, down_far, *refs = refs
        mixed_in_send, mixed_in_own, back_in_send, back_in_own, *refs = refs
        mixed_send, mixed_own, back_send, back_own, *refs = refs
        parts, refs = refs[:4], refs[4:]
        w_up, w_down, *refs = refs
    rows, grads, actives, grad_ups, w_grads = refs
    step = pl.program_id(0)
    block = n2_own.shape[0]
    early = step < steps // 2

    if not first:

        @pl.when(step == 0)
        def _():
            join(place[2], w_up, up_near, up_far)
            join(place[2], w_down, down_near, down_far)

    here = pl.ds(pl.multiple_of(step * block, block), block)
    row = jnp.where(early, n2_other[...], n2_own[...])
    grad = jnp.where(early, g_other[...], g_own[...])
    rows[here, :] = row
    grads[here, :] = grad
    active, slope = gelu_pair(dot(row, w_up[...], NN))
    active = active.astype(BF16)
    grad_up = (dot(grad, w_down[...], NT) * slope).astype(BF16)
    actives[here, :] = active
    grad_ups[here, :] = grad_up
    back = dot(grad_up, w_up[...], NT)
    mixed = dot(active, w_down[...], NN)

    @pl.when(early)
    def _():
        if first:
            back_send[...] = back.astype(back_send.dtype)
            mixed_send[...] = mixed.astype(mixed_send.dtype)
        else:
            back_send[...] = (back + back_in_send[...]).astype(back_send.dtype)
            mixed_send[...] = (mixed + mixed_in_send[...]).astype(mixed_send.dtype)

    @pl.when(jnp.logical_not(early))
    def _():
        if first:
            back_own[...] = back
            mixed_own[...] = mixed
        else:
            back_own[...] = back + back_in_own[...]
            mixed_own[...] = mixed + mixed_in_own[...]

    @pl.when(step == steps - 1)
    def _():
        w_grads[0] = dot(rows[...], grad_ups[...], TN).astype(BF16)
        w_grads[1] = dot(actives[...], grads[...], TN).astype(BF16)
        if first:
            split(place, 0, w_grads, keep, send)
        else:
            scatter(place, w_grads, parts)


def mlp_call(order, place, n2_other, n2_own, g_other, g_own, weights, before=None, after=()):
    size, dim = n2_own.shape
    first = before is None
    units = weights[0].shape[1]
    block = min(256, size // 2)
    steps = 2 * size // block
    last = steps // 2 - 1
    sent = pl.BlockSpec((block, dim), lambda i: (jnp.minimum(i, last), 0))
    kept = pl.BlockSpec((block, dim), lambda i: (jnp.maximum(i - last - 1, 0), 0))
    operands = (place, n2_other, n2_own, g_other, g_own) + tuple(weights)
    in_specs = [SMEM, sent, kept, sent, kept] + [whole(weight.shape) for weight in weights]
    sent_type = F32 if first else BF16
    scratch = []
    if not first:
        operands += tuple(before)
        in_specs += [sent, kept, sent, kept]
        scratch = [pltpu.VMEM((dim, units), BF16), pltpu.VMEM((units, dim), BF16)]
    count = 2 if first else 4
    part = (2, units // count, dim)
    tall = pltpu.VMEM((2 * size, dim), BF16)
    flat = pltpu.VMEM((2 * size, units), BF16)
    return order.run(
        14.6,
        functools.partial(mlp_kernel, first, steps),
        operands,
        [
            sds((size, dim), sent_type),
            sds((size, dim), F32),
            sds((size, dim), sent_type),
            sds((size, dim), F32),
        ]
        + [sds(part, BF16)] * count,
        in_specs,
        after,
        grid=(steps,),
        out_specs=[sent, kept, sent, kept] + [whole(part)] * count,
        scratch_shapes=scratch + [tall, tall, flat, flat, pltpu.VMEM((2, units, dim), BF16)],
    )


def norm2_back_kernel(hidden, own, received, grad, gain, grad_hidden, low, sums):
    normed_grad = own[...] + received[...].astype(F32)
    scaled, inverse = normalize(hidden[...])
    total = grad[...].astype(F32) + norm_back(normed_grad, scaled, inverse, gain[...])
    grad_hidden[...] = total
    low[...] = total.astype(BF16)
    add_sums(sums, normed_grad, scaled)


def add_sums(sums, normed_grad, scaled):
    @pl.when(pl.program_id(0) == 0)
    def _():
        sums[...] = jnp.zeros(sums.shape, F32)

    sums[0:1, :] += jnp.sum(normed_grad * scaled, axis=0, keepdims=True)
    sums[1:2, :] += jnp.sum(normed_grad, axis=0, keepdims=True)


def norm2_back_call(order, hidden, own, received, grad, gain, after=()):
    size, dim = hidden.shape
    rows = rows_spec(size // 4, dim)
    return order.run(
        5,
        norm2_back_kernel,
        (hidden, own, received, grad, gain),
        [sds(hidden.shape, F32), sds(hidden.shape, BF16), sds((8, dim), F32)],
        [rows] * 4 + [whole((1, dim))],
        after,
        grid=(4,),
        out_specs=[rows, rows, whole((8, dim))],
    )


def mixed_kernel(place, hidden, own, received, near, far, out, keep, send, total):
    out[...] = (hidden[...] + (own[...] + received[...].astype(F32))).astype(BF16)
    total[...] = low_sum(near[...], far[...])
    split(place, 1, total, keep, send)


def mixed_call(order, place, hidden, own, received, near, far):
    groups, rows, dim = near.shape
    return order.run(
        4,
        mixed_kernel,
        (place, hidden, own, received, near, far),
        [sds(hidden.shape, BF16)] + [sds((groups, rows // 2, dim), BF16)] * 2,
        [SMEM] + [VMEM] * 5,
        scratch_shapes=[pltpu.VMEM(near.shape, BF16)],
    )


def backward_kernel(first, block, *refs):
    place, g_own, g_other, w_out, heads_out, qkv, lse, penalty, *refs = refs
    if not first:
        before, *refs = refs
    grads, w_grad, logit_sum, grad_full, grad_heads, key_sum, value_sum, *refs = refs
    head = pl.program_id(0)
    third = qkv.shape[0] // 3
    seq = qkv.shape[1]
    half = seq // 2
    total = logit_sum if first else refs[0]

    @pl.when(head == 0)
    def _():
        core = place[0]
        grad_full[pl.ds(pl.multiple_of(core * half, half), half), :] = g_own[...]
        grad_full[pl.ds(pl.multiple_of((1 - core) * half, half), half), :] = g_other[...]
        whole_grad = grad_full[...]
        grad_heads[...] = dot(w_out[...], whole_grad, NT).astype(BF16)
        w_grad[...] = dot(heads_out[...], whole_grad, NN).astype(BF16)
        for low in range(0, seq, block):
            high = low + block
            if first:
                total[:high, low:high] = jnp.zeros((high, block), F32)
            else:
                total[:high, low:high] = before[:high, low:high]

    at = pl.multiple_of(head * HEAD_DIM, HEAD_DIM)
    query = qkv[pl.ds(at, HEAD_DIM), :]
    key = qkv[pl.ds(third + at, HEAD_DIM), :]
    value = qkv[pl.ds(2 * third + at, HEAD_DIM), :]
    grad = grad_heads[pl.ds(at, HEAD_DIM), :]
    for low in range(0, seq, block):
        high = low + block
        cols = slice(low, high)
        score = dot(key[:, :high], query[:, cols], TN)
        probs = jnp.exp(score - penalty[:high, cols] - lse[:, cols])
        grad_probs = dot(value[:, :high], grad[:, cols], TN)
        row_dot = jnp.sum(probs * grad_probs, axis=0, keepdims=True)
        grad_logits = probs * (grad_probs - row_dot)
        total[:high, cols] += grad_logits
        low_logits = grad_logits.astype(BF16)
        low_probs = probs.astype(BF16)
        grads[pl.ds(at, HEAD_DIM), cols] = (
            dot(key[:, :high], low_logits, NN) * 0.125
        ).astype(BF16)
        value_new = dot(grad[:, cols], low_probs, NT)
        key_new = dot(query[:, cols], low_logits, NT)
        if low:
            key_sum[:, :low] += key_new[:, :low]
            value_sum[:, :low] += value_new[:, :low]
        key_sum[:, cols] = key_new[:, low:]
        value_sum[:, cols] = value_new[:, low:]
    grads[pl.ds(third + at, HEAD_DIM), :] = key_sum[...].astype(BF16)
    grads[pl.ds(2 * third + at, HEAD_DIM), :] = value_sum[...].astype(BF16)
    if not first:

        @pl.when(head == pl.num_programs(0) - 1)
        def _():
            for low in range(0, seq, block):
                high = low + block
                logit_sum[:high, low:high] = total[:high, low:high].astype(BF16)


def backward_call(order, place, g_own, g_other, w_out, heads_out, qkv, lse, penalty, before=None):
    width, seq = qkv.shape
    half, dim = g_own.shape
    heads = width // (3 * HEAD_DIM)
    first = before is None
    square = whole((seq, seq))
    operands = (place, g_own, g_other, w_out, heads_out, qkv, lse, penalty)
    in_specs = [SMEM] + [whole(x.shape) for x in operands[1:6]]
    in_specs += [pl.BlockSpec((None, 1, seq), lambda h: (h, 0, 0)), square]
    scratch = [
        pltpu.VMEM((seq, dim), BF16),
        pltpu.VMEM((width // 3, seq), BF16),
        pltpu.VMEM((HEAD_DIM, seq), F32),
        pltpu.VMEM((HEAD_DIM, seq), F32),
    ]
    if not first:
        operands += (before,)
        in_specs.append(square)
        scratch.append(pltpu.VMEM((seq, seq), F32))
    return order.run(
        17,
        functools.partial(backward_kernel, first, 256),
        operands,
        [
            sds((width, seq), BF16),
            sds(w_out.shape, BF16),
            sds((seq, seq), F32 if first else BF16),
        ],
        in_specs,
        grid=(heads,),
        out_specs=[whole((width, seq)), whole(w_out.shape), square],
        scratch_shapes=scratch,
    )


def halves(value):
    high = value.astype(BF16)
    return high, (value - high.astype(F32)).astype(BF16)


def select_back(block, core, own, received, qk0, seg_pad, n1, out, w_grad, total_grad):
    seq = own.shape[0]
    q0 = qk0[:HEAD_DIM, :]
    k0 = qk0[HEAD_DIM:, :]
    seg_value = seg_pad[...]
    cols = seg_value.T
    later = lax.broadcasted_iota(jnp.int32, (block, block + 128), 0)
    earlier = lax.broadcasted_iota(jnp.int32, (block, block + 128), 1)
    sums = ((later > earlier) | (earlier >= block)).astype(F32).astype(BF16)
    carry = jnp.zeros((seq, 128), F32)
    total_grad[...] = jnp.zeros(total_grad.shape, F32)
    for low in range(seq - block, -1, -block):
        high = low + block
        logit_sum = own[:high, low:high].astype(F32) + received[:high, low:high].astype(F32)
        top, bottom = halves(logit_sum)
        total = dot(top, sums, NN) + dot(bottom, sums, NN)
        after = jnp.concatenate([carry[:high]] * (block // 128), axis=1)
        select_grad = -(total[:, :block] + after)
        carry = carry[:high] + total[:, block:]
        _, picked = masks(seg_value, cols, low, high)
        score = dot(k0[:, :high], q0[:, low:high], TN)
        through = jnp.where(picked, select_grad / (1.0 + jnp.exp(-score)), 0.0)
        top, bottom = halves(through)
        total_grad[:HEAD_DIM, low:high] = 0.125 * (
            dot(k0[:, :high], top, NN) + dot(k0[:, :high], bottom, NN)
        )
        total_grad[HEAD_DIM:, :high] += dot(q0[:, low:high], top, NT) + dot(
            q0[:, low:high], bottom, NT
        )
    out[...] = jnp.where(core == 0, total_grad[...], 0.0).astype(BF16)
    w_grad[...] = dot(out[...], n1[...], NN).astype(BF16)


def weights_first_kernel(place, n1, grads, weights, w_out, *refs):
    ff_near, ff_far, *refs = refs
    ff_parts, refs = refs[:4], refs[4:]
    back, ff, ff_move, *refs = refs
    parts, total = refs[:4], refs[4]
    width = grads.shape[0]
    ff[...] = low_sum(ff_near[...], ff_far[...])
    ff_move[...] = low_sum(*(part[...] for part in ff_parts))
    total[0, :width, :] = dot(grads[...], n1[...], NN).astype(BF16)
    total[0, width:, :] = w_out[...]
    scatter(place, total, parts)
    back[...] = dot(grads[...], weights[...], TT)


def weights_first_call(order, place, n1, grads, weights, w_out, ff_terms, ff_parts, after=()):
    seq, dim = n1.shape
    rows = grads.shape[0] + w_out.shape[0]
    shape = ff_parts[0].shape
    return order.run(
        8,
        weights_first_kernel,
        (place, n1, grads, weights, w_out, *ff_terms, *ff_parts),
        [sds((seq, dim), F32), sds(shape, BF16), sds(shape, BF16)]
        + [sds((1, rows // 4, dim), BF16)] * 4,
        [SMEM] + [VMEM] * 10,
        after,
        scratch_shapes=[pltpu.VMEM((1, rows, dim), BF16)],
    )


def weights_second_kernel(place, n1, grads, w_out, *refs):
    parts_r, refs = refs[:4], refs[4:]
    ff_own, ff_got, move_r, ff, *refs = refs
    parts, total = refs[:4], refs[4]
    width = grads.shape[0]
    move_r[...] = low_sum(*(part[...] for part in parts_r))
    ff[...] = low_sum(ff_own[...], ff_got[...])
    total[0, :width, :] = dot(grads[...], n1[...], NN).astype(BF16)
    total[0, width:, :] = w_out[...]
    scatter(place, total, parts)


def weights_second_call(order, place, n1, grads, w_out, parts_r, ff_terms):
    dim = n1.shape[1]
    rows = grads.shape[0] + w_out.shape[0]
    part = sds((1, rows // 4, dim), BF16)
    return order.run(
        6,
        weights_second_kernel,
        (place, n1, grads, w_out, *parts_r, *ff_terms),
        [part, sds(ff_terms[0].shape, BF16)] + [part] * 4,
        [SMEM] + [VMEM] * 9,
        scratch_shapes=[pltpu.VMEM((1, rows, dim), BF16)],
    )


def norm1_grad_kernel(block, place, logit_own, logit_got, qk0, seg_pad, n1, grads, weights, first, *refs):
    before, gain, shift, sums2, own, send, late, extra, extra_w, total_grad = refs
    select_back(
        block, place[0], logit_own, logit_got, qk0, seg_pad, n1, extra, extra_w, total_grad
    )
    half = own.shape[0]
    total = before[...] + dot(grads[...], weights[...], TT) + dot(extra[...], first[...], TT)
    for core in range(2):

        @pl.when(place[0] == core)
        def _():
            own[...] = total[core * half : (core + 1) * half]
            send[...] = total[(1 - core) * half : (2 - core) * half].astype(BF16)

    scaled = (n1[...].astype(F32) - shift[...]) * (1.0 / gain[...])
    gain_sum = jnp.sum(total * scaled, axis=0, keepdims=True)
    shift_sum = jnp.sum(total, axis=0, keepdims=True)
    norms = jnp.concatenate([gain_sum, shift_sum, sums2[0:2, :], sums2[4:8, :]], axis=0)
    rows = extra_w.shape[0]
    late[:rows, :] = extra_w[...]
    high, low = halves(norms)
    late[rows : rows + 8, :] = high
    late[rows + 8 :, :] = low


def norm1_grad_call(order, place, logits, qk0, seg_pad, n1, grads, weights, first, *rest):
    seq, dim = n1.shape
    rows = qk0.shape[0]
    return order.run(
        14,
        functools.partial(norm1_grad_kernel, 256),
        (place, *logits, qk0, seg_pad, n1, grads, weights, first, *rest),
        [
            sds((seq // 2, dim), F32),
            sds((seq // 2, dim), BF16),
            sds((rows + 16, dim), BF16),
        ],
        [SMEM] + [VMEM] * 12,
        scratch_shapes=[
            pltpu.VMEM((rows, seq), BF16),
            pltpu.VMEM((rows, dim), BF16),
            pltpu.VMEM((rows, seq), F32),
        ],
    )


def norm1_back_kernel(tokens, own, received, grad_hidden, gain, out):
    normed_grad = own[...] + received[...].astype(F32)
    scaled, inverse = normalize(tokens[...].astype(F32))
    total = grad_hidden[...] + norm_back(normed_grad, scaled, inverse, gain[...])
    out[...] = total.astype(BF16)


def norm1_back_call(order, tokens, own, received, grad_hidden, gain, after=()):
    size, dim = tokens.shape
    rows = rows_spec(size // 2, dim)
    return order.run(
        4,
        norm1_back_kernel,
        (tokens, own, received, grad_hidden, gain),
        sds(tokens.shape, BF16),
        [rows] * 4 + [whole((1, dim))],
        after,
        grid=(2,),
        out_specs=rows,
    )


def add_late(terms, out):
    def pairs(values):
        while len(values) > 1:
            values = [values[i] + values[i + 1] for i in range(0, len(values), 2)]
        return values[0]

    rows = out.shape[0] - 16
    out[:rows, :] = pairs([term[:rows, :].astype(F32) for term in terms]).astype(BF16)
    norms = pairs(
        [term[rows : rows + 8, :].astype(F32) + term[rows + 8 :, :].astype(F32) for term in terms]
    )
    high, low = halves(norms)
    out[rows : rows + 8, :] = high
    out[rows + 8 :, :] = low


def step1_kernel(late_own, late_got, *refs):
    at_terms, refs = refs[:5], refs[5:]
    ff_own, ff_got, both, ff = refs
    size = at_terms[0].shape[1]
    both[:size, :] = low_sum(*(term[0] for term in at_terms))
    add_late((late_own, late_got), both.at[size:, :])
    ff[...] = low_sum(ff_own[...], ff_got[...])


def step1_call(order, late_terms, at_terms, ff_terms):
    _, size, dim = at_terms[0].shape
    rows = size + late_terms[0].shape[0]
    return order.run(
        3.5,
        step1_kernel,
        (*late_terms, *at_terms, *ff_terms),
        [sds((rows, dim), BF16), sds(ff_terms[0].shape, BF16)],
    )


def step2_kernel(size, place, own, got, *refs):
    *ff_parts, both, ff = refs
    both[:size, :] = low_sum(own[:size, :], got[:size, :])
    add_late((own.at[size:, :], got.at[size:, :]), both.at[size:, :])
    gather(place, ff_parts, ff)


def step2_call(order, place, size, own, got, ff_parts, after=()):
    groups, rows, dim = ff_parts[0].shape
    return order.run(
        4.5,
        functools.partial(step2_kernel, size),
        (place, own, got, *ff_parts),
        [sds(own.shape, BF16), sds((groups, 4 * rows, dim), BF16)],
        [SMEM] + [VMEM] * 6,
        after,
    )


def step3_kernel(size, place, *refs):
    parts, refs = refs[:4], refs[4:]
    mixed, grad, both, mixed_out, grad_out = refs
    for partner, part in enumerate(parts):
        both[part_rows(quarter(place) ^ partner, size), :] = part[:size, :]
    add_late([part.at[size:, :] for part in parts], both.at[4 * size :, :])
    mixed_out[...] = mixed[...]
    grad_out[...] = grad[...]


def step3_call(order, place, size, parts, mixed, grad):
    rows, dim = parts[0].shape
    return order.run(
        3.5,
        functools.partial(step3_kernel, size),
        (place, *parts, mixed, grad),
        [sds((rows + 3 * size, dim), BF16), sds(mixed.shape, BF16), sds(grad.shape, BF16)],
        [SMEM] + [VMEM] * 6,
    )


def finish_attention_kernel(place, near, far, w_query, w_key, w_value, w_out, norms):
    width = w_out.shape[0] // 2
    late = 4 * width
    rows = late + 2 * HEAD_DIM
    total = jnp.zeros(norms.shape, F32)
    for ref in (near, far):
        total = total + (ref[rows : rows + 8, :].astype(F32) + ref[rows + 8 :, :].astype(F32))
    norms[...] = total
    extra = near[late:rows, :].astype(F32) + far[late:rows, :].astype(F32)
    extra = jnp.where(place[1] == 0, extra, 0.0)
    for core in range(2):

        @pl.when(place[0] == core)
        def _():
            low, high = (near, far) if core == 0 else (far, near)
            for i, out in enumerate((w_query, w_key, w_value)):
                piece = slice(i * width, (i + 1) * width)
                part = low[piece, :].astype(F32)
                if i < 2:
                    more = extra[i * HEAD_DIM : (i + 1) * HEAD_DIM]
                    part = jnp.concatenate([part[:HEAD_DIM] + more, part[HEAD_DIM:]], axis=0)
                out[...] = jnp.concatenate([part, high[piece, :].astype(F32)], axis=0).T
            w_out[:width, :] = low[3 * width : late, :].astype(F32)
            w_out[width:, :] = high[3 * width : late, :].astype(F32)


def finish_attention_call(order, place, width, near, far):
    dim = near.shape[1]
    return order.run(
        4.5,
        finish_attention_kernel,
        (place, near, far),
        [sds((dim, 2 * width), F32)] * 3 + [sds((2 * width, dim), F32), sds((8, dim), F32)],
        [SMEM] + [VMEM] * 2,
    )


def finish_mlp_kernel(place, near, far, w_up, w_down):
    units = near.shape[1]
    for core in range(2):

        @pl.when(place[0] == core)
        def _():
            low, high = (near, far) if core == 0 else (far, near)
            w_up[:, :units] = low[0].astype(F32)
            w_up[:, units:] = high[0].astype(F32)
            w_down[:units, :] = low[1].astype(F32)
            w_down[units:, :] = high[1].astype(F32)


def finish_mlp_call(order, place, near, far):
    _, units, dim = near.shape
    return order.run(
        6.8,
        finish_mlp_kernel,
        (place, near, far),
        [sds((dim, 2 * units), F32), sds((2 * units, dim), F32)],
        [SMEM] + [VMEM] * 2,
    )


def make_body(devices, parts):
    axes = ("dp", "tensor")
    chips = devices // 2
    in_order = [1 << bit for bit in range(chips.bit_length() - 1)]
    turned = [in_order[1], in_order[0], *in_order[2:]]
    rounds = len(in_order)
    rounds_more = range(3, rounds)

    def pairs(move):
        found = []
        for device in range(devices):
            for part in range(parts):
                to_chip, to_core, to_part = move(device // 2, device % 2, part)
                source = device * parts + part
                found.append((source, (to_chip * 2 + to_core) * parts + to_part))
        return found

    def by_bit(bit):
        return pairs(
            lambda chip, core, part: (chip ^ (turned if core else in_order)[bit], core, part)
        )

    by_role = pairs(lambda chip, core, part: (chip, part, core))
    by_core = pairs(lambda chip, core, part: (chip, 1 - core, part))
    by_part = pairs(lambda chip, core, part: (chip, core, 1 - part))
    from_first_part = [pair for pair in by_part if pair[0] % parts == 0]
    extra_to_first = [
        pair for pair in by_part if pair[0] % parts == 1 and (pair[0] // parts) % 2 == 0
    ]
    to_first_core = [pair for pair in by_core if (pair[0] // parts) % 2 == 1]
    by_chip = [by_bit(bit) for bit in range(rounds)]

    def by_quarter(partner):
        def across(chip, core, part):
            for bit in range(2):
                if partner >> (1 - bit) & 1:
                    chip ^= (turned if core else in_order)[bit]
            return chip, core, part

        return pairs(across)

    def move(value, how):
        return lax.ppermute(value, axes, how)

    def add_more(value):
        for bit in rounds_more:
            other = move(value, by_chip[bit])
            value = (value.astype(F32) + other.astype(F32)).astype(value.dtype)
        return value

    def exchange(values):
        return [values[0]] + [move(values[i], by_quarter(i)) for i in range(1, 4)]

    def body(
        tokens,
        segment_ids,
        pad_mask,
        norm1_gain,
        norm1_shift,
        w_query,
        w_key,
        w_value,
        w_out,
        norm2_gain,
        norm2_shift,
        w_up,
        w_down,
        cotangent,
    ):
        order = Order()
        device = lax.axis_index("dp")
        part = lax.axis_index("tensor")
        core = device % 2
        chip = device // 2
        bits = [
            jnp.where(core == 1, (chip & turned[i]) != 0, (chip & in_order[i]) != 0)
            for i in range(rounds)
        ]
        place = jnp.stack([core, part] + bits).astype(jnp.int32)
        gain1, shift1, gain2, shift2 = (
            vector[None, :] for vector in (norm1_gain, norm1_shift, norm2_gain, norm2_shift)
        )

        mine = move(tokens, by_role)
        ints = jnp.concatenate([segment_ids, pad_mask], axis=0)
        ints = jnp.where(core == part, ints, move(ints, by_core)).astype(F32)
        seg_pad = jnp.concatenate([ints, jnp.zeros((6, ints.shape[1]), F32)], axis=0)

        qkv_l, qkv_s, first = pack_first_call(order, place, w_query, w_key, w_value)
        first_moved = move(first, from_first_part)
        qkv_near = move(qkv_s, by_part)
        n1_own = norm1_call(order, mine, gain1, shift1)
        n1_other = move(n1_own, by_core)
        out_l, up_l, up_s, down_l, down_s, grad = pack_last_call(
            order, place, w_out, w_up, w_down, cotangent
        )
        out_r = move(out_l, by_part)
        up_near = move(up_s, by_part)
        grad_own = move(grad, by_role)
        down_near = move(down_s, by_part)
        n1, penalty, qk0, first = penalty_call(
            order, place, n1_own, n1_other, first, first_moved, seg_pad
        )
        (qkv_near,) = order.hold((qkv_near,), (penalty,))
        qkv_far = move(qkv_near, by_chip[0])
        qkvt_l, heads_l, lse_l = forward_call(order, n1, (qkv_l,), penalty)
        qkvt_r, heads_r, lse_r, qkv_r = forward_call(
            order, n1, (qkv_near, qkv_far), penalty, place, after=(up_near,)
        )
        (up_near,) = order.hold((up_near,), (lse_r,))
        up_far = move(up_near, by_chip[0])
        (grad_own,) = order.hold((grad_own,), (lse_r,))
        grad_other = move(grad_own, by_core)
        own, send = project_call(order, place, heads_l, heads_r, out_l, out_r, after=(down_near,))
        (down_near,) = order.hold((down_near,), (send,))
        down_far = move(down_near, by_chip[0])
        hidden, n2_own = norm2_call(order, mine, own, move(send, by_core), gain2, shift2)
        n2_other = move(n2_own, by_core)
        *before, keep, send = mlp_call(
            order, place, n2_other, n2_own, grad_other, grad_own, (up_l, down_l)
        )
        got = move(send, by_chip[0])
        weights = (up_near, up_far, down_near, down_far)
        mixed_send, mixed_own, back_send, back_own, *ff_r = mlp_call(
            order, place, n2_other, n2_own, grad_other, grad_own, weights, before
        )
        back_send, mixed_send, *ff_r = order.hold((back_send, mixed_send, *ff_r), (got,))
        ff_r = exchange(ff_r)
        grad_hidden, low_own, sums2 = norm2_back_call(
            order, hidden, back_own, move(back_send, by_core), grad_own, gain2
        )
        low_other = move(low_own, by_core)
        mixed, keep, send = mixed_call(
            order, place, hidden, mixed_own, move(mixed_send, by_core), keep, got
        )
        mixed = move(mixed, by_role)
        got = move(send, by_chip[1])

        low = (low_own, low_other)
        grads_r, wo_r, logit_sum = backward_call(
            order, place, *low, out_r, heads_r, qkvt_r, lse_r, penalty
        )
        back, ff, ff_move, *at_r = weights_first_call(
            order, place, n1, grads_r, qkv_r, wo_r, (keep, got), ff_r, (mixed,)
        )
        ff_got = move(ff_move, by_part)
        at_r = exchange(at_r)
        grads_l, wo_l, logit_sum = backward_call(
            order, place, *low, out_l, heads_l, qkvt_l, lse_l, penalty, logit_sum
        )
        logit_got = move(logit_sum, to_first_core)
        at_r, ff, *at = weights_second_call(
            order, place, n1, grads_l, wo_l, at_r, (ff, ff_got)
        )
        at_r = move(at_r, by_part)
        ff_got = move(ff, by_chip[2])
        at = exchange(at)
        own, send, late = norm1_grad_call(
            order,
            place,
            (logit_sum, logit_got),
            qk0,
            seg_pad,
            n1,
            grads_l,
            qkv_l,
            first,
            back,
            gain1,
            shift1,
            sums2,
        )
        send, late = order.hold((send, late), (*at, at_r))
        received = move(send, by_core)
        late_got = move(late, by_part)
        both, ff = step1_call(order, (late, late_got), (*at, at_r), (ff, ff_got))
        size = at_r.shape[1]
        both_got = move(both, by_chip[2])
        ff = exchange([add_more(ff)] * 4)
        tokens_grad = norm1_back_call(order, mine, own, received, grad_hidden, gain1)
        tokens_grad = move(tokens_grad, by_role)
        both, ff = step2_call(order, place, size, both, both_got, ff)
        both = exchange([add_more(both)] * 4)
        ff_far = move(ff, by_core)
        up_grad, down_grad = finish_mlp_call(order, place, ff, ff_far)
        both, mixed, tokens_grad = step3_call(order, place, size, both, mixed, tokens_grad)
        query_grad, key_grad, value_grad, out_grad, norms = finish_attention_call(
            order, place, size, both, move(both, by_core)
        )
        return (
            mixed,
            tokens_grad,
            norms[0],
            norms[1],
            query_grad,
            key_grad,
            value_grad,
            out_grad,
            norms[2],
            norms[3],
            up_grad,
            down_grad,
        )

    return body


def solution(mesh):
    in_specs = (
        P(("dp", "tensor"), None),
        P("dp", None),
        P("dp", None),
        P(),
        P(),
        P(None, "tensor"),
        P(None, "tensor"),
        P(None, "tensor"),
        P("tensor", None),
        P(),
        P(),
        P(None, "tensor"),
        P("tensor", None),
        P(("dp", "tensor"), None),
    )
    out_specs = (
        P(("dp", "tensor"), None),
        P(("dp", "tensor"), None),
        P(),
        P(),
        P(None, "tensor"),
        P(None, "tensor"),
        P(None, "tensor"),
        P("tensor", None),
        P(),
        P(),
        P(None, "tensor"),
        P("tensor", None),
    )
    body = make_body(mesh.shape["dp"], mesh.shape["tensor"])
    return jax.shard_map(body, mesh=mesh, in_specs=in_specs, out_specs=out_specs, check_vma=False)
```

time: 333 us -> 318 us (0.955)
  waiting for transfers between devices: 47.6 us -> 68.4 us
  Pallas kernels: 186 us -> 167 us
  starting transfers between devices: 70.8 us -> 60.8 us
  local copies, waits for them, and re-layouts: 21.7 us -> 15.2 us
    ppermute x46, waiting for transfers between devices: 47.6 us -> 68.4 us  [move(): return lax.ppermute(value, axes, how)]
    pallas_call x29 -> x23, Pallas kernels: 186 us -> 167 us  [run(): pl.pallas_call(body, out_shape=out_shape, in_specs=in_specs, compiler_par...]
    ppermute x46, starting transfers between devices: 70.8 us -> 60.8 us  [move(): return lax.ppermute(value, axes, how)]
    unnamed x58 -> x46, local copies, waits for them, and re-layouts: 13.8 us -> 10.1 us
  transfers between devices with their start and end apart: 46 -> 46, of which waited for: 10 -> 13; matrix products, arithmetic and copies ran while one was open for 2% -> 1% of each run, Pallas kernels for 48% -> 47%
where the time goes in v3:
time: 318 us; the launch traced here: 313 us
  Pallas kernels  167 us (53%)
  waiting for transfers between devices  68.4 us (22%)
  starting transfers between devices  60.8 us (19%)
  local copies, waits for them, and re-layouts  15.2 us (5%)
    pallas_call x23, Pallas kernels, run(): pl.pallas_call(body, out_shape=out_shape, in_specs=in_specs, compiler_par...  167 us
    ppermute x46, waiting for transfers between devices, move(): return lax.ppermute(value, axes, how)  68.4 us
    ppermute x46, starting transfers between devices, move(): return lax.ppermute(value, axes, how)  60.8 us
    unnamed x46, local copies, waits for them, and re-layouts  10.1 us
  transfers between devices with their start and end apart: 46, of which 13 were waited for; matrix products, arithmetic and copies ran while one was open for 1% of the time, Pallas kernels for 47%

profile of v3, /device:TPU:1, one launch (start us, length us, event | category | flops | bytes accessed | tf_op | source)
XLA Modules:
  0.0 313.3 jit_solution(13722323080087427624)
XLA Ops:
  1.5 4.5 %collective-permute-start = (bf16[512,768]{1,0:T(8,128)(2,1)}, bf16[512,768]{1,0:T(8,128)(2,1)S(1)}, u32[]{:S(2)}, u32[]{:S(2)}) collective-permute-start(bf16[512,768]{1,0:T(8,128)(2,1)} %param.14), channel_id=1, source_target_pairs={{0,0},{1,2},{2,1},{3,3},{4,4},{5,6},{6,5},{7,7},{8,8},{9,10},{10,9... | collective-permute-start | bytes 2359304 | tf_op jit(solution)/shard_map/ppermute | solution.py:1029
  6.7 3.1 shard_map.229
  9.8 2.5 collective-permute-start.2
  14.1 3.2 %collective-permute-done.refs_0_ = bf16[512,768]{1,0:T(8,128)(2,1)S(1)} collective-permute-done((bf16[512,768]{1,0:T(8,128)(2,1)}, bf16[512,768]{1,0:T(8,128)(2,1)S(1)}, u32[]{:S(2)}, u32[]{:S(2)}) %collective-permute-start) | collective-permute-done | bytes 786464 | tf_op jit(solution)/shard_map/ppermute | solution.py:1029
  18.3 2.6 shard_map.230.refs_5_.refs_1_
  20.9 5.1 %shard_map.231 = (bf16[192,768]{1,0:T(8,128)(2,1)}, bf16[768,768]{1,0:T(8,128)(2,1)}, bf16[384,768]{1,0:T(8,128)(2,1)}, bf16[768,768]{1,0:T(8,128)(2,1)}, bf16[3...) custom-call(s32[5]{0:T(128)} %stack.35.refs_0_, bf16[384,768]{1,0:T(8,128)(2,1)} %refs_1_.3, bf16[768,1536]{1,0:T(8,128)(2,1)} %refs_2_.3, ...), custom_call_target="tpu_custom_call" | custom-call | flops 115000000512 | tf_op jit(solution)/shard_map/pallas_call | solution.py:60
  26.0 2.5 collective-permute-start.7
  28.5 1.4 collective-permute-start.8
  30.0 2.4 collective-permute-start.11
  32.4 6.5 %shard_map.232 = (bf16[1024,768]{1,0:T(8,128)(2,1)}, f32[1024,1024]{1,0:T(8,128)}, bf16[128,1024]{1,0:T(8,128)(2,1)}, bf16[768,128]{1,0:T(8,128)(2,1)}) custom-call(s32[5]{0:T(128)} %stack.35.refs_0_, bf16[512,768]{1,0:T(8,128)(2,1)} %shard_map.230.refs_5_.refs_1_, bf16[512,768]{1,0:T(8,128)(2,1)} %copy-done.14, ...), custom_call_target="tpu_custom_call" | custom-call | flops 149500002304 | tf_op jit(solution)/shard_map/pallas_call | solution.py:60
  38.9 1.6 collective-permute-start.5
  40.5 9.2 %shard_map.233 = (bf16[576,1024]{1,0:T(8,128)(2,1)}, bf16[192,1024]{1,0:T(8,128)(2,1)}, f32[3,1,1024]{2,1,0:T(1,128)}) custom-call(bf16[1024,768]{1,0:T(8,128)(2,1)} %get-tuple-element.102.refs_0_.refs_1_.refs_5_, bf16[768,576]{1,0:T(8,128)(2,1)} %get-tuple-element.103.refs_1_.refs_7_, f32[1024,1024]{1,0:T(8,128)} %get-tuple-element.104.refs_2_.refs_1_.refs_4_.refs_7_, ...), custom_call_target="tpu_custom_call" | custom-call | flops 213900001280 | tf_op jit(solution)/shard_map/pallas_call | solution.py:60
  49.7 9.4 %shard_map.235 = (bf16[576,1024]{1,0:T(8,128)(2,1)}, bf16[192,1024]{1,0:T(8,128)(2,1)}, f32[3,1,1024]{2,1,0:T(1,128)}, bf16[768,576]{1,0:T(8,128)(2,1)}) custom-call(s32[5]{0:T(128)} %stack.35.refs_0_, bf16[1024,768]{1,0:T(8,128)(2,1)} %get-tuple-element.102.refs_0_.refs_1_.refs_5_, bf16[384,576]{1,0:T(8,128)(2,1)} %shard_map.234.refs_2_, ...), custom_call_target="tpu_custom_call" | custom-call | flops 213900001280 | tf_op jit(solution)/shard_map/pallas_call | solution.py:60
  59.2 2.4 collective-permute-done.8.refs_5_.refs_0_
  61.6 3.5 %shard_map.236 = (f32[512,768]{1,0:T(8,128)}, bf16[512,768]{1,0:T(8,128)(2,1)}) custom-call(s32[5]{0:T(128)} %stack.35.refs_0_, bf16[192,1024]{1,0:T(8,128)(2,1)} %get-tuple-element.106.refs_1_.refs_4_, bf16[192,1024]{1,0:T(8,128)(2,1)} %get-tuple-element.110.refs_2_.refs_4_, bf16[192,768]{1,0:T(8,128)(2,1)} %get-tuple-element.111.refs_3_, ...), custom_call_target="tpu_custom_call" | custom-call | flops 80499998720 | tf_op jit(solution)/shard_map/pallas_call | solution.py:60
  65.0 2.9 collective-permute-start.9
  69.1 0.9 collective-permute-done.11.refs_0_
  70.9 4.2 %shard_map.237 = (f32[512,768]{1,0:T(8,128)}, bf16[512,768]{1,0:T(8,128)(2,1)}) custom-call(bf16[512,768]{1,0:T(8,128)(2,1)} %copy-done.9, f32[512,768]{1,0:T(8,128)} %get-tuple-element.114.refs_1_, bf16[512,768]{1,0:T(8,128)(2,1)} %copy-done.17, f32[1,768]{1,0:T(1,128)} %broadcast_in_dim.15.refs_3_.refs_4_, f32[1,768]{1,0:T(1,128)} %broadcast_in_dim.16.refs_4_, ...), custom_call_target="tpu_custom_call" | custom-call | flops 92000002048 | tf_op jit(solution)/shard_map/pallas_call | solution.py:60
  75.6 1.3 collective-permute-start.13
  78.6 14.7 %shard_map.241 = (f32[512,768]{1,0:T(8,128)}, f32[512,768]{1,0:T(8,128)}, f32[512,768]{1,0:T(8,128)}, f32[512,768]{1,0:T(8,128)}, bf16[2,384,768]{2,1,0:T(8,128)(2,1)}, /*index=5*/bf16[2,384,768]{2,1,0:T(8,128)(2,1)}) custom-call(s32[5]{0:T(128)} %stack.35.refs_0_, bf16[512,768]{1,0:T(8,128)(2,1)} %copy-done.12, ...), custom_call_target="tpu_custom_call" | custom-call | flops 335800008704 | tf_op jit(solution)/shard_map/pallas_call | solution.py:60
  93.3 1.4 collective-permute-start.15
  94.7 16.2 %shard_map.242 = (bf16[512,768]{1,0:T(8,128)(2,1)}, f32[512,768]{1,0:T(8,128)}, bf16[512,768]{1,0:T(8,128)(2,1)}, f32[512,768]{1,0:T(8,128)}, bf16[2,192,768]{2,...) custom-call(s32[5]{0:T(128)} %stack.35.refs_0_, ...), custom_call_target="tpu_custom_call" | custom-call | flops 335800008704 | tf_op jit(solution)/shard_map/pallas_call | solution.py:60
  113.1 1.1 collective-permute-start.22
  114.2 0.9 collective-permute-start.18
  115.1 0.9 copy-done.16
  116.0 4.9 %shard_map.244 = (f32[512,768]{1,0:T(8,128)}, bf16[512,768]{1,0:T(8,128)(2,1)}, f32[8,768]{1,0:T(8,128)}) custom-call(f32[512,768]{1,0:T(8,128)} %get-tuple-element.116.refs_0_.refs_1_, f32[512,768]{1,0:T(8,128)} %get-tuple-element.126.refs_1_, bf16[512,768]{1,0:T(8,128)(2,1)} %copy-done.16, bf16[512,768]{1,0:T(8,128)(2,1)} %shard_map.238.refs_4_.refs_3_, ...), custom_call_target="tpu_custom_call" | custom-call | flops 115000000512 | tf_op jit(solution)/shard_map/pallas_call | solution.py:60
  121.9 4.9 %shard_map.245 = (bf16[512,768]{1,0:T(8,128)(2,1)}, bf16[2,192,768]{2,1,0:T(8,128)(2,1)}, bf16[2,192,768]{2,1,0:T(8,128)(2,1)}) custom-call(s32[5]{0:T(128)} %stack.35.refs_0_, f32[512,768]{1,0:T(8,128)} %get-tuple-element.116.refs_0_.refs_1_, f32[512,768]{1,0:T(8,128)} %get-tuple-element.138.refs_2_, bf16[512,768]{1,0:T(8,128)(2,1)} %copy-done.15, ...), custom_call_target="tpu_custom_call" | custom-call | flops 92000002048 | tf_op jit(solution)/shard_map/pallas_call | solution.py:60
  126.8 1.1 collective-permute-start.19
  127.9 5.2 %collective-permute-start.23 = (bf16[512,768]{1,0:T(8,128)(2,1)}, bf16[512,768]{1,0:T(8,128)(2,1)}, u32[]{:S(2)}, u32[]{:S(2)}) collective-permute-start(bf16[512,768]{1,0:T(8,128)(2,1)} %get-tuple-element.150), channel_id=1, source_target_pairs={{0,0},{1,2},{2,1},{3,3},{4,4},{5,6},{6,5},{7,7},{8,8},{9,10},{10,9... | collective-permute-start | bytes 2359304 | tf_op jit(solution)/shard_map/ppermute | solution.py:1029
  133.0 15.1 %shard_map.246 = (bf16[576,1024]{1,0:T(8,128)(2,1)}, bf16[192,768]{1,0:T(8,128)(2,1)}, f32[1024,1024]{1,0:T(8,128)}) custom-call(s32[5]{0:T(128)} %stack.35.refs_0_, bf16[512,768]{1,0:T(8,128)(2,1)} %get-tuple-element.135.refs_1_, bf16[512,768]{1,0:T(8,128)(2,1)} %copy-done.10, bf16[192,768]{1,0:T(8,128)(2,1)} %collective-permute-done.7.refs_4_.refs_3_, ...), custom_call_target="tpu_custom_call" | custom-call | flops 390999998464 | tf_op jit(solution)/shard_map/pallas_call | solution.py:60
  148.2 7.7 %shard_map.247 = (f32[1024,768]{1,0:T(8,128)}, bf16[2,192,768]{2,1,0:T(8,128)(2,1)}, bf16[2,192,768]{2,1,0:T(8,128)(2,1)}, bf16[1,192,768]{2,1,0:T(8,128)(2,1)},...) custom-call(s32[5]{0:T(128)} %stack.35.refs_0_, ...), custom_call_target="tpu_custom_call" | custom-call | flops 184000004096 | tf_op jit(solution)/shard_map/pallas_call | solution.py:60
  156.2 1.1 collective-permute-start.26
  157.3 1.3 collective-permute-start.27
  158.6 4.7 %collective-permute-start.28 = (bf16[2,192,768]{2,1,0:T(8,128)(2,1)}, bf16[2,192,768]{2,1,0:T(8,128)(2,1)}, u32[]{:S(2)}, u32[]{:S(2)}) collective-permute-start(bf16[2,192,768]{2,1,0:T(8,128)(2,1)} %get-tuple-element.161), channel_id=1, source_target_pairs={{0,1},{1,0},{2,3},{3,2},{4,5},{5,4},{6,7},{7,6},{8,9},{9,8},{10,11... | collective-permute-start | bytes 1769480 | tf_op jit(solution)/shard_map/ppermute | solution.py:1029
  163.3 16.3 %shard_map.248 = (bf16[576,1024]{1,0:T(8,128)(2,1)}, bf16[192,768]{1,0:T(8,128)(2,1)}, bf16[1024,1024]{1,0:T(8,128)(2,1)}) custom-call(s32[5]{0:T(128)} %stack.35.refs_0_, bf16[512,768]{1,0:T(8,128)(2,1)} %get-tuple-element.135.refs_1_, bf16[512,768]{1,0:T(8,128)(2,1)} %copy-done.10, bf16[192,768]{1,0:T(8,128)(2,1)} %get-tuple-element.111.refs_3_, ...), custom_call_target="tpu_custom_call" | custom-call | flops 390999998464 | tf_op jit(solution)/shard_map/pallas_call | solution.py:60
  179.6 1.6 collective-permute-start.24
  181.3 5.0 %shard_map.249 = (bf16[1,192,768]{2,1,0:T(8,128)(2,1)}, bf16[2,192,768]{2,1,0:T(8,128)(2,1)}, bf16[1,192,768]{2,1,0:T(8,128)(2,1)}, bf16[1,192,768]{2,1,0:T(8,12...) custom-call(s32[5]{0:T(128)} %stack.35.refs_0_, ...), custom_call_target="tpu_custom_call" | custom-call | flops 138000007168 | tf_op jit(solution)/shard_map/pallas_call | solution.py:60
  186.7 1.3 collective-permute-start.30
  188.0 1.4 collective-permute-start.32
  189.4 1.4 collective-permute-start.31
  190.8 2.3 collective-permute-start.34
  193.1 12.6 %shard_map.250 = (f32[512,768]{1,0:T(8,128)}, bf16[512,768]{1,0:T(8,128)(2,1)}, bf16[144,768]{1,0:T(8,128)(2,1)}) custom-call(s32[5]{0:T(128)} %stack.35.refs_0_, bf16[1024,1024]{1,0:T(8,128)(2,1)} %get-tuple-element.152.refs_10_.refs_1_, bf16[1024,1024]{1,0:T(8,128)(2,1)} %copy-done.7, bf16[128,1024]{1,0:T(8,128)(2,1)} %get-tuple-element.153.refs_3_, ...), custom_call_target="tpu_custom_call" | custom-call | flops 321999994880 | tf_op jit(solution)/shard_map/pallas_call | solution.py:60
  205.7 5.3 %collective-permute-done.31.refs_5_ = bf16[1,192,768]{2,1,0:T(8,128)(2,1)} collective-permute-done((bf16[1,192,768]{2,1,0:T(8,128)(2,1)}, bf16[1,192,768]{2,1,0:T(8,128)(2,1)}, u32[]{:S(2)}, u32[]{:S(2)}) %collective-permute-start.31) | collective-permute-done | bytes 294944 | tf_op jit(solution)/shard_map/ppermute | solution.py:1029
  210.9 3.5 %collective-permute-start.33 = (bf16[144,768]{1,0:T(8,128)(2,1)}, bf16[144,768]{1,0:T(8,128)(2,1)S(1)}, u32[]{:S(2)}, u32[]{:S(2)}) collective-permute-start(bf16[144,768]{1,0:T(8,128)(2,1)} %get-tuple-element.169.refs_0_.refs_9_), channel_id=1, source_target_pairs={{0,1},{1,0},{2,3},{3,2},{4,5},{5,4},{6,7},{7,6},{8,9},{9,8},{10,11... | collective-permute-start | bytes 663560 | tf_op jit(solution)/shard_map/ppermute | solution.py:1029
  214.4 4.8 %collective-permute-done.34.refs_8_ = bf16[2,192,768]{2,1,0:T(8,128)(2,1)} collective-permute-done((bf16[2,192,768]{2,1,0:T(8,128)(2,1)}, bf16[2,192,768]{2,1,0:T(8,128)(2,1)}, u32[]{:S(2)}, u32[]{:S(2)}) %collective-permute-start.34) | collective-permute-done | bytes 589856 | tf_op jit(solution)/shard_map/ppermute | solution.py:1029
  220.4 3.1 shard_map.252
  223.5 3.1 %collective-permute-start.37 = (bf16[2,192,768]{2,1,0:T(8,128)(2,1)}, bf16[2,192,768]{2,1,0:T(8,128)(2,1)S(1)}, u32[]{:S(2)}, u32[]{:S(2)}) collective-permute-start(bf16[2,192,768]{2,1,0:T(8,128)(2,1)} %get-tuple-element.172.refs_5_.refs_3_), channel_id=1, source_target_pairs={{0,4},{1,5},{2,10},{3,11},{4,0},{5,1},{6,14},{7,15},{8,12},{9,13},... | collective-permute-start | bytes 1769480 | tf_op jit(solution)/shard_map/ppermute | solution.py:1029
  226.7 0.9 copy-done.13
  227.6 3.6 %shard_map.253.refs_7_ = bf16[512,768]{1,0:T(8,128)(2,1)} custom-call(bf16[512,768]{1,0:T(8,128)(2,1)} %copy-done.9, f32[512,768]{1,0:T(8,128)} %get-tuple-element.173.refs_1_, bf16[512,768]{1,0:T(8,128)(2,1)} %copy-done.13, f32[512,768]{1,0:T(8,128)} %get-tuple-element.175.refs_3_, f32[1,768]{1,0:T(1,128)} %broadcast_in_dim.13.refs_1_.refs_10_.refs_4_, ...), custom_call_target="tpu_custom_call" | custom-call | flops 92000002048 | tf_op jit(solution)/shard_map/pallas_call | solution.py:60
  231.2 28.1 %collective-permute-done.35.refs_2_ = bf16[336,768]{1,0:T(8,128)(2,1)S(1)} collective-permute-done((bf16[336,768]{1,0:T(8,128)(2,1)}, bf16[336,768]{1,0:T(8,128)(2,1)S(1)}, u32[]{:S(2)}, u32[]{:S(2)}) %collective-permute-start.35) | collective-permute-done | bytes 516128 | tf_op jit(solution)/shard_map/ppermute | solution.py:1029
  259.3 4.3 %collective-permute-done.37.refs_5_ = bf16[2,192,768]{2,1,0:T(8,128)(2,1)S(1)} collective-permute-done((bf16[2,192,768]{2,1,0:T(8,128)(2,1)}, bf16[2,192,768]{2,1,0:T(8,128)(2,1)S(1)}, u32[]{:S(2)}, u32[]{:S(2)}) %collective-permute-start.37) | collective-permute-done | bytes 589856 | tf_op jit(solution)/shard_map/ppermute | solution.py:1029
  265.2 3.7 %shard_map.254 = (bf16[336,768]{1,0:T(8,128)(2,1)}, bf16[2,768,768]{2,1,0:T(8,128)(2,1)}) custom-call(s32[5]{0:T(128)} %stack.35.refs_0_, bf16[336,768]{1,0:T(8,128)(2,1)} %get-tuple-element.171.refs_1_, bf16[336,768]{1,0:T(8,128)(2,1)} %copy-done.21, bf16[2,192,768]{2,1,0:T(8,128)(2,1)} %get-tuple-element.172.refs_5_.refs_3_, ...), custom_call_target="tpu_custom_call" | custom-call | flops 103499997184 | tf_op jit(solution)/shard_map/pallas_call | solution.py:60
  269.4 3.1 collective-permute-start.43
  272.6 1.2 collective-permute-start.41
  273.8 1.4 collective-permute-start.40
  275.2 1.4 copy-done.6
  276.6 6.7 %shard_map.255 = (f32[768,1536]{1,0:T(8,128)}, f32[1536,768]{1,0:T(8,128)}) custom-call(s32[5]{0:T(128)} %stack.35.refs_0_, bf16[2,768,768]{2,1,0:T(8,128)(2,1)} %get-tuple-element.177.refs_1_.refs_3_, bf16[2,768,768]{2,1,0:T(8,128)(2,1)} %copy-done.6, bf16[2,768,768]{2,1,0:T(8,128)(2,1)} %get-tuple-element.177.refs_1_.refs_3_), custom_call_target="tpu_custom_call" | custom-call | flops 156399992832 | tf_op jit(solution)/shard_map/pallas_call | solution.py:60
  283.4 9.9 %collective-permute-done.41.refs_3_ = bf16[336,768]{1,0:T(8,128)(2,1)} collective-permute-done((bf16[336,768]{1,0:T(8,128)(2,1)}, bf16[336,768]{1,0:T(8,128)(2,1)}, u32[]{:S(2)}, u32[]{:S(2)}) %collective-permute-start.41) | collective-permute-done | bytes 516128 | tf_op jit(solution)/shard_map/ppermute | solution.py:1029
  293.3 5.2 %collective-permute-done.40.refs_2_ = bf16[336,768]{1,0:T(8,128)(2,1)} collective-permute-done((bf16[336,768]{1,0:T(8,128)(2,1)}, bf16[336,768]{1,0:T(8,128)(2,1)}, u32[]{:S(2)}, u32[]{:S(2)}) %collective-permute-start.40) | collective-permute-done | bytes 516128 | tf_op jit(solution)/shard_map/ppermute | solution.py:1029
  298.5 3.8 %shard_map.256 = (bf16[912,768]{1,0:T(8,128)(2,1)}, bf16[512,768]{1,0:T(8,128)(2,1)}, bf16[512,768]{1,0:T(8,128)(2,1)}) custom-call(s32[5]{0:T(128)} %stack.35.refs_0_, bf16[336,768]{1,0:T(8,128)(2,1)} %get-tuple-element.176.refs_1_, bf16[336,768]{1,0:T(8,128)(2,1)} %collective-permute-done.40.refs_2_, bf16[336,768]{1,0:T(8,128)(2,1)} %collective-permute-done.41.refs_3_, ...), custom_call_target="tpu_custom_call" | custom-call | flops 80499998720 | tf_op jit(solution)/shard_map/pallas_call | solution.py:60
  302.8 3.0 collective-permute-done.45.refs_2_
  305.8 1.1 copy-done.8
  306.9 4.7 %shard_map.257 = (f32[768,384]{1,0:T(8,128)}, f32[768,384]{1,0:T(8,128)}, f32[768,384]{1,0:T(8,128)}, f32[384,768]{1,0:T(8,128)}, f32[8,768]{1,0:T(8,128)}) custom-call(s32[5]{0:T(128)} %stack.35.refs_0_, bf16[912,768]{1,0:T(8,128)(2,1)} %get-tuple-element.181.refs_1_, bf16[912,768]{1,0:T(8,128)(2,1)} %copy-done.8, bf16[512,768]{1,0:T(8,128)(2,1)} %get-tuple-element.89.refs_3_), custom_call_target="tpu_custom_call" | custom-call | flops 103499997184 | tf_op jit(solution)/shard_map/pallas_call | solution.py:60
  311.6 1.5 slice_reduce_fusion
  (112 shorter events, 16.3 us)
Async XLA Ops:
  1.4 12.1 %collective-permute-start.3 = (s32[2,1024]{1,0:T(2,128)S(1)}, s32[2,1024]{1,0:T(2,128)S(1)}, u32[]{:S(2)}, u32[]{:S(2)}) collective-permute-start(s32[2,1024]{1,0:T(2,128)S(1)} %pad_add_fusion), channel_id=1, source_target_pairs={{0,2},{1,3},{2,0},{3,1},{4,6},{5,7},{6,4},{7,5},{8,10},{9,11},{10,... | collective-permute-start | bytes 24584 | tf_op jit(solution)/shard_map/ppermute | solution.py:1029
  1.5 15.9 %collective-permute-start = (bf16[512,768]{1,0:T(8,128)(2,1)}, bf16[512,768]{1,0:T(8,128)(2,1)S(1)}, u32[]{:S(2)}, u32[]{:S(2)}) collective-permute-start(bf16[512,768]{1,0:T(8,128)(2,1)} %param.14), channel_id=1, source_target_pairs={{0,0},{1,2},{2,1},{3,3},{4,4},{5,6},{6,5},{7,7},{8,8},{9,10},{10,9... | collective-permute-start | bytes 2359304 | tf_op jit(solution)/shard_map/ppermute | solution.py:1029
  6.7 5.6 %copy-start.2 = (f32[768]{0:T(1024)S(1)}, f32[768]{0:T(1024)}, u32[]{:S(2)}) copy-start(f32[768]{0:T(1024)} %param.17) | copy-start | bytes 9220
  6.7 6.2 %copy-start.3 = (f32[768]{0:T(1024)S(1)}, f32[768]{0:T(1024)}, u32[]{:S(2)}) copy-start(f32[768]{0:T(1024)} %param.18) | copy-start | bytes 9220
  6.7 6.8 %copy-start = (s32[1,1024]{1,0:T(1,128)S(1)}, s32[1,1024]{1,0:T(1,128)}, u32[]{:S(2)}) copy-start(s32[1,1024]{1,0:T(1,128)} %param.16) | copy-start | bytes 12292
  6.7 6.8 %copy-start.1 = (s32[1,1024]{1,0:T(1,128)S(1)}, s32[1,1024]{1,0:T(1,128)}, u32[]{:S(2)}) copy-start(s32[1,1024]{1,0:T(1,128)} %param.15) | copy-start | bytes 12292
  9.8 18.7 %collective-permute-start.2 = (bf16[768,128]{1,0:T(8,128)(2,1)}, bf16[768,128]{1,0:T(8,128)(2,1)}, u32[]{:S(2)}, u32[]{:S(2)}) collective-permute-start(bf16[768,128]{1,0:T(8,128)(2,1)} %get-tuple-element.100.refs_3_), channel_id=1, source_target_pairs={{0,1},{2,3},{4,5},{6,7},{8,9},{10,11},{12,13},{14,15},{16,17},{18,... | collective-permute-start | bytes 589832 | tf_op jit(solution)/shard_map/ppermute | solution.py:1029
  12.3 26.6 %collective-permute-start.4 = (bf16[384,576]{1,0:T(8,128)(2,1)}, bf16[384,576]{1,0:T(8,128)(2,1)}, u32[]{:S(2)}, u32[]{:S(2)}) collective-permute-start(bf16[384,576]{1,0:T(8,128)(2,1)} %get-tuple-element.107), channel_id=1, source_target_pairs={{0,1},{1,0},{2,3},{3,2},{4,5},{5,4},{6,7},{7,6},{8,9},{9,8},{10,11... | collective-permute-start | bytes 1327112 | tf_op jit(solution)/shard_map/ppermute | solution.py:1029
  17.4 0.9 copy-start.9
  20.9 9.1 %collective-permute-start.1 = (bf16[512,768]{1,0:T(8,128)(2,1)}, bf16[512,768]{1,0:T(8,128)(2,1)S(1)}, u32[]{:S(2)}, u32[]{:S(2)}) collective-permute-start(bf16[512,768]{1,0:T(8,128)(2,1)} %shard_map.230.refs_5_.refs_1_), channel_id=1, source_target_pairs={{0,2},{1,3},{2,0},{3,1},{4,6},{5,7},{6,4},{7,5},{8,10},{9,11},{10,... | collective-permute-start | bytes 2359304 | tf_op jit(solution)/shard_map/ppermute | solution.py:1029
  26.0 33.2 %collective-permute-start.7 = (bf16[192,768]{1,0:T(8,128)(2,1)}, bf16[192,768]{1,0:T(8,128)(2,1)}, u32[]{:S(2)}, u32[]{:S(2)}) collective-permute-start(bf16[192,768]{1,0:T(8,128)(2,1)} %get-tuple-element.111.refs_3_), channel_id=1, source_target_pairs={{0,1},{1,0},{2,3},{3,2},{4,5},{5,4},{6,7},{7,6},{8,9},{9,8},{10,11... | collective-permute-start | bytes 884744 | tf_op jit(solution)/shard_map/ppermute | solution.py:1029
  28.5 21.2 %collective-permute-start.6 = (bf16[384,768]{1,0:T(8,128)(2,1)}, bf16[384,768]{1,0:T(8,128)(2,1)}, u32[]{:S(2)}, u32[]{:S(2)}) collective-permute-start(bf16[384,768]{1,0:T(8,128)(2,1)} %get-tuple-element.108), channel_id=1, source_target_pairs={{0,1},{1,0},{2,3},{3,2},{4,5},{5,4},{6,7},{7,6},{8,9},{9,8},{10,11... | collective-permute-start | bytes 1769480 | tf_op jit(solution)/shard_map/ppermute | solution.py:1029
  28.5 33.0 %collective-permute-start.8 = (bf16[384,768]{1,0:T(8,128)(2,1)}, bf16[384,768]{1,0:T(8,128)(2,1)}, u32[]{:S(2)}, u32[]{:S(2)}) collective-permute-start(bf16[384,768]{1,0:T(8,128)(2,1)} %get-tuple-element.112), channel_id=1, source_target_pairs={{0,1},{1,0},{2,3},{3,2},{4,5},{5,4},{6,7},{7,6},{8,9},{9,8},{10,11... | collective-permute-start | bytes 1769480 | tf_op jit(solution)/shard_map/ppermute | solution.py:1029
  30.0 2.4 copy-start.14
  30.0 40.0 %collective-permute-start.11 = (bf16[512,768]{1,0:T(8,128)(2,1)}, bf16[512,768]{1,0:T(8,128)(2,1)}, u32[]{:S(2)}, u32[]{:S(2)}) collective-permute-start(bf16[512,768]{1,0:T(8,128)(2,1)} %get-tuple-element.101.refs_6_), channel_id=1, source_target_pairs={{0,0},{1,2},{2,1},{3,3},{4,4},{5,6},{6,5},{7,7},{8,8},{9,10},{10,9... | collective-permute-start | bytes 2359304 | tf_op jit(solution)/shard_map/ppermute | solution.py:1029
  38.9 10.8 %collective-permute-start.5 = (bf16[384,576]{1,0:T(8,128)(2,1)}, bf16[384,576]{1,0:T(8,128)(2,1)}, u32[]{:S(2)}, u32[]{:S(2)}) collective-permute-start(bf16[384,576]{1,0:T(8,128)(2,1)} %shard_map.234.refs_2_), channel_id=1, source_target_pairs={{0,4},{1,5},{2,10},{3,11},{4,0},{5,1},{6,14},{7,15},{8,12},{9,13},... | collective-permute-start | bytes 1327112 | tf_op jit(solution)/shard_map/ppermute | solution.py:1029
  61.6 6.4 %copy-start.4 = (f32[768]{0:T(1024)S(1)}, f32[768]{0:T(1024)}, u32[]{:S(2)}) copy-start(f32[768]{0:T(1024)} %param.23) | copy-start | bytes 9220
  61.6 7.0 %copy-start.5 = (f32[768]{0:T(1024)S(1)}, f32[768]{0:T(1024)}, u32[]{:S(2)}) copy-start(f32[768]{0:T(1024)} %param.24) | copy-start | bytes 9220
  65.0 5.0 %collective-permute-start.9 = (bf16[512,768]{1,0:T(8,128)(2,1)}, bf16[512,768]{1,0:T(8,128)(2,1)S(1)}, u32[]{:S(2)}, u32[]{:S(2)}) collective-permute-start(bf16[512,768]{1,0:T(8,128)(2,1)} %get-tuple-element.115.refs_5_.refs_1_), channel_id=1, source_target_pairs={{0,2},{1,3},{2,0},{3,1},{4,6},{5,7},{6,4},{7,5},{8,10},{9,11},{10,... | collective-permute-start | bytes 2359304 | tf_op jit(solution)/shard_map/ppermute | solution.py:1029
  70.0 7.0 %collective-permute-start.12 = (bf16[512,768]{1,0:T(8,128)(2,1)}, bf16[512,768]{1,0:T(8,128)(2,1)S(1)}, u32[]{:S(2)}, u32[]{:S(2)}) collective-permute-start(bf16[512,768]{1,0:T(8,128)(2,1)} %shard_map.238.refs_4_.refs_3_), channel_id=1, source_target_pairs={{0,2},{1,3},{2,0},{3,1},{4,6},{5,7},{6,4},{7,5},{8,10},{9,11},{10,... | collective-permute-start | bytes 2359304 | tf_op jit(solution)/shard_map/ppermute | solution.py:1029
  75.1 2.6 collective-permute-start.10
  75.6 19.1 %collective-permute-start.13 = (bf16[384,768]{1,0:T(8,128)(2,1)}, bf16[384,768]{1,0:T(8,128)(2,1)}, u32[]{:S(2)}, u32[]{:S(2)}) collective-permute-start(bf16[384,768]{1,0:T(8,128)(2,1)} %shard_map.239.refs_5_), channel_id=1, source_target_pairs={{0,4},{1,5},{2,10},{3,11},{4,0},{5,1},{6,14},{7,15},{8,12},{9,13},... | collective-permute-start | bytes 1769480 | tf_op jit(solution)/shard_map/ppermute | solution.py:1029
  76.9 17.8 %collective-permute-start.14 = (bf16[384,768]{1,0:T(8,128)(2,1)}, bf16[384,768]{1,0:T(8,128)(2,1)}, u32[]{:S(2)}, u32[]{:S(2)}) collective-permute-start(bf16[384,768]{1,0:T(8,128)(2,1)} %shard_map.240.refs_7_), channel_id=1, source_target_pairs={{0,4},{1,5},{2,10},{3,11},{4,0},{5,1},{6,14},{7,15},{8,12},{9,13},... | collective-permute-start | bytes 1769480 | tf_op jit(solution)/shard_map/ppermute | solution.py:1029
  77.7 0.9 copy-start.12
  93.3 17.6 %collective-permute-start.15 = (bf16[2,384,768]{2,1,0:T(8,128)(2,1)}, bf16[2,384,768]{2,1,0:T(8,128)(2,1)}, u32[]{:S(2)}, u32[]{:S(2)}) collective-permute-start(bf16[2,384,768]{2,1,0:T(8,128)(2,1)} %get-tuple-element.125.refs_13_), channel_id=1, source_target_pairs={{0,4},{1,5},{2,10},{3,11},{4,0},{5,1},{6,14},{7,15},{8,12},{9,13},... | collective-permute-start | bytes 3538952 | tf_op jit(solution)/shard_map/ppermute | solution.py:1029
  110.9 4.2 %collective-permute-start.16 = (bf16[512,768]{1,0:T(8,128)(2,1)}, bf16[512,768]{1,0:T(8,128)(2,1)S(1)}, u32[]{:S(2)}, u32[]{:S(2)}) collective-permute-start(bf16[512,768]{1,0:T(8,128)(2,1)} %get-tuple-element.133), channel_id=1, source_target_pairs={{0,2},{1,3},{2,0},{3,1},{4,6},{5,7},{6,4},{7,5},{8,10},{9,11},{10,... | collective-permute-start | bytes 2359304 | tf_op jit(solution)/shard_map/ppermute | solution.py:1029
  111.5 36.6 %collective-permute-start.20 = (bf16[2,192,768]{2,1,0:T(8,128)(2,1)}, bf16[2,192,768]{2,1,0:T(8,128)(2,1)}, u32[]{:S(2)}, u32[]{:S(2)}) collective-permute-start(bf16[2,192,768]{2,1,0:T(8,128)(2,1)} %get-tuple-element.148), channel_id=1, source_target_pairs={{0,8},{1,9},{2,6},{3,7},{4,12},{5,13},{6,2},{7,3},{8,0},{9,1},{10,... | collective-permute-start | bytes 1769480 | tf_op jit(solution)/shard_map/ppermute | solution.py:1029
  112.3 35.9 %collective-permute-start.21 = (bf16[2,192,768]{2,1,0:T(8,128)(2,1)}, bf16[2,192,768]{2,1,0:T(8,128)(2,1)}, u32[]{:S(2)}, u32[]{:S(2)}) collective-permute-start(bf16[2,192,768]{2,1,0:T(8,128)(2,1)} %get-tuple-element.149), channel_id=1, source_target_pairs={{0,4},{1,5},{2,10},{3,11},{4,0},{5,1},{6,14},{7,15},{8,12},{9,13},... | collective-permute-start | bytes 1769480 | tf_op jit(solution)/shard_map/ppermute | solution.py:1029
  113.1 35.1 %collective-permute-start.22 = (bf16[2,192,768]{2,1,0:T(8,128)(2,1)}, bf16[2,192,768]{2,1,0:T(8,128)(2,1)}, u32[]{:S(2)}, u32[]{:S(2)}) collective-permute-start(bf16[2,192,768]{2,1,0:T(8,128)(2,1)} %get-tuple-element.134.refs_5_), channel_id=1, source_target_pairs={{0,12},{1,13},{2,14},{3,15},{4,8},{5,9},{6,10},{7,11},{8,4},{9,5},... | collective-permute-start | bytes 1769480 | tf_op jit(solution)/shard_map/ppermute | solution.py:1029
  114.2 6.8 %collective-permute-start.18 = (bf16[512,768]{1,0:T(8,128)(2,1)}, bf16[512,768]{1,0:T(8,128)(2,1)S(1)}, u32[]{:S(2)}, u32[]{:S(2)}) collective-permute-start(bf16[512,768]{1,0:T(8,128)(2,1)} %get-tuple-element.139), channel_id=1, source_target_pairs={{0,2},{1,3},{2,0},{3,1},{4,6},{5,7},{6,4},{7,5},{8,10},{9,11},{10,... | collective-permute-start | bytes 2359304 | tf_op jit(solution)/shard_map/ppermute | solution.py:1029
  115.1 0.9 copy-start.16
  120.9 7.0 %collective-permute-start.17 = (bf16[512,768]{1,0:T(8,128)(2,1)}, bf16[512,768]{1,0:T(8,128)(2,1)S(1)}, u32[]{:S(2)}, u32[]{:S(2)}) collective-permute-start(bf16[512,768]{1,0:T(8,128)(2,1)} %get-tuple-element.135.refs_1_), channel_id=1, source_target_pairs={{0,2},{1,3},{2,0},{3,1},{4,6},{5,7},{6,4},{7,5},{8,10},{9,11},{10,... | collective-permute-start | bytes 2359304 | tf_op jit(solution)/shard_map/ppermute | solution.py:1029
  121.0 0.9 copy-start.15
  126.8 21.4 %collective-permute-start.19 = (bf16[2,192,768]{2,1,0:T(8,128)(2,1)}, bf16[2,192,768]{2,1,0:T(8,128)(2,1)}, u32[]{:S(2)}, u32[]{:S(2)}) collective-permute-start(bf16[2,192,768]{2,1,0:T(8,128)(2,1)} %get-tuple-element.142.refs_8_), channel_id=1, source_target_pairs={{0,8},{1,9},{2,6},{3,7},{4,12},{5,13},{6,2},{7,3},{8,0},{9,1},{10,... | collective-permute-start | bytes 1769480 | tf_op jit(solution)/shard_map/ppermute | solution.py:1029
  127.9 5.2 %copy-start.10 = (bf16[512,768]{1,0:T(8,128)(2,1)}, bf16[512,768]{1,0:T(8,128)(2,1)S(1)}, u32[]{:S(2)}) copy-start(bf16[512,768]{1,0:T(8,128)(2,1)S(1)} %collective-permute-done.17.refs_2_) | copy-start | bytes 2359300
  127.9 20.3 %collective-permute-start.23 = (bf16[512,768]{1,0:T(8,128)(2,1)}, bf16[512,768]{1,0:T(8,128)(2,1)}, u32[]{:S(2)}, u32[]{:S(2)}) collective-permute-start(bf16[512,768]{1,0:T(8,128)(2,1)} %get-tuple-element.150), channel_id=1, source_target_pairs={{0,0},{1,2},{2,1},{3,3},{4,4},{5,6},{6,5},{7,7},{8,8},{9,10},{10,9... | collective-permute-start | bytes 2359304 | tf_op jit(solution)/shard_map/ppermute | solution.py:1029
  156.0 25.3 %collective-permute-start.25 = (bf16[1,192,768]{2,1,0:T(8,128)(2,1)}, bf16[1,192,768]{2,1,0:T(8,128)(2,1)}, u32[]{:S(2)}, u32[]{:S(2)}) collective-permute-start(bf16[1,192,768]{2,1,0:T(8,128)(2,1)} %get-tuple-element.158), channel_id=1, source_target_pairs={{0,8},{1,9},{2,6},{3,7},{4,12},{5,13},{6,2},{7,3},{8,0},{9,1},{10,... | collective-permute-start | bytes 884744 | tf_op jit(solution)/shard_map/ppermute | solution.py:1029
  156.2 25.0 %collective-permute-start.26 = (bf16[1,192,768]{2,1,0:T(8,128)(2,1)}, bf16[1,192,768]{2,1,0:T(8,128)(2,1)}, u32[]{:S(2)}, u32[]{:S(2)}) collective-permute-start(bf16[1,192,768]{2,1,0:T(8,128)(2,1)} %get-tuple-element.159), channel_id=1, source_target_pairs={{0,4},{1,5},{2,10},{3,11},{4,0},{5,1},{6,14},{7,15},{8,12},{9,13},... | collective-permute-start | bytes 884744 | tf_op jit(solution)/shard_map/ppermute | solution.py:1029
  157.3 24.0 %collective-permute-start.27 = (bf16[1,192,768]{2,1,0:T(8,128)(2,1)}, bf16[1,192,768]{2,1,0:T(8,128)(2,1)}, u32[]{:S(2)}, u32[]{:S(2)}) collective-permute-start(bf16[1,192,768]{2,1,0:T(8,128)(2,1)} %get-tuple-element.151.refs_9_), channel_id=1, source_target_pairs={{0,12},{1,13},{2,14},{3,15},{4,8},{5,9},{6,10},{7,11},{8,4},{9,5},... | collective-permute-start | bytes 884744 | tf_op jit(solution)/shard_map/ppermute | solution.py:1029
  158.6 22.7 %collective-permute-start.28 = (bf16[2,192,768]{2,1,0:T(8,128)(2,1)}, bf16[2,192,768]{2,1,0:T(8,128)(2,1)}, u32[]{:S(2)}, u32[]{:S(2)}) collective-permute-start(bf16[2,192,768]{2,1,0:T(8,128)(2,1)} %get-tuple-element.161), channel_id=1, source_target_pairs={{0,1},{1,0},{2,3},{3,2},{4,5},{5,4},{6,7},{7,6},{8,9},{9,8},{10,11... | collective-permute-start | bytes 1769480 | tf_op jit(solution)/shard_map/ppermute | solution.py:1029
  179.6 11.1 %collective-permute-start.24 = (bf16[1024,1024]{1,0:T(8,128)(2,1)}, bf16[1024,1024]{1,0:T(8,128)(2,1)S(1)}, u32[]{:S(2)}, u32[]{:S(2)}) collective-permute-start(bf16[1024,1024]{1,0:T(8,128)(2,1)} %get-tuple-element.152.refs_10_.refs_1_), channel_id=1, source_target_pairs={{2,0},{3,1},{6,4},{7,5},{10,8},{11,9},{14,12},{15,13},{18,16},{19,... | collective-permute-start | bytes 6291464 | tf_op jit(solution)/shard_map/ppermute | solution.py:1029
  186.3 19.3 %collective-permute-start.29 = (bf16[1,192,768]{2,1,0:T(8,128)(2,1)}, bf16[1,192,768]{2,1,0:T(8,128)(2,1)}, u32[]{:S(2)}, u32[]{:S(2)}) collective-permute-start(bf16[1,192,768]{2,1,0:T(8,128)(2,1)} %get-tuple-element.166), channel_id=1, source_target_pairs={{0,8},{1,9},{2,6},{3,7},{4,12},{5,13},{6,2},{7,3},{8,0},{9,1},{10,... | collective-permute-start | bytes 884744 | tf_op jit(solution)/shard_map/ppermute | solution.py:1029
  186.7 19.0 %collective-permute-start.30 = (bf16[1,192,768]{2,1,0:T(8,128)(2,1)}, bf16[1,192,768]{2,1,0:T(8,128)(2,1)}, u32[]{:S(2)}, u32[]{:S(2)}) collective-permute-start(bf16[1,192,768]{2,1,0:T(8,128)(2,1)} %get-tuple-element.167), channel_id=1, source_target_pairs={{0,4},{1,5},{2,10},{3,11},{4,0},{5,1},{6,14},{7,15},{8,12},{9,13},... | collective-permute-start | bytes 884744 | tf_op jit(solution)/shard_map/ppermute | solution.py:1029
  188.0 17.7 %collective-permute-start.32 = (bf16[1,192,768]{2,1,0:T(8,128)(2,1)}, bf16[1,192,768]{2,1,0:T(8,128)(2,1)}, u32[]{:S(2)}, u32[]{:S(2)}) collective-permute-start(bf16[1,192,768]{2,1,0:T(8,128)(2,1)} %get-tuple-element.168), channel_id=1, source_target_pairs={{0,1},{1,0},{2,3},{3,2},{4,5},{5,4},{6,7},{7,6},{8,9},{9,8},{10,11... | collective-permute-start | bytes 884744 | tf_op jit(solution)/shard_map/ppermute | solution.py:1029
  189.4 21.6 %collective-permute-start.31 = (bf16[1,192,768]{2,1,0:T(8,128)(2,1)}, bf16[1,192,768]{2,1,0:T(8,128)(2,1)}, u32[]{:S(2)}, u32[]{:S(2)}) collective-permute-start(bf16[1,192,768]{2,1,0:T(8,128)(2,1)} %get-tuple-element.162.refs_13_), channel_id=1, source_target_pairs={{0,12},{1,13},{2,14},{3,15},{4,8},{5,9},{6,10},{7,11},{8,4},{9,5},... | collective-permute-start | bytes 884744 | tf_op jit(solution)/shard_map/ppermute | solution.py:1029
  190.8 2.3 copy-start.7
  190.8 28.5 %collective-permute-start.34 = (bf16[2,192,768]{2,1,0:T(8,128)(2,1)}, bf16[2,192,768]{2,1,0:T(8,128)(2,1)}, u32[]{:S(2)}, u32[]{:S(2)}) collective-permute-start(bf16[2,192,768]{2,1,0:T(8,128)(2,1)} %get-tuple-element.170.refs_7_), channel_id=1, source_target_pairs={{0,16},{1,17},{2,18},{3,19},{4,20},{5,21},{6,22},{7,23},{8,24},{9,... | collective-permute-start | bytes 1769480 | tf_op jit(solution)/shard_map/ppermute | solution.py:1029
  210.9 8.8 %collective-permute-start.33 = (bf16[144,768]{1,0:T(8,128)(2,1)}, bf16[144,768]{1,0:T(8,128)(2,1)S(1)}, u32[]{:S(2)}, u32[]{:S(2)}) collective-permute-start(bf16[144,768]{1,0:T(8,128)(2,1)} %get-tuple-element.169.refs_0_.refs_9_), channel_id=1, source_target_pairs={{0,1},{1,0},{2,3},{3,2},{4,5},{5,4},{6,7},{7,6},{8,9},{9,8},{10,11... | collective-permute-start | bytes 663560 | tf_op jit(solution)/shard_map/ppermute | solution.py:1029
  214.4 12.3 %collective-permute-start.39 = (bf16[512,768]{1,0:T(8,128)(2,1)}, bf16[512,768]{1,0:T(8,128)(2,1)S(1)}, u32[]{:S(2)}, u32[]{:S(2)}) collective-permute-start(bf16[512,768]{1,0:T(8,128)(2,1)} %get-tuple-element.174), channel_id=1, source_target_pairs={{0,2},{1,3},{2,0},{3,1},{4,6},{5,7},{6,4},{7,5},{8,10},{9,11},{10,... | collective-permute-start | bytes 2359304 | tf_op jit(solution)/shard_map/ppermute | solution.py:1029
  223.5 35.8 %collective-permute-start.38 = (bf16[2,192,768]{2,1,0:T(8,128)(2,1)}, bf16[2,192,768]{2,1,0:T(8,128)(2,1)S(1)}, u32[]{:S(2)}, u32[]{:S(2)}) collective-permute-start(bf16[2,192,768]{2,1,0:T(8,128)(2,1)} %get-tuple-element.172.refs_5_.refs_3_), channel_id=1, source_target_pairs={{0,12},{1,13},{2,14},{3,15},{4,8},{5,9},{6,10},{7,11},{8,4},{9,5},... | collective-permute-start | bytes 1769480 | tf_op jit(solution)/shard_map/ppermute | solution.py:1029
  223.5 40.1 %collective-permute-start.37 = (bf16[2,192,768]{2,1,0:T(8,128)(2,1)}, bf16[2,192,768]{2,1,0:T(8,128)(2,1)S(1)}, u32[]{:S(2)}, u32[]{:S(2)}) collective-permute-start(bf16[2,192,768]{2,1,0:T(8,128)(2,1)} %get-tuple-element.172.refs_5_.refs_3_), channel_id=1, source_target_pairs={{0,4},{1,5},{2,10},{3,11},{4,0},{5,1},{6,14},{7,15},{8,12},{9,13},... | collective-permute-start | bytes 1769480 | tf_op jit(solution)/shard_map/ppermute | solution.py:1029
  226.6 37.0 %collective-permute-start.36 = (bf16[2,192,768]{2,1,0:T(8,128)(2,1)}, bf16[2,192,768]{2,1,0:T(8,128)(2,1)S(1)}, u32[]{:S(2)}, u32[]{:S(2)}) collective-permute-start(bf16[2,192,768]{2,1,0:T(8,128)(2,1)} %get-tuple-element.172.refs_5_.refs_3_), channel_id=1, source_target_pairs={{0,8},{1,9},{2,6},{3,7},{4,12},{5,13},{6,2},{7,3},{8,0},{9,1},{10,... | collective-permute-start | bytes 1769480 | tf_op jit(solution)/shard_map/ppermute | solution.py:1029
  226.6 32.7 %collective-permute-start.35 = (bf16[336,768]{1,0:T(8,128)(2,1)}, bf16[336,768]{1,0:T(8,128)(2,1)S(1)}, u32[]{:S(2)}, u32[]{:S(2)}) collective-permute-start(bf16[336,768]{1,0:T(8,128)(2,1)} %get-tuple-element.171.refs_1_), channel_id=1, source_target_pairs={{0,16},{1,17},{2,18},{3,19},{4,20},{5,21},{6,22},{7,23},{8,24},{9,... | collective-permute-start | bytes 1548296 | tf_op jit(solution)/shard_map/ppermute | solution.py:1029
  226.7 0.9 copy-start.13
  259.3 4.3 %copy-start.21 = (bf16[336,768]{1,0:T(8,128)(2,1)}, bf16[336,768]{1,0:T(8,128)(2,1)S(1)}, u32[]{:S(2)}) copy-start(bf16[336,768]{1,0:T(8,128)(2,1)S(1)} %collective-permute-done.35.refs_2_) | copy-start | bytes 1548292
  259.3 4.3 %copy-start.18 = (bf16[2,192,768]{2,1,0:T(8,128)(2,1)}, bf16[2,192,768]{2,1,0:T(8,128)(2,1)S(1)}, u32[]{:S(2)}) copy-start(bf16[2,192,768]{2,1,0:T(8,128)(2,1)S(1)} %collective-permute-done.38.refs_6_) | copy-start | bytes 1769476
  268.9 6.3 %collective-permute-start.44 = (bf16[2,768,768]{2,1,0:T(8,128)(2,1)}, bf16[2,768,768]{2,1,0:T(8,128)(2,1)S(1)}, u32[]{:S(2)}, u32[]{:S(2)}) collective-permute-start(bf16[2,768,768]{2,1,0:T(8,128)(2,1)} %get-tuple-element.177.refs_1_.refs_3_), channel_id=1, source_target_pairs={{0,2},{1,3},{2,0},{3,1},{4,6},{5,7},{6,4},{7,5},{8,10},{9,11},{10,... | collective-permute-start | bytes 7077896 | tf_op jit(solution)/shard_map/ppermute | solution.py:1029
  269.4 29.1 %collective-permute-start.43 = (bf16[512,768]{1,0:T(8,128)(2,1)}, bf16[512,768]{1,0:T(8,128)(2,1)}, u32[]{:S(2)}, u32[]{:S(2)}) collective-permute-start(bf16[512,768]{1,0:T(8,128)(2,1)} %shard_map.253.refs_7_), channel_id=1, source_target_pairs={{0,0},{1,2},{2,1},{3,3},{4,4},{5,6},{6,5},{7,7},{8,8},{9,10},{10,9... | collective-permute-start | bytes 2359304 | tf_op jit(solution)/shard_map/ppermute | solution.py:1029
  272.5 10.9 %collective-permute-start.42 = (bf16[336,768]{1,0:T(8,128)(2,1)}, bf16[336,768]{1,0:T(8,128)(2,1)}, u32[]{:S(2)}, u32[]{:S(2)}) collective-permute-start(bf16[336,768]{1,0:T(8,128)(2,1)} %get-tuple-element.176.refs_1_), channel_id=1, source_target_pairs={{0,12},{1,13},{2,14},{3,15},{4,8},{5,9},{6,10},{7,11},{8,4},{9,5},... | collective-permute-start | bytes 1548296 | tf_op jit(solution)/shard_map/ppermute | solution.py:1029
  272.6 20.7 %collective-permute-start.41 = (bf16[336,768]{1,0:T(8,128)(2,1)}, bf16[336,768]{1,0:T(8,128)(2,1)}, u32[]{:S(2)}, u32[]{:S(2)}) collective-permute-start(bf16[336,768]{1,0:T(8,128)(2,1)} %get-tuple-element.176.refs_1_), channel_id=1, source_target_pairs={{0,4},{1,5},{2,10},{3,11},{4,0},{5,1},{6,14},{7,15},{8,12},{9,13},... | collective-permute-start | bytes 1548296 | tf_op jit(solution)/shard_map/ppermute | solution.py:1029
  273.8 24.7 %collective-permute-start.40 = (bf16[336,768]{1,0:T(8,128)(2,1)}, bf16[336,768]{1,0:T(8,128)(2,1)}, u32[]{:S(2)}, u32[]{:S(2)}) collective-permute-start(bf16[336,768]{1,0:T(8,128)(2,1)} %get-tuple-element.176.refs_1_), channel_id=1, source_target_pairs={{0,8},{1,9},{2,6},{3,7},{4,12},{5,13},{6,2},{7,3},{8,0},{9,1},{10,... | collective-permute-start | bytes 1548296 | tf_op jit(solution)/shard_map/ppermute | solution.py:1029
  275.2 1.4 copy-start.6
  302.3 3.5 %collective-permute-start.45 = (bf16[912,768]{1,0:T(8,128)(2,1)}, bf16[912,768]{1,0:T(8,128)(2,1)S(1)}, u32[]{:S(2)}, u32[]{:S(2)}) collective-permute-start(bf16[912,768]{1,0:T(8,128)(2,1)} %get-tuple-element.181.refs_1_), channel_id=1, source_target_pairs={{0,2},{1,3},{2,0},{3,1},{4,6},{5,7},{6,4},{7,5},{8,10},{9,11},{10,... | collective-permute-start | bytes 4202504 | tf_op jit(solution)/shard_map/ppermute | solution.py:1029
  305.8 1.1 copy-start.8
  (5 other events, 4.1 us)
